TPU v7x, 32 devices: a whole 2x2x4 slice. The times are simulated.
32 devices in a mesh: seq: 8 (over y, x, core), chan: 4 (over z).
Axes of the slice: x: 2, y: 2, z: 4, core: 2. Of those that a mesh axis runs over, the one named last changes fastest.
Arguments:
- signal: bfloat16 [1024, 2048], P('chan', 'seq'), may hold values from -6 to 6
- gating: bfloat16 [1024, 2048], P('chan', 'seq'), may hold values from -6 to 6
- filter_taps: float32 [1024, 2048], P('chan', 'seq'), may hold values from -6 to 6
- decay_rates: float32 [1024], P('chan'), may hold values from 0.00012207031 to 0.0078125
- out_weight: bfloat16 [1024, 2048], P(None, 'chan'), may hold values from -0.1875 to 0.1875
- out_grad: bfloat16 [2048, 2048], P('seq', 'chan'), may hold values from -1.5 to 1.5
Outputs:
- mixed_out: bfloat16 [2048, 2048], P('seq', 'chan')
- signal_grad: float32 [1024, 2048], P('chan', 'seq')
- gating_grad: float32 [1024, 2048], P('chan', 'seq')
- taps_grad: float32 [1024, 2048], P('chan', 'seq')
All inputs are finite; a program needn't handle non-finite values.
Results may differ from a plain program's by a relative error of at most 0.013.
Values may be sent and summed in bfloat16 or wider, within the bound.
No kernel may reach another device: no remote copies, remote signals or barrier semaphores. Data moves between devices by JAX's collectives and lax.ppermute only.
A program may use at most 64 MiB of HBM per device.

v0:
```python
import functools

import jax
import jax.numpy as jnp
import ml_dtypes
import numpy as np
from jax import lax
from jax.experimental import pallas as pl
from jax.experimental.pallas import tpu as pltpu
from jax.sharding import PartitionSpec as P

f32 = jnp.float32
bf16 = jnp.bfloat16
VMEM = pl.BlockSpec(memory_space=pltpu.VMEM)
ROWS = 16
LANES = 128


def call(kernel, out_shape, count, scratch=(), flops=0, moved=0):
    return pl.pallas_call(
        kernel,
        out_shape=out_shape,
        in_specs=[VMEM] * count,
        out_specs=jax.tree.map(lambda _: VMEM, out_shape),
        scratch_shapes=list(scratch),
        cost_estimate=pl.CostEstimate(flops=flops, bytes_accessed=moved, transcendentals=0),
        compiler_params=pltpu.CompilerParams(vmem_limit_bytes=48 * 1024 * 1024),
    )


def within_table(lanes):
    index = np.arange(lanes)
    angle = 2.0 * np.pi * (np.outer(index, index) % lanes) / lanes
    cos, sin = np.cos(angle), np.sin(angle)
    table = np.concatenate(
        [np.concatenate([cos, -sin], 1), np.concatenate([sin, cos], 1)], 0
    )
    return table.astype(ml_dtypes.bfloat16)


def twiddle_table(blocks, lanes):
    rows = np.arange(blocks + 1)[:, None]
    angle = 2.0 * np.pi * rows * np.arange(lanes)[None, :] / (2 * blocks * lanes)
    return np.stack([np.cos(angle), np.sin(angle)], 1).astype(np.float32)


def turned(real, imag, turn, size):
    angle = 2.0 * np.pi * turn / size
    cos, sin = float(np.cos(angle)), float(np.sin(angle))
    if turn == 0:
        return real, imag
    if abs(abs(cos) - abs(sin)) < 1e-9:
        root = abs(cos)
        cs, ss = (1 if cos > 0 else -1), (1 if sin > 0 else -1)
        first = real if cs > 0 else -real
        if cs == ss:
            return (root * cs) * (real - imag), (root * cs) * (real + imag)
        return (root * cs) * (real + imag), (root * cs) * (imag - real)
    return cos * real - sin * imag, sin * real + cos * imag


def real_forward(tiles, size):
    if size == 2:
        return [(tiles[0], None), (tiles[0], None)]
    even = real_forward(tiles[0::2], size // 2)
    odd = real_forward(tiles[1::2], size // 2)
    quarter = size // 4
    out = [None] * (size // 2 + 1)
    out[0] = (even[0][0] + odd[0][0], None)
    out[size // 2] = (even[0][0] - odd[0][0], None)
    for row in range(1, quarter):
        real, imag = turned(odd[row][0], odd[row][1], -row, size)
        out[row] = (even[row][0] + real, even[row][1] + imag)
        out[size // 2 - row] = (even[row][0] - real, imag - even[row][1])
    out[quarter] = (even[quarter][0], -odd[quarter][0])
    return out


def real_inverse(rows, size):
    if size == 2:
        return [rows[0][0] + rows[1][0]]
    quarter = size // 4
    even, odd = [], []
    for row in range(quarter + 1):
        real, imag = rows[row]
        if row == 0:
            last = rows[size // 2][0]
            even.append((real + last, None))
            odd.append((real - last, None))
        elif row == quarter:
            even.append((2.0 * real, None))
            odd.append((-2.0 * imag, None))
        else:
            far_real, far_imag = rows[size // 2 - row]
            even.append((real + far_real, imag - far_imag))
            odd.append(turned(real - far_real, imag + far_imag, row, size))
    firsts = real_inverse(even, size // 2)
    seconds = real_inverse(odd, size // 2)
    return [tile for pair in zip(firsts, seconds) for tile in pair]


def tile_slices(rows, lanes):
    for row in range(0, rows, ROWS):
        for lane in range(0, lanes, LANES):
            yield row, lane


def first_step(read, twiddle_ref, out_ref, base, blocks, rows, lanes):
    for row, lane in tile_slices(rows, lanes):
        tiles = [read(block, row, lane) for block in range(blocks)]
        for step, (real, imag) in enumerate(real_forward(tiles, 2 * blocks)):
            cos = twiddle_ref[step, 0:1, lane : lane + LANES]
            sin = twiddle_ref[step, 1:2, lane : lane + LANES]
            if step == 0:
                new_real, new_imag = real, jnp.zeros_like(real)
            elif imag is None:
                new_real, new_imag = real * cos, -real * sin
            else:
                new_real, new_imag = real * cos + imag * sin, imag * cos - real * sin
            at = base + step * rows + row
            out_ref[at : at + ROWS, lane : lane + LANES] = new_real.astype(bf16)
            out_ref[at : at + ROWS, lanes + lane : lanes + lane + LANES] = new_imag.astype(bf16)


def last_step(spec_ref, base, twiddle_ref, write, blocks, rows, lanes):
    scale = 1.0 / (2 * blocks * lanes)
    for row, lane in tile_slices(rows, lanes):
        steps = []
        for step in range(blocks + 1):
            at = base + step * rows + row
            imag = spec_ref[at : at + ROWS, lane : lane + LANES]
            real = spec_ref[at : at + ROWS, lanes + lane : lanes + lane + LANES]
            cos = twiddle_ref[step, 0:1, lane : lane + LANES] * scale
            sin = twiddle_ref[step, 1:2, lane : lane + LANES] * scale
            new_real = real * cos - imag * sin
            if step == 0 or step == blocks:
                steps.append((new_real, None))
            else:
                steps.append((new_real, imag * cos + real * sin))
        for block, tile in enumerate(real_inverse(steps, 2 * blocks)):
            write(block, row, lane, tile)


def tile_read(ref, base):
    def read(block, row, lane):
        at = base + row
        return ref[block, at : at + ROWS, lane : lane + LANES].astype(f32)

    return read


def tile_write(ref, base):
    def write(block, row, lane, tile):
        at = base + row
        ref[block, at : at + ROWS, lane : lane + LANES] = tile.astype(ref.dtype)

    return write


def product(first_real, first_imag, second_real, second_imag, out_ref, base, conjugate):
    rows, lanes = first_real.shape
    if conjugate:
        real = first_real * second_real + first_imag * second_imag
        imag = first_imag * second_real - first_real * second_imag
    else:
        real = first_real * second_real - first_imag * second_imag
        imag = first_real * second_imag + first_imag * second_real
    out_ref[base : base + rows, :lanes] = imag.astype(bf16)
    out_ref[base : base + rows, lanes:] = real.astype(bf16)


def convolve_kernel(pair_ref, table_ref, twiddle_ref, mixed_ref, spec_ref, left_ref, back_ref):
    blocks, rows, lanes = mixed_ref.shape
    height = (blocks + 1) * rows
    first_step(tile_read(pair_ref, 0), twiddle_ref, left_ref, 0, blocks, rows, lanes)
    first_step(tile_read(pair_ref, rows), twiddle_ref, left_ref, height, blocks, rows, lanes)
    spec_ref[...] = jnp.dot(left_ref[...], table_ref[...], preferred_element_type=f32)
    product(
        spec_ref[:height, :lanes],
        spec_ref[:height, lanes:],
        spec_ref[height:, :lanes],
        spec_ref[height:, lanes:],
        left_ref,
        0,
        False,
    )
    back_ref[...] = jnp.dot(left_ref[:height], table_ref[...], preferred_element_type=f32)
    last_step(back_ref, 0, twiddle_ref, tile_write(mixed_ref, 0), blocks, rows, lanes)


def correlate_kernel(grad_ref, spec_ref, table_ref, twiddle_ref, out_ref, left_ref, back_ref):
    blocks, rows, lanes = grad_ref.shape
    height = (blocks + 1) * rows
    first_step(tile_read(grad_ref, 0), twiddle_ref, left_ref, 0, blocks, rows, lanes)
    grad = jnp.dot(left_ref[:height], table_ref[...], preferred_element_type=f32)
    for base, other in ((0, height), (height, 0)):
        product(
            grad[:, :lanes],
            grad[:, lanes:],
            spec_ref[other : other + height, :lanes],
            spec_ref[other : other + height, lanes:],
            left_ref,
            base,
            True,
        )
    back_ref[...] = jnp.dot(left_ref[...], table_ref[...], preferred_element_type=f32)
    last_step(back_ref, 0, twiddle_ref, tile_write(out_ref, 0), blocks, rows, lanes)
    last_step(back_ref, height, twiddle_ref, tile_write(out_ref, rows), blocks, rows, lanes)


def window_kernel(decay_ref, taps_ref, signal_ref, pair_ref, window_ref):
    channels, length = taps_ref.shape
    shards, twice, _ = pair_ref.shape
    owned = twice // 2
    start = lax.axis_index("seq") * length
    places = (start + lax.broadcasted_iota(jnp.int32, (1, length), 1)).astype(f32)
    rates = jnp.broadcast_to(decay_ref[...], (length, channels)).T
    window = jnp.exp(-rates * places) * jnp.sqrt(2.0 * rates)
    window_ref[...] = window
    filters = (taps_ref[...] * window).astype(bf16)
    for shard in range(shards):
        rows = slice(shard * owned, (shard + 1) * owned)
        pair_ref[shard, :owned] = signal_ref[rows]
        pair_ref[shard, owned:] = filters[rows]


def spread_kernel(weight_ref, grad_ref, *out_refs):
    count = len(out_refs)
    rows = weight_ref.shape[0] // count
    me = lax.axis_index("chan")
    for step in list(range(1, count)) + [0]:
        place = lax.rem(me + step, count)
        block = weight_ref[pl.ds(pl.multiple_of(place * rows, rows), rows), :]
        out_refs[step][...] = lax.dot_general(
            block, grad_ref[...], (((1,), (1,)), ((), ())), preferred_element_type=f32
        ).astype(out_refs[step].dtype)


def project_kernel(weight_ref, *refs):
    gated_refs, out_ref = refs[:-1], refs[-1]
    count = len(gated_refs)
    rows = weight_ref.shape[0] // count
    me = lax.axis_index("chan")
    total = None
    for step in range(count):
        place = lax.rem(me + count - step, count)
        block = weight_ref[pl.ds(pl.multiple_of(place * rows, rows), rows), :]
        term = lax.dot_general(
            gated_refs[step][...], block, (((0,), (0,)), ((), ())), preferred_element_type=f32
        )
        total = term if total is None else total + term
    out_ref[...] = total.astype(out_ref.dtype)


def return_kernel(back_ref, window_ref, signal_ref, taps_ref):
    shards, twice, _ = back_ref.shape
    owned = twice // 2
    for shard in range(shards):
        rows = slice(shard * owned, (shard + 1) * owned)
        signal_ref[rows] = back_ref[shard, :owned].astype(f32)
        taps_ref[rows] = back_ref[shard, owned:].astype(f32) * window_ref[rows]


def padded(array, owned, held):
    if owned == held:
        return array
    blocks, rows, lanes = array.shape
    groups = array.reshape(blocks, rows // owned, owned, lanes)
    groups = jnp.pad(groups, ((0, 0), (0, 0), (0, held - owned), (0, 0)))
    return groups.reshape(blocks, -1, lanes)


def trimmed(array, owned, held):
    if owned == held:
        return array
    blocks, rows, lanes = array.shape
    return array.reshape(blocks, rows // held, held, lanes)[:, :, :owned].reshape(blocks, -1, lanes)


def exchange(array):
    return lax.all_to_all(array, "seq", split_axis=0, concat_axis=0, tiled=True)


def per_device(signal, gating, filter_taps, decay_rates, out_weight, out_grad):
    channels, length = signal.shape
    shards = lax.axis_size("seq")
    parts = lax.axis_size("chan")
    owned = channels // shards
    held = -(-owned // ROWS) * ROWS
    height = (shards + 1) * held
    table = jnp.asarray(within_table(length))
    twiddle = jnp.asarray(twiddle_table(shards, length))
    shape = jax.ShapeDtypeStruct
    pass_flops = 2 * height * (2 * length) ** 2

    def shift(array, step):
        return lax.ppermute(array, "chan", [(i, (i + step) % parts) for i in range(parts)])

    pairs, window = call(
        window_kernel,
        (shape((shards, 2 * held, length), bf16), shape((channels, length), f32)),
        3,
    )(decay_rates.reshape(1, channels), filter_taps, signal) if owned == held else window_plain(
        decay_rates, filter_taps, signal, shards
    )
    arrived = exchange(pairs)

    partial = call(
        spread_kernel,
        tuple(shape((channels, length), f32 if k == 0 else bf16) for k in range(parts)),
        2,
        flops=2 * out_weight.shape[0] * out_weight.shape[1] * length,
        moved=2 * out_weight.size,
    )(out_weight, out_grad)
    shares = [shift(partial[step], step) for step in range(1, parts)]

    mixed_owned, spectra = call(
        convolve_kernel,
        (shape((shards, held, length), bf16), shape((2 * height, 2 * length), f32)),
        3,
        (pltpu.VMEM((2 * height, 2 * length), bf16), pltpu.VMEM((height, 2 * length), f32)),
        flops=3 * pass_flops,
        moved=4 * 2 * height * 2 * length,
    )(padded(arrived, owned, held), table, twiddle)
    mixed = exchange(trimmed(mixed_owned, owned, held)).reshape(channels, length).astype(f32)

    gate_values = gating.astype(f32)
    grad_mixed_out = partial[0]
    for share in shares:
        grad_mixed_out = grad_mixed_out + share.astype(f32)
    grad_mixed = (grad_mixed_out * gate_values).astype(bf16)
    grad_whole = exchange(grad_mixed.reshape(shards, owned, length))

    gating_grad = grad_mixed_out * mixed
    gated = (gate_values * mixed).astype(bf16)
    gathered = [gated] + [shift(gated, step) for step in range(1, parts)]
    mixed_out = call(
        project_kernel,
        shape((length, out_weight.shape[1]), bf16),
        1 + parts,
        flops=2 * out_weight.shape[0] * out_weight.shape[1] * length,
        moved=2 * out_weight.size,
    )(out_weight, *gathered)

    grads_owned = call(
        correlate_kernel,
        shape((shards, 2 * held, length), bf16),
        4,
        (pltpu.VMEM((2 * height, 2 * length), bf16), pltpu.VMEM((2 * height, 2 * length), f32)),
        flops=3 * pass_flops,
        moved=4 * 2 * height * 2 * length,
    )(padded(grad_whole, owned, held), spectra, table, twiddle)
    returned = exchange(trimmed(grads_owned, owned, held))
    if owned == held:
        signal_grad, taps_grad = call(
            return_kernel,
            (shape((channels, length), f32), shape((channels, length), f32)),
            2,
        )(returned, window)
    else:
        both = returned.reshape(shards, 2, owned, length).astype(f32)
        signal_grad = both[:, 0].reshape(channels, length)
        taps_grad = both[:, 1].reshape(channels, length) * window
    return (mixed_out, signal_grad, gating_grad, taps_grad)


def window_plain(decay_rates, filter_taps, signal, shards):
    channels, length = signal.shape
    owned = channels // shards
    places = (lax.axis_index("seq") * length + jnp.arange(length, dtype=jnp.int32)).astype(f32)
    rates = decay_rates[:, None]
    window = jnp.exp(-rates * places[None, :]) * jnp.sqrt(2.0 * rates)
    filters = (filter_taps * window).astype(bf16)
    pairs = jnp.stack(
        [signal.reshape(shards, owned, length), filters.reshape(shards, owned, length)], 1
    )
    return pairs.reshape(shards, 2 * owned, length), window


def solution(mesh):
    in_specs = (
        P("chan", "seq"),
        P("chan", "seq"),
        P("chan", "seq"),
        P("chan"),
        P(None, "chan"),
        P("seq", "chan"),
    )
    out_specs = (P("seq", "chan"), P("chan", "seq"), P("chan", "seq"), P("chan", "seq"))
    return jax.shard_map(
        per_device, mesh=mesh, in_specs=in_specs, out_specs=out_specs, check_vma=False
    )
```

profile of v0, /device:TPU:0, one launch (start us, length us, event | category | flops | bytes accessed | tf_op | source)
XLA Modules:
  0.0 59.6 jit_solution(15051038842559798635)
XLA Ops:
  0.6 0.0 copy-start.2
  0.7 1.0 %copy-done.4 = f32[256,256]{1,0:T(8,128)S(1)} copy-done((f32[256,256]{1,0:T(8,128)S(1)}, f32[256,256]{1,0:T(8,128)}, u32[]{:S(2)}) %copy-start.4) | copy-done | bytes 262168
  1.7 0.9 %copy-done.5 = bf16[256,256]{1,0:T(8,128)(2,1)S(1)} copy-done((bf16[256,256]{1,0:T(8,128)(2,1)S(1)}, bf16[256,256]{1,0:T(8,128)(2,1)}, u32[]{:S(2)}) %copy-start.5) | copy-done | bytes 131096
  2.6 0.7 %copy-done.7 = f32[256]{0:T(256)S(1)} copy-done((f32[256]{0:T(256)S(1)}, f32[256]{0:T(256)}, u32[]{:S(2)}) %copy-start.7) | copy-done | bytes 1048
  3.2 0.9 %shard_map.111 = (bf16[8,64,256]{2,1,0:T(8,128)(2,1)}, f32[256,256]{1,0:T(8,128)S(1)}) custom-call(f32[1,256]{1,0:T(1,128)S(1)} %bitcast.6, f32[256,256]{1,0:T(8,128)S(1)} %copy-done.4, bf16[256,256]{1,0:T(8,128)(2,1)S(1)} %copy-done.5), custom_call_target="tpu_custom_call" | custom-call | tf_op jit(solution)/shard_map/pallas_call | solution.py:299
  4.1 5.2 %all-to-all-start = ((bf16[8,64,256]{2,1,0:T(8,128)(2,1)}), bf16[8,64,256]{2,1,0:T(8,128)(2,1)S(1)}, u32[]{:S(2)}, u32[]{:S(2)}) async-start(bf16[8,64,256]{2,1,0:T(8,128)(2,1)} %get-tuple-element.14), calls=%async_computation | async-start | bytes 524288 | tf_op jit(solution)/shard_map/all_to_all | solution.py:281
  9.3 1.2 %copy-done = bf16[1024,512]{1,0:T(8,128)(2,1)S(1)} copy-done((bf16[1024,512]{1,0:T(8,128)(2,1)S(1)}, bf16[1024,512]{1,0:T(8,128)(2,1)}, u32[]{:S(2)}) %copy-start) | copy-done | bytes 1048600
  10.5 0.9 %copy-done.3 = bf16[256,512]{1,0:T(8,128)(2,1)S(1)} copy-done((bf16[256,512]{1,0:T(8,128)(2,1)S(1)}, bf16[256,512]{1,0:T(8,128)(2,1)}, u32[]{:S(2)}) %copy-start.3) | copy-done | bytes 262168
  11.4 0.5 shard_map.114
  11.9 0.0 copy-start.8
  11.9 1.6 %collective-permute-start.3 = (bf16[256,256]{1,0:T(8,128)(2,1)S(1)}, bf16[256,256]{1,0:T(8,128)(2,1)S(1)}, u32[]{:S(2)}, u32[]{:S(2)}) collective-permute-start(bf16[256,256]{1,0:T(8,128)(2,1)S(1)} %get-tuple-element.17), channel_id=1, source_target_pairs={{0,1},{1,2},{2,3},{3,0},{4,5},{5,6},{6,7},{7,4},{8,9},{9,10},{10,1... | collective-permute-start | bytes 393224 | tf_op jit(solution)/shard_map/ppermute | solution.py:297
  13.6 2.6 %collective-permute-start.4 = (bf16[256,256]{1,0:T(8,128)(2,1)S(1)}, bf16[256,256]{1,0:T(8,128)(2,1)S(1)}, u32[]{:S(2)}, u32[]{:S(2)}) collective-permute-start(bf16[256,256]{1,0:T(8,128)(2,1)S(1)} %get-tuple-element.18), channel_id=1, source_target_pairs={{0,2},{1,3},{2,0},{3,1},{4,6},{5,7},{6,4},{7,5},{8,10},{9,11},{10,... | collective-permute-start | bytes 393224 | tf_op jit(solution)/shard_map/ppermute | solution.py:297
  16.1 1.4 %collective-permute-start.5 = (bf16[256,256]{1,0:T(8,128)(2,1)S(1)}, bf16[256,256]{1,0:T(8,128)(2,1)S(1)}, u32[]{:S(2)}, u32[]{:S(2)}) collective-permute-start(bf16[256,256]{1,0:T(8,128)(2,1)S(1)} %get-tuple-element.19), channel_id=1, source_target_pairs={{0,3},{1,0},{2,1},{3,2},{4,7},{5,4},{6,5},{7,6},{8,11},{9,8},{10,9... | collective-permute-start | bytes 393224 | tf_op jit(solution)/shard_map/ppermute | solution.py:297
  17.5 0.0 all-to-all-done.pair_ref
  17.5 1.6 %shard_map.112 = (bf16[8,32,256]{2,1,0:T(8,128)(2,1)}, f32[576,512]{1,0:T(8,128)S(1)}) custom-call(bf16[8,64,256]{2,1,0:T(8,128)(2,1)S(1)} %all-to-all-done.pair_ref, bf16[512,512]{1,0:T(8,128)(2,1)S(1)} %copy-done.2, f32[9,2,256]{2,1,0:T(2,128)S(1)} %copy-done.6), custom_call_target="tpu_custom_call" | custom-call | flops 452984832 | bytes 1179648 | tf_op jit(solution)/shard_map/pallas_call | solution.py:317
  19.1 4.2 %all-to-all-start.1 = ((bf16[8,32,256]{2,1,0:T(8,128)(2,1)}), bf16[8,32,256]{2,1,0:T(8,128)(2,1)S(1)}, u32[]{:S(2)}, u32[]{:S(2)}) async-start(bf16[8,32,256]{2,1,0:T(8,128)(2,1)} %get-tuple-element.15), calls=%async_computation.1 | async-start | bytes 262144 | tf_op jit(solution)/shard_map/all_to_all | solution.py:281
  23.3 0.0 collective-permute-done.3
  23.3 2.1 %collective-permute-done.4 = bf16[256,256]{1,0:T(8,128)(2,1)S(1)} collective-permute-done((bf16[256,256]{1,0:T(8,128)(2,1)S(1)}, bf16[256,256]{1,0:T(8,128)(2,1)S(1)}, u32[]{:S(2)}, u32[]{:S(2)}) %collective-permute-start.4) | collective-permute-done | bytes 131104 | tf_op jit(solution)/shard_map/ppermute | solution.py:297
  25.4 0.0 collective-permute-done.5
  25.4 3.4 %all-to-all-done.1 = bf16[8,32,256]{2,1,0:T(8,128)(2,1)S(1)} async-done(((bf16[8,32,256]{2,1,0:T(8,128)(2,1)}), bf16[8,32,256]{2,1,0:T(8,128)(2,1)S(1)}, u32[]{:S(2)}, u32[]{:S(2)}) %all-to-all-start.1) | async-done | bytes 131104 | tf_op jit(solution)/shard_map/all_to_all | solution.py:281
  28.9 0.8 %convert_multiply_fusion = (f32[256,256]{1,0:T(8,128)}, bf16[256,256]{1,0:T(8,128)(2,1)S(1)}, bf16[256,256]{1,0:T(8,128)(2,1)S(1)}) fusion(bf16[8,32,256]{2,1,0:T(8,128)(2,1)S(1)} %all-to-all-done.1, bf16[256,256]{1,0:T(8,128)(2,1)S(1)} %collective-permute-done.5, bf16[256,256]{1,0:T(8,128)(2,1)S(1)} %collective-permute-done.4, ...), kind=kLoop, calls=%fused_computation | loop fusion | flops 851968 | bytes 1441792 | tf_op jit(solution)/shard_map/mul | solution.py:334
  29.7 7.9 %all_to_all.20.grad_ref = bf16[8,32,256]{2,1,0:T(8,128)(2,1)S(1)} all-to-all(bf16[8,32,256]{2,1,0:T(8,128)(2,1)S(1)} %bitcast.7), channel_id=1, replica_groups=mesh['seq'=8,'chan'=4] {'seq'}, dimensions={0} | all-to-all | bytes 262144 | tf_op jit(solution)/shard_map/all_to_all | solution.py:281
  37.6 1.7 %shard_map.115 = bf16[8,64,256]{2,1,0:T(8,128)(2,1)} custom-call(bf16[8,32,256]{2,1,0:T(8,128)(2,1)S(1)} %all_to_all.20.grad_ref, f32[576,512]{1,0:T(8,128)S(1)} %get-tuple-element.20.spec_ref, bf16[512,512]{1,0:T(8,128)(2,1)S(1)} %copy-done.2, f32[9,2,256]{2,1,0:T(2,128)S(1)} %copy-done.6), custom_call_target="tpu_custom_call" | custom-call | flops 452984832 | bytes 1179648 | tf_op jit(solution)/shard_map/pallas_call | solution.py:345
  39.3 3.4 %all-to-all-start.3 = ((bf16[8,64,256]{2,1,0:T(8,128)(2,1)}), bf16[8,64,256]{2,1,0:T(8,128)(2,1)S(1)}, u32[]{:S(2)}, u32[]{:S(2)}) async-start(bf16[8,64,256]{2,1,0:T(8,128)(2,1)} %shard_map.115), calls=%async_computation.3 | async-start | bytes 524288 | tf_op jit(solution)/shard_map/all_to_all | solution.py:281
  42.8 2.3 %collective-permute-start.2 = (bf16[256,256]{1,0:T(8,128)(2,1)S(1)}, bf16[256,256]{1,0:T(8,128)(2,1)S(1)}, u32[]{:S(2)}, u32[]{:S(2)}) collective-permute-start(bf16[256,256]{1,0:T(8,128)(2,1)S(1)} %get-tuple-element.26.refs_0_), channel_id=1, source_target_pairs={{0,3},{1,0},{2,1},{3,2},{4,7},{5,4},{6,5},{7,6},{8,11},{9,8},{10,9... | collective-permute-start | bytes 393224 | tf_op jit(solution)/shard_map/ppermute | solution.py:297
  45.0 0.4 collective-permute-start.1
  45.4 0.3 collective-permute-start
  45.7 3.3 %collective-permute-done.2.refs_3_ = bf16[256,256]{1,0:T(8,128)(2,1)S(1)} collective-permute-done((bf16[256,256]{1,0:T(8,128)(2,1)S(1)}, bf16[256,256]{1,0:T(8,128)(2,1)S(1)}, u32[]{:S(2)}, u32[]{:S(2)}) %collective-permute-start.2) | collective-permute-done | bytes 131104 | tf_op jit(solution)/shard_map/ppermute | solution.py:297
  48.9 8.6 %collective-permute-done.1.refs_2_ = bf16[256,256]{1,0:T(8,128)(2,1)S(1)} collective-permute-done((bf16[256,256]{1,0:T(8,128)(2,1)S(1)}, bf16[256,256]{1,0:T(8,128)(2,1)S(1)}, u32[]{:S(2)}, u32[]{:S(2)}) %collective-permute-start.1) | collective-permute-done | bytes 131104 | tf_op jit(solution)/shard_map/ppermute | solution.py:297
  57.6 0.0 collective-permute-done.refs_1_
  57.6 1.2 %shard_map.113 = bf16[256,512]{1,0:T(8,128)(2,1)} custom-call(bf16[1024,512]{1,0:T(8,128)(2,1)S(1)} %copy-done.1, bf16[256,256]{1,0:T(8,128)(2,1)S(1)} %get-tuple-element.26.refs_0_, bf16[256,256]{1,0:T(8,128)(2,1)S(1)} %collective-permute-done.refs_1_, bf16[256,256]{1,0:T(8,128)(2,1)S(1)} %collective-permute-done.1.refs_2_, ...), custom_call_target="tpu_custom_call" | custom-call | flops 268435456 | bytes 1048576 | tf_op jit(solution)/shard_map/pallas_call | solution.py:337
  58.7 0.8 %shard_map.116 = (f32[256,256]{1,0:T(8,128)}, f32[256,256]{1,0:T(8,128)}) custom-call(bf16[8,64,256]{2,1,0:T(8,128)(2,1)S(1)} %all-to-all-done.3.back_ref, f32[256,256]{1,0:T(8,128)S(1)} %get-tuple-element.21.window_ref), custom_call_target="tpu_custom_call" | custom-call | tf_op jit(solution)/shard_map/pallas_call | solution.py:355
  (12 shorter events, 0.0 us)
Async XLA Ops:
  0.6 16.9 %copy-start.2 = (bf16[512,512]{1,0:T(8,128)(2,1)S(1)}, bf16[512,512]{1,0:T(8,128)(2,1)}, u32[]{:S(2)}) copy-start(bf16[512,512]{1,0:T(8,128)(2,1)} %constant.4.clone.table_ref) | copy-start | bytes 1572868
  0.6 1.0 %copy-start.4 = (f32[256,256]{1,0:T(8,128)S(1)}, f32[256,256]{1,0:T(8,128)}, u32[]{:S(2)}) copy-start(f32[256,256]{1,0:T(8,128)} %taps_ref.1) | copy-start | bytes 786436
  1.7 0.9 %copy-start.5 = (bf16[256,256]{1,0:T(8,128)(2,1)S(1)}, bf16[256,256]{1,0:T(8,128)(2,1)}, u32[]{:S(2)}) copy-start(bf16[256,256]{1,0:T(8,128)(2,1)} %signal_ref.1) | copy-start | bytes 393220
  2.6 0.7 %copy-start.7 = (f32[256]{0:T(256)S(1)}, f32[256]{0:T(256)}, u32[]{:S(2)}) copy-start(f32[256]{0:T(256)} %param.11) | copy-start | bytes 3076
  3.2 14.3 %copy-start.6 = (f32[9,2,256]{2,1,0:T(2,128)S(1)}, f32[9,2,256]{2,1,0:T(2,128)}, u32[]{:S(2)}) copy-start(f32[9,2,256]{2,1,0:T(2,128)} %constant.5.clone.twiddle_ref) | copy-start | bytes 55300
  4.1 13.4 %all-to-all-start = ((bf16[8,64,256]{2,1,0:T(8,128)(2,1)}), bf16[8,64,256]{2,1,0:T(8,128)(2,1)S(1)}, u32[]{:S(2)}, u32[]{:S(2)}) async-start(bf16[8,64,256]{2,1,0:T(8,128)(2,1)} %get-tuple-element.14), calls=%async_computation | async-start | bytes 524288 | tf_op jit(solution)/shard_map/all_to_all | solution.py:281
  9.3 1.2 %copy-start = (bf16[1024,512]{1,0:T(8,128)(2,1)S(1)}, bf16[1024,512]{1,0:T(8,128)(2,1)}, u32[]{:S(2)}) copy-start(bf16[1024,512]{1,0:T(8,128)(2,1)} %weight_ref.3) | copy-start | bytes 3145732
  10.5 0.9 %copy-start.3 = (bf16[256,512]{1,0:T(8,128)(2,1)S(1)}, bf16[256,512]{1,0:T(8,128)(2,1)}, u32[]{:S(2)}) copy-start(bf16[256,512]{1,0:T(8,128)(2,1)} %grad_ref.1) | copy-start | bytes 786436
  11.9 16.9 %copy-start.8 = (bf16[256,256]{1,0:T(8,128)(2,1)S(1)}, bf16[256,256]{1,0:T(8,128)(2,1)}, u32[]{:S(2)}) copy-start(bf16[256,256]{1,0:T(8,128)(2,1)} %param.9) | copy-start | bytes 393220
  11.9 11.4 %collective-permute-start.3 = (bf16[256,256]{1,0:T(8,128)(2,1)S(1)}, bf16[256,256]{1,0:T(8,128)(2,1)S(1)}, u32[]{:S(2)}, u32[]{:S(2)}) collective-permute-start(bf16[256,256]{1,0:T(8,128)(2,1)S(1)} %get-tuple-element.17), channel_id=1, source_target_pairs={{0,1},{1,2},{2,3},{3,0},{4,5},{5,6},{6,7},{7,4},{8,9},{9,10},{10,1... | collective-permute-start | bytes 393224 | tf_op jit(solution)/shard_map/ppermute | solution.py:297
  13.6 11.9 %collective-permute-start.4 = (bf16[256,256]{1,0:T(8,128)(2,1)S(1)}, bf16[256,256]{1,0:T(8,128)(2,1)S(1)}, u32[]{:S(2)}, u32[]{:S(2)}) collective-permute-start(bf16[256,256]{1,0:T(8,128)(2,1)S(1)} %get-tuple-element.18), channel_id=1, source_target_pairs={{0,2},{1,3},{2,0},{3,1},{4,6},{5,7},{6,4},{7,5},{8,10},{9,11},{10,... | collective-permute-start | bytes 393224 | tf_op jit(solution)/shard_map/ppermute | solution.py:297
  16.1 9.3 %collective-permute-start.5 = (bf16[256,256]{1,0:T(8,128)(2,1)S(1)}, bf16[256,256]{1,0:T(8,128)(2,1)S(1)}, u32[]{:S(2)}, u32[]{:S(2)}) collective-permute-start(bf16[256,256]{1,0:T(8,128)(2,1)S(1)} %get-tuple-element.19), channel_id=1, source_target_pairs={{0,3},{1,0},{2,1},{3,2},{4,7},{5,4},{6,5},{7,6},{8,11},{9,8},{10,9... | collective-permute-start | bytes 393224 | tf_op jit(solution)/shard_map/ppermute | solution.py:297
  19.1 9.7 %all-to-all-start.1 = ((bf16[8,32,256]{2,1,0:T(8,128)(2,1)}), bf16[8,32,256]{2,1,0:T(8,128)(2,1)S(1)}, u32[]{:S(2)}, u32[]{:S(2)}) async-start(bf16[8,32,256]{2,1,0:T(8,128)(2,1)} %get-tuple-element.15), calls=%async_computation.1 | async-start | bytes 262144 | tf_op jit(solution)/shard_map/all_to_all | solution.py:281
  37.6 20.0 %copy-start.1 = (bf16[1024,512]{1,0:T(8,128)(2,1)S(1)}, bf16[1024,512]{1,0:T(8,128)(2,1)}, u32[]{:S(2)}) copy-start(bf16[1024,512]{1,0:T(8,128)(2,1)} %weight_ref.3) | copy-start | bytes 3145732
  39.3 19.4 %all-to-all-start.3 = ((bf16[8,64,256]{2,1,0:T(8,128)(2,1)}), bf16[8,64,256]{2,1,0:T(8,128)(2,1)S(1)}, u32[]{:S(2)}, u32[]{:S(2)}) async-start(bf16[8,64,256]{2,1,0:T(8,128)(2,1)} %shard_map.115), calls=%async_computation.3 | async-start | bytes 524288 | tf_op jit(solution)/shard_map/all_to_all | solution.py:281
  42.8 6.2 %collective-permute-start.2 = (bf16[256,256]{1,0:T(8,128)(2,1)S(1)}, bf16[256,256]{1,0:T(8,128)(2,1)S(1)}, u32[]{:S(2)}, u32[]{:S(2)}) collective-permute-start(bf16[256,256]{1,0:T(8,128)(2,1)S(1)} %get-tuple-element.26.refs_0_), channel_id=1, source_target_pairs={{0,3},{1,0},{2,1},{3,2},{4,7},{5,4},{6,5},{7,6},{8,11},{9,8},{10,9... | collective-permute-start | bytes 393224 | tf_op jit(solution)/shard_map/ppermute | solution.py:297
  45.0 12.5 %collective-permute-start.1 = (bf16[256,256]{1,0:T(8,128)(2,1)S(1)}, bf16[256,256]{1,0:T(8,128)(2,1)S(1)}, u32[]{:S(2)}, u32[]{:S(2)}) collective-permute-start(bf16[256,256]{1,0:T(8,128)(2,1)S(1)} %get-tuple-element.26.refs_0_), channel_id=1, source_target_pairs={{0,2},{1,3},{2,0},{3,1},{4,6},{5,7},{6,4},{7,5},{8,10},{9,11},{10,... | collective-permute-start | bytes 393224 | tf_op jit(solution)/shard_map/ppermute | solution.py:297
  45.4 12.2 %collective-permute-start = (bf16[256,256]{1,0:T(8,128)(2,1)S(1)}, bf16[256,256]{1,0:T(8,128)(2,1)S(1)}, u32[]{:S(2)}, u32[]{:S(2)}) collective-permute-start(bf16[256,256]{1,0:T(8,128)(2,1)S(1)} %get-tuple-element.26.refs_0_), channel_id=1, source_target_pairs={{0,1},{1,2},{2,3},{3,0},{4,5},{5,6},{6,7},{7,4},{8,9},{9,10},{10,1... | collective-permute-start | bytes 393224 | tf_op jit(solution)/shard_map/ppermute | solution.py:297
where the time goes:
time: 60.1 us; the launch traced here: 59.6 us
  starting transfers between devices  21.2 us (35%)
  waiting for transfers between devices  17.4 us (29%)
  blocking collectives  7.91 us (13%)
  Pallas kernels  6.69 us (11%)
  local copies, waits for them, and re-layouts  4.77 us (8%)
  other arithmetic  0.83 us (1%)
  between operations  0.7 us (1%)
    ppermute x6, waiting for transfers between devices, shift(): lax.ppermute(array, 'chan', [(i, (i + step) % parts) for i in range(parts)])  14 us
    all_to_all x3, starting transfers between devices, exchange(): return lax.all_to_all(array, 'seq', split_axis=0, concat_axis=0, tiled=True)  12.8 us
    ppermute x6, starting transfers between devices, shift(): lax.ppermute(array, 'chan', [(i, (i + step) % parts) for i in range(parts)])  8.45 us
    all_to_all x1, blocking collectives, exchange(): return lax.all_to_all(array, 'seq', split_axis=0, concat_axis=0, tiled=True)  7.91 us
    unnamed x18, local copies, waits for them, and re-layouts  4.77 us
    all_to_all x3, waiting for transfers between devices, exchange(): return lax.all_to_all(array, 'seq', split_axis=0, concat_axis=0, tiled=True)  3.43 us
    pallas_call x1, Pallas kernels, per_device(): call(correlate_kernel, shape((shards, 2 * held, length), bf16), 4, (pltpu...  1.73 us
    pallas_call x1, Pallas kernels, per_device(): call(convolve_kernel, (shape((shards, held, length), bf16), shape((2 * he...  1.63 us
  transfers between devices with their start and end apart: 9, of which 4 were waited for; matrix products, arithmetic and copies ran while one was open for 0% of the time, Pallas kernels for 5%

commit v1 on v0

--- a/solution.py
+++ b/solution.py
@@ -12,19 +12,23 @@
 f32 = jnp.float32
 bf16 = jnp.bfloat16
 VMEM = pl.BlockSpec(memory_space=pltpu.VMEM)
+ANY = pl.BlockSpec(memory_space=pl.ANY)
+PEAK_FLOPS_A_MICRO = 1.15e9
 ROWS = 16
 LANES = 128
 
 
-def call(kernel, out_shape, count, scratch=(), flops=0, moved=0):
+def call(kernel, out_shape, in_specs, scratch=(), micros=1, out_specs=None, moved=0, room=16):
     return pl.pallas_call(
         kernel,
         out_shape=out_shape,
-        in_specs=[VMEM] * count,
-        out_specs=jax.tree.map(lambda _: VMEM, out_shape),
+        in_specs=in_specs,
+        out_specs=jax.tree.map(lambda _: VMEM, out_shape) if out_specs is None else out_specs,
         scratch_shapes=list(scratch),
-        cost_estimate=pl.CostEstimate(flops=flops, bytes_accessed=moved, transcendentals=0),
-        compiler_params=pltpu.CompilerParams(vmem_limit_bytes=48 * 1024 * 1024),
+        cost_estimate=pl.CostEstimate(
+            flops=int(micros * PEAK_FLOPS_A_MICRO), bytes_accessed=moved, transcendentals=0
+        ),
+        compiler_params=pltpu.CompilerParams(vmem_limit_bytes=room * 1024 * 1024),
     )
 
 
@@ -169,17 +173,38 @@
     out_ref[base : base + rows, lanes:] = real.astype(bf16)
 
 
-def convolve_kernel(pair_ref, table_ref, twiddle_ref, mixed_ref, spec_ref, left_ref, back_ref):
+def convolve_kernel(
+    pair_ref,
+    table_ref,
+    twiddle_ref,
+    mixed_ref,
+    signal_real,
+    signal_imag,
+    filter_real,
+    filter_imag,
+    left_ref,
+    back_ref,
+):
     blocks, rows, lanes = mixed_ref.shape
     height = (blocks + 1) * rows
     first_step(tile_read(pair_ref, 0), twiddle_ref, left_ref, 0, blocks, rows, lanes)
     first_step(tile_read(pair_ref, rows), twiddle_ref, left_ref, height, blocks, rows, lanes)
-    spec_ref[...] = jnp.dot(left_ref[...], table_ref[...], preferred_element_type=f32)
+    spectra = []
+    for base, real_ref, imag_ref in (
+        (0, signal_real, signal_imag),
+        (height, filter_real, filter_imag),
+    ):
+        spectrum = jnp.dot(
+            left_ref[base : base + height], table_ref[...], preferred_element_type=f32
+        )
+        real_ref[...] = spectrum[:, :lanes].astype(bf16)
+        imag_ref[...] = spectrum[:, lanes:].astype(bf16)
+        spectra.append(spectrum)
     product(
-        spec_ref[:height, :lanes],
-        spec_ref[:height, lanes:],
-        spec_ref[height:, :lanes],
-        spec_ref[height:, lanes:],
+        spectra[0][:, :lanes],
+        spectra[0][:, lanes:],
+        spectra[1][:, :lanes],
+        spectra[1][:, lanes:],
         left_ref,
         0,
         False,
@@ -188,17 +213,31 @@
     last_step(back_ref, 0, twiddle_ref, tile_write(mixed_ref, 0), blocks, rows, lanes)
 
 
-def correlate_kernel(grad_ref, spec_ref, table_ref, twiddle_ref, out_ref, left_ref, back_ref):
+def correlate_kernel(
+    grad_ref,
+    signal_real,
+    signal_imag,
+    filter_real,
+    filter_imag,
+    table_ref,
+    twiddle_ref,
+    out_ref,
+    left_ref,
+    back_ref,
+):
     blocks, rows, lanes = grad_ref.shape
     height = (blocks + 1) * rows
     first_step(tile_read(grad_ref, 0), twiddle_ref, left_ref, 0, blocks, rows, lanes)
     grad = jnp.dot(left_ref[:height], table_ref[...], preferred_element_type=f32)
-    for base, other in ((0, height), (height, 0)):
+    for base, real_ref, imag_ref in (
+        (0, filter_real, filter_imag),
+        (height, signal_real, signal_imag),
+    ):
         product(
             grad[:, :lanes],
             grad[:, lanes:],
-            spec_ref[other : other + height, :lanes],
-            spec_ref[other : other + height, lanes:],
+            real_ref[...].astype(f32),
+            imag_ref[...].astype(f32),
             left_ref,
             base,
             True,
@@ -208,15 +247,28 @@
     last_step(back_ref, height, twiddle_ref, tile_write(out_ref, rows), blocks, rows, lanes)
 
 
-def window_kernel(decay_ref, taps_ref, signal_ref, pair_ref, window_ref):
+def window_kernel(
+    decay_in, taps_in, signal_in, pair_ref, window_ref, decay_ref, taps_ref, signal_ref, sems
+):
+    fetches = [
+        pltpu.make_async_copy(source, target, sems.at[at])
+        for at, (source, target) in enumerate(
+            ((decay_in, decay_ref), (taps_in, taps_ref), (signal_in, signal_ref))
+        )
+    ]
+    for fetch in fetches:
+        fetch.start()
     channels, length = taps_ref.shape
     shards, twice, _ = pair_ref.shape
     owned = twice // 2
     start = lax.axis_index("seq") * length
     places = (start + lax.broadcasted_iota(jnp.int32, (1, length), 1)).astype(f32)
+    fetches[0].wait()
     rates = jnp.broadcast_to(decay_ref[...], (length, channels)).T
     window = jnp.exp(-rates * places) * jnp.sqrt(2.0 * rates)
     window_ref[...] = window
+    fetches[1].wait()
+    fetches[2].wait()
     filters = (taps_ref[...] * window).astype(bf16)
     for shard in range(shards):
         rows = slice(shard * owned, (shard + 1) * owned)
@@ -234,6 +286,18 @@
         out_refs[step][...] = lax.dot_general(
             block, grad_ref[...], (((1,), (1,)), ((), ())), preferred_element_type=f32
         ).astype(out_refs[step].dtype)
+
+
+def gate_kernel(gating_ref, mixed_ref, *refs):
+    gating_grad_ref, grad_mixed_ref, gated_ref = refs[-3:]
+    total = refs[0][...].astype(f32)
+    for share in refs[1:-3]:
+        total = total + share[...].astype(f32)
+    gates = gating_ref[...].astype(f32)
+    mixed = mixed_ref[...].astype(f32)
+    grad_mixed_ref[...] = (total * gates).astype(bf16)
+    gated_ref[...] = (gates * mixed).astype(bf16)
+    gating_grad_ref[...] = total * mixed
 
 
 def project_kernel(weight_ref, *refs):
@@ -291,71 +355,81 @@
     table = jnp.asarray(within_table(length))
     twiddle = jnp.asarray(twiddle_table(shards, length))
     shape = jax.ShapeDtypeStruct
-    pass_flops = 2 * height * (2 * length) ** 2
 
     def shift(array, step):
         return lax.ppermute(array, "chan", [(i, (i + step) % parts) for i in range(parts)])
 
-    pairs, window = call(
-        window_kernel,
-        (shape((shards, 2 * held, length), bf16), shape((channels, length), f32)),
-        3,
-    )(decay_rates.reshape(1, channels), filter_taps, signal) if owned == held else window_plain(
-        decay_rates, filter_taps, signal, shards
-    )
+    if owned == held:
+        pairs, window = call(
+            window_kernel,
+            (shape((shards, 2 * owned, length), bf16), shape((channels, length), f32)),
+            [ANY] * 3,
+            (
+                pltpu.VMEM((1, channels), f32),
+                pltpu.VMEM((channels, length), f32),
+                pltpu.VMEM((channels, length), bf16),
+                pltpu.SemaphoreType.DMA((3,)),
+            ),
+            room=62,
+        )(decay_rates.reshape(1, channels), filter_taps, signal)
+    else:
+        pairs, window = window_plain(decay_rates, filter_taps, signal, shards)
     arrived = exchange(pairs)
 
     partial = call(
         spread_kernel,
-        tuple(shape((channels, length), f32 if k == 0 else bf16) for k in range(parts)),
-        2,
-        flops=2 * out_weight.shape[0] * out_weight.shape[1] * length,
-        moved=2 * out_weight.size,
+        tuple(shape((channels, length), bf16) for k in range(parts)),
+        [VMEM] * 2,
+        micros=1.0,
     )(out_weight, out_grad)
     shares = [shift(partial[step], step) for step in range(1, parts)]
 
-    mixed_owned, spectra = call(
+    mixed_owned, *spectra = call(
         convolve_kernel,
-        (shape((shards, held, length), bf16), shape((2 * height, 2 * length), f32)),
-        3,
-        (pltpu.VMEM((2 * height, 2 * length), bf16), pltpu.VMEM((height, 2 * length), f32)),
-        flops=3 * pass_flops,
-        moved=4 * 2 * height * 2 * length,
+        (shape((shards, held, length), bf16),) + 4 * (shape((height, length), bf16),),
+        [VMEM] * 3,
+        (
+            pltpu.VMEM((2 * height, 2 * length), bf16),
+            pltpu.VMEM((height, 2 * length), f32),
+        ),
+        micros=2.0,
     )(padded(arrived, owned, held), table, twiddle)
-    mixed = exchange(trimmed(mixed_owned, owned, held)).reshape(channels, length).astype(f32)
-
-    gate_values = gating.astype(f32)
-    grad_mixed_out = partial[0]
-    for share in shares:
-        grad_mixed_out = grad_mixed_out + share.astype(f32)
-    grad_mixed = (grad_mixed_out * gate_values).astype(bf16)
+    mixed = exchange(trimmed(mixed_owned, owned, held)).reshape(channels, length)
+
+    gating_grad, grad_mixed, gated = call(
+        gate_kernel,
+        (
+            shape((channels, length), f32),
+            shape((channels, length), bf16),
+            shape((channels, length), bf16),
+        ),
+        [VMEM] * (3 + len(shares)),
+    )(gating, mixed, partial[0], *shares)
     grad_whole = exchange(grad_mixed.reshape(shards, owned, length))
-
-    gating_grad = grad_mixed_out * mixed
-    gated = (gate_values * mixed).astype(bf16)
     gathered = [gated] + [shift(gated, step) for step in range(1, parts)]
     mixed_out = call(
         project_kernel,
         shape((length, out_weight.shape[1]), bf16),
-        1 + parts,
-        flops=2 * out_weight.shape[0] * out_weight.shape[1] * length,
-        moved=2 * out_weight.size,
+        [VMEM] * (1 + parts),
+        micros=12.0,
     )(out_weight, *gathered)
 
     grads_owned = call(
         correlate_kernel,
         shape((shards, 2 * held, length), bf16),
-        4,
-        (pltpu.VMEM((2 * height, 2 * length), bf16), pltpu.VMEM((2 * height, 2 * length), f32)),
-        flops=3 * pass_flops,
-        moved=4 * 2 * height * 2 * length,
-    )(padded(grad_whole, owned, held), spectra, table, twiddle)
+        [VMEM] * 7,
+        (
+            pltpu.VMEM((2 * height, 2 * length), bf16),
+            pltpu.VMEM((2 * height, 2 * length), f32),
+        ),
+        micros=2.0,
+    )(padded(grad_whole, owned, held), *spectra, table, twiddle)
     returned = exchange(trimmed(grads_owned, owned, held))
     if owned == held:
         signal_grad, taps_grad = call(
             return_kernel,
             (shape((channels, length), f32), shape((channels, length), f32)),
-            2,
+            [VMEM] * 2,
         )(returned, window)
     else:
         both = returned.reshape(shards, 2, owned, length).astype(f32)

time: 60.1 us -> 48.6 us (0.81)
  blocking collectives: 7.91 us -> 0 us
  local copies, waits for them, and re-layouts: 4.77 us -> 0.03 us
  starting transfers between devices: 21.2 us -> 25.8 us
  waiting for transfers between devices: 17.4 us -> 12.8 us
  Pallas kernels: 6.69 us -> 8.59 us
  other arithmetic: 0.83 us -> 0 us
    all_to_all x1 -> x0, blocking collectives: 7.91 us -> none  [exchange(): return lax.all_to_all(array, 'seq', split_axis=0, concat_axis=0, tiled=True)]
    ppermute x6, waiting for transfers between devices: 14 us -> 6.86 us  [shift(): lax.ppermute(array, 'chan', [(i, (i + step) % parts) for i in range(parts)])]
    unnamed x18 -> x12, local copies, waits for them, and re-layouts: 4.77 us -> 0.03 us
    all_to_all x3 -> x4, starting transfers between devices: 12.8 us -> 15.6 us  [exchange(): return lax.all_to_all(array, 'seq', split_axis=0, concat_axis=0, tiled=True)]
    all_to_all x3 -> x4, waiting for transfers between devices: 3.43 us -> 5.98 us  [exchange(): return lax.all_to_all(array, 'seq', split_axis=0, concat_axis=0, tiled=True)]
    pallas_call x5 -> x6, Pallas kernels: 5.87 us -> 7.76 us  [the longest x1 1.9 us: per_device(): call(window_kernel, (shape((shards, 2 * owned, length), bf16), shape((cha...]
    ppermute x6, starting transfers between devices: 8.45 us -> 10.2 us  [shift(): lax.ppermute(array, 'chan', [(i, (i + step) % parts) for i in range(parts)])]
    mul x1 -> x0, other arithmetic: 0.83 us -> none  [per_device(): gating_grad = grad_mixed_out * mixed]
  transfers between devices with their start and end apart: 9 -> 10, of which waited for: 4 -> 6; matrix products, arithmetic and copies ran while one was open for 0% -> 0% of each run, Pallas kernels for 5% -> 10%
where the time goes in v1:
time: 48.6 us; the launch traced here: 48 us
  starting transfers between devices  25.8 us (53%)
  waiting for transfers between devices  12.8 us (26%)
  Pallas kernels  8.59 us (18%)
  between operations  0.75 us (2%)
    all_to_all x4, starting transfers between devices, exchange(): return lax.all_to_all(array, 'seq', split_axis=0, concat_axis=0, tiled=True)  15.6 us
    ppermute x6, starting transfers between devices, shift(): lax.ppermute(array, 'chan', [(i, (i + step) % parts) for i in range(parts)])  10.2 us
    ppermute x6, waiting for transfers between devices, shift(): lax.ppermute(array, 'chan', [(i, (i + step) % parts) for i in range(parts)])  6.86 us
    all_to_all x4, waiting for transfers between devices, exchange(): return lax.all_to_all(array, 'seq', split_axis=0, concat_axis=0, tiled=True)  5.98 us
    pallas_call x1, Pallas kernels, per_device(): call(window_kernel, (shape((shards, 2 * owned, length), bf16), shape((cha...  1.9 us
    pallas_call x1, Pallas kernels, per_device(): call(correlate_kernel, shape((shards, 2 * held, length), bf16), [VMEM] *...  1.78 us
    pallas_call x1, Pallas kernels, per_device(): call(convolve_kernel, (shape((shards, held, length), bf16),) + 4 * (shape...  1.62 us
    pallas_call x1, Pallas kernels, per_device(): call(project_kernel, shape((length, out_weight.shape[1]), bf16), [VMEM] *...  1.17 us
  transfers between devices with their start and end apart: 10, of which 6 were waited for; matrix products, arithmetic and copies ran while one was open for 0% of the time, Pallas kernels for 10%

profile of v1, /device:TPU:0, one launch (start us, length us, event | category | flops | bytes accessed | tf_op | source)
XLA Modules:
  0.0 48.0 jit_solution(11324568297555147256)
XLA Ops:
  0.6 1.9 %shard_map.111 = (bf16[8,64,256]{2,1,0:T(8,128)(2,1)}, f32[256,256]{1,0:T(8,128)}) custom-call(f32[1,256]{1,0:T(1,128)} %bitcast.4, f32[256,256]{1,0:T(8,128)} %taps_in.1, bf16[256,256]{1,0:T(8,128)(2,1)} %signal_in.1), custom_call_target="tpu_custom_call" | custom-call | flops 1150000000 | tf_op jit(solution)/shard_map/pallas_call | solution.py:363
  2.6 0.0 copy-start.1
  2.6 5.3 %all-to-all-start = ((bf16[8,64,256]{2,1,0:T(8,128)(2,1)}), bf16[8,64,256]{2,1,0:T(8,128)(2,1)S(1)}, u32[]{:S(2)}, u32[]{:S(2)}) async-start(bf16[8,64,256]{2,1,0:T(8,128)(2,1)} %get-tuple-element.20), calls=%async_computation | async-start | bytes 524288 | tf_op jit(solution)/shard_map/all_to_all | solution.py:345
  7.9 0.0 copy-start.3
  7.9 0.0 copy-start.4
  7.9 0.5 shard_map.113
  8.4 1.6 %collective-permute-start = (bf16[256,256]{1,0:T(8,128)(2,1)S(1)}, bf16[256,256]{1,0:T(8,128)(2,1)S(1)}, u32[]{:S(2)}, u32[]{:S(2)}) collective-permute-start(bf16[256,256]{1,0:T(8,128)(2,1)S(1)} %get-tuple-element.23), channel_id=1, source_target_pairs={{0,1},{1,2},{2,3},{3,0},{4,5},{5,6},{6,7},{7,4},{8,9},{9,10},{10,1... | collective-permute-start | bytes 393224 | tf_op jit(solution)/shard_map/ppermute | solution.py:360
  10.0 2.6 %collective-permute-start.1 = (bf16[256,256]{1,0:T(8,128)(2,1)S(1)}, bf16[256,256]{1,0:T(8,128)(2,1)S(1)}, u32[]{:S(2)}, u32[]{:S(2)}) collective-permute-start(bf16[256,256]{1,0:T(8,128)(2,1)S(1)} %get-tuple-element.24), channel_id=1, source_target_pairs={{0,2},{1,3},{2,0},{3,1},{4,6},{5,7},{6,4},{7,5},{8,10},{9,11},{10,... | collective-permute-start | bytes 393224 | tf_op jit(solution)/shard_map/ppermute | solution.py:360
  12.6 1.3 %collective-permute-start.2 = (bf16[256,256]{1,0:T(8,128)(2,1)S(1)}, bf16[256,256]{1,0:T(8,128)(2,1)S(1)}, u32[]{:S(2)}, u32[]{:S(2)}) collective-permute-start(bf16[256,256]{1,0:T(8,128)(2,1)S(1)} %get-tuple-element.25), channel_id=1, source_target_pairs={{0,3},{1,0},{2,1},{3,2},{4,7},{5,4},{6,5},{7,6},{8,11},{9,8},{10,9... | collective-permute-start | bytes 393224 | tf_op jit(solution)/shard_map/ppermute | solution.py:360
  14.0 0.9 %all-to-all-done.pair_ref = bf16[8,64,256]{2,1,0:T(8,128)(2,1)S(1)} async-done(((bf16[8,64,256]{2,1,0:T(8,128)(2,1)}), bf16[8,64,256]{2,1,0:T(8,128)(2,1)S(1)}, u32[]{:S(2)}, u32[]{:S(2)}) %all-to-all-start) | async-done | bytes 262176 | tf_op jit(solution)/shard_map/all_to_all | solution.py:345
  14.8 0.0 copy-done.4
  14.8 1.6 %shard_map.112 = (bf16[8,32,256]{2,1,0:T(8,128)(2,1)}, bf16[288,256]{1,0:T(8,128)(2,1)S(1)}, bf16[288,256]{1,0:T(8,128)(2,1)S(1)}, bf16[288,256]{1,0:T(8,128)(2,1)S(1)}, bf16[288,256]{1,0:T(8,128)(2,1)S(1)}) custom-call(bf16[8,64,256]{2,1,0:T(8,128)(2,1)S(1)} %all-to-all-done.pair_ref, bf16[512,512]{1,0:T(8,128)(2,1)S(1)} %copy-done.3, ...), custom_call_target="tpu_custom_call" | custom-call | flops 2300000000 | tf_op jit(solution)/shard_map/pallas_call | solution.py:387
  16.4 3.5 %all-to-all-start.1 = ((bf16[8,32,256]{2,1,0:T(8,128)(2,1)}), bf16[8,32,256]{2,1,0:T(8,128)(2,1)S(1)}, u32[]{:S(2)}, u32[]{:S(2)}) async-start(bf16[8,32,256]{2,1,0:T(8,128)(2,1)} %get-tuple-element.21), calls=%async_computation.1 | async-start | bytes 262144 | tf_op jit(solution)/shard_map/all_to_all | solution.py:345
  20.0 0.0 collective-permute-done.refs_1_
  20.0 1.9 %collective-permute-done.1.refs_2_ = bf16[256,256]{1,0:T(8,128)(2,1)S(1)} collective-permute-done((bf16[256,256]{1,0:T(8,128)(2,1)S(1)}, bf16[256,256]{1,0:T(8,128)(2,1)S(1)}, u32[]{:S(2)}, u32[]{:S(2)}) %collective-permute-start.1) | collective-permute-done | bytes 131104 | tf_op jit(solution)/shard_map/ppermute | solution.py:360
  21.9 0.0 collective-permute-done.2.refs_3_
  21.9 3.6 %all-to-all-done.1 = bf16[8,32,256]{2,1,0:T(8,128)(2,1)S(1)} async-done(((bf16[8,32,256]{2,1,0:T(8,128)(2,1)}), bf16[8,32,256]{2,1,0:T(8,128)(2,1)S(1)}, u32[]{:S(2)}, u32[]{:S(2)}) %all-to-all-start.1) | async-done | bytes 131104 | tf_op jit(solution)/shard_map/all_to_all | solution.py:345
  25.4 0.8 %shard_map.114 = (f32[256,256]{1,0:T(8,128)}, bf16[256,256]{1,0:T(8,128)(2,1)}, bf16[256,256]{1,0:T(8,128)(2,1)S(1)}) custom-call(bf16[256,256]{1,0:T(8,128)(2,1)S(1)} %copy-done.2, bf16[256,256]{1,0:T(8,128)(2,1)S(1)} %bitcast.3, bf16[256,256]{1,0:T(8,128)(2,1)S(1)} %get-tuple-element.22.refs_0_, bf16[256,256]{1,0:T(8,128)(2,1)S(1)} %collective-permute-done.refs_1_, ...), custom_call_target="tpu_custom_call" | custom-call | flops 1150000000 | tf_op jit(solution)/shard_map/pallas_call | solution.py:399
  26.3 3.4 %all-to-all-start.2 = ((bf16[8,32,256]{2,1,0:T(8,128)(2,1)}), bf16[8,32,256]{2,1,0:T(8,128)(2,1)S(1)}, u32[]{:S(2)}, u32[]{:S(2)}) async-start(bf16[8,32,256]{2,1,0:T(8,128)(2,1)} %bitcast.2), calls=%async_computation.2 | async-start | bytes 262144 | tf_op jit(solution)/shard_map/all_to_all | solution.py:345
  29.7 3.6 %collective-permute-start.5 = (bf16[256,256]{1,0:T(8,128)(2,1)S(1)}, bf16[256,256]{1,0:T(8,128)(2,1)S(1)}, u32[]{:S(2)}, u32[]{:S(2)}) collective-permute-start(bf16[256,256]{1,0:T(8,128)(2,1)S(1)} %get-tuple-element.26.refs_0_), channel_id=1, source_target_pairs={{0,3},{1,0},{2,1},{3,2},{4,7},{5,4},{6,5},{7,6},{8,11},{9,8},{10,9... | collective-permute-start | bytes 393224 | tf_op jit(solution)/shard_map/ppermute | solution.py:360
  33.3 0.0 collective-permute-start.4
  33.3 1.0 %collective-permute-start.3 = (bf16[256,256]{1,0:T(8,128)(2,1)S(1)}, bf16[256,256]{1,0:T(8,128)(2,1)S(1)}, u32[]{:S(2)}, u32[]{:S(2)}) collective-permute-start(bf16[256,256]{1,0:T(8,128)(2,1)S(1)} %get-tuple-element.26.refs_0_), channel_id=1, source_target_pairs={{0,1},{1,2},{2,3},{3,0},{4,5},{5,6},{6,7},{7,4},{8,9},{9,10},{10,1... | collective-permute-start | bytes 393224 | tf_op jit(solution)/shard_map/ppermute | solution.py:360
  34.3 0.8 %all-to-all-done.2.grad_ref = bf16[8,32,256]{2,1,0:T(8,128)(2,1)S(1)} async-done(((bf16[8,32,256]{2,1,0:T(8,128)(2,1)}), bf16[8,32,256]{2,1,0:T(8,128)(2,1)S(1)}, u32[]{:S(2)}, u32[]{:S(2)}) %all-to-all-start.2) | async-done | bytes 131104 | tf_op jit(solution)/shard_map/all_to_all | solution.py:345
  35.1 1.8 %shard_map.116 = bf16[8,64,256]{2,1,0:T(8,128)(2,1)} custom-call(bf16[8,32,256]{2,1,0:T(8,128)(2,1)S(1)} %all-to-all-done.2.grad_ref, bf16[288,256]{1,0:T(8,128)(2,1)S(1)} %get-tuple-element.28.signal_real, bf16[288,256]{1,0:T(8,128)(2,1)S(1)} %get-tuple-element.29.signal_imag, bf16[288,256]{1,0:T(8,128)(2,1)S(1)} %get-tuple-element.30.filter_real, ...), custom_call_target="tpu_custom_call" | custom-call | flops 2300000000 | tf_op jit(solution)/shard_map/pallas_call | solution.py:417
  36.9 3.4 %all-to-all-start.3 = ((bf16[8,64,256]{2,1,0:T(8,128)(2,1)}), bf16[8,64,256]{2,1,0:T(8,128)(2,1)S(1)}, u32[]{:S(2)}, u32[]{:S(2)}) async-start(bf16[8,64,256]{2,1,0:T(8,128)(2,1)} %shard_map.116), calls=%async_computation.3 | async-start | bytes 524288 | tf_op jit(solution)/shard_map/all_to_all | solution.py:345
  40.3 0.0 copy-start.5
  40.3 0.0 collective-permute-done.5.refs_3_
  40.3 4.9 %collective-permute-done.4.refs_2_ = bf16[256,256]{1,0:T(8,128)(2,1)S(1)} collective-permute-done((bf16[256,256]{1,0:T(8,128)(2,1)S(1)}, bf16[256,256]{1,0:T(8,128)(2,1)S(1)}, u32[]{:S(2)}, u32[]{:S(2)}) %collective-permute-start.4) | collective-permute-done | bytes 131104 | tf_op jit(solution)/shard_map/ppermute | solution.py:360
  45.3 0.0 collective-permute-done.3.refs_1_
  45.3 1.2 %shard_map.115 = bf16[256,512]{1,0:T(8,128)(2,1)} custom-call(bf16[1024,512]{1,0:T(8,128)(2,1)S(1)} %copy-done, bf16[256,256]{1,0:T(8,128)(2,1)S(1)} %get-tuple-element.26.refs_0_, bf16[256,256]{1,0:T(8,128)(2,1)S(1)} %collective-permute-done.3.refs_1_, bf16[256,256]{1,0:T(8,128)(2,1)S(1)} %collective-permute-done.4.refs_2_, ...), custom_call_target="tpu_custom_call" | custom-call | flops 13799999488 | tf_op jit(solution)/shard_map/pallas_call | solution.py:410
  46.4 0.7 %all-to-all-done.3.back_ref = bf16[8,64,256]{2,1,0:T(8,128)(2,1)S(1)} async-done(((bf16[8,64,256]{2,1,0:T(8,128)(2,1)}), bf16[8,64,256]{2,1,0:T(8,128)(2,1)S(1)}, u32[]{:S(2)}, u32[]{:S(2)}) %all-to-all-start.3) | async-done | bytes 262176 | tf_op jit(solution)/shard_map/all_to_all | solution.py:345
  47.2 0.8 %shard_map.117 = (f32[256,256]{1,0:T(8,128)}, f32[256,256]{1,0:T(8,128)}) custom-call(bf16[8,64,256]{2,1,0:T(8,128)(2,1)S(1)} %all-to-all-done.3.back_ref, f32[256,256]{1,0:T(8,128)S(1)} %copy-done.5), custom_call_target="tpu_custom_call" | custom-call | flops 1150000000 | tf_op jit(solution)/shard_map/pallas_call | solution.py:429
  (7 shorter events, 0.0 us)
Async XLA Ops:
  0.6 7.2 %copy-start = (bf16[1024,512]{1,0:T(8,128)(2,1)S(1)}, bf16[1024,512]{1,0:T(8,128)(2,1)}, u32[]{:S(2)}) copy-start(bf16[1024,512]{1,0:T(8,128)(2,1)} %weight_ref.3) | copy-start | bytes 3145732
  2.6 5.3 %copy-start.1 = (bf16[256,512]{1,0:T(8,128)(2,1)S(1)}, bf16[256,512]{1,0:T(8,128)(2,1)}, u32[]{:S(2)}) copy-start(bf16[256,512]{1,0:T(8,128)(2,1)} %grad_ref.1) | copy-start | bytes 786436
  2.6 12.3 %all-to-all-start = ((bf16[8,64,256]{2,1,0:T(8,128)(2,1)}), bf16[8,64,256]{2,1,0:T(8,128)(2,1)S(1)}, u32[]{:S(2)}, u32[]{:S(2)}) async-start(bf16[8,64,256]{2,1,0:T(8,128)(2,1)} %get-tuple-element.20), calls=%async_computation | async-start | bytes 524288 | tf_op jit(solution)/shard_map/all_to_all | solution.py:345
  7.9 6.9 %copy-start.3 = (bf16[512,512]{1,0:T(8,128)(2,1)S(1)}, bf16[512,512]{1,0:T(8,128)(2,1)}, u32[]{:S(2)}) copy-start(bf16[512,512]{1,0:T(8,128)(2,1)} %constant.4.clone.table_ref) | copy-start | bytes 1572868
  7.9 6.9 %copy-start.4 = (f32[9,2,256]{2,1,0:T(2,128)S(1)}, f32[9,2,256]{2,1,0:T(2,128)}, u32[]{:S(2)}) copy-start(f32[9,2,256]{2,1,0:T(2,128)} %constant.5.clone.twiddle_ref) | copy-start | bytes 55300
  8.4 11.6 %collective-permute-start = (bf16[256,256]{1,0:T(8,128)(2,1)S(1)}, bf16[256,256]{1,0:T(8,128)(2,1)S(1)}, u32[]{:S(2)}, u32[]{:S(2)}) collective-permute-start(bf16[256,256]{1,0:T(8,128)(2,1)S(1)} %get-tuple-element.23), channel_id=1, source_target_pairs={{0,1},{1,2},{2,3},{3,0},{4,5},{5,6},{6,7},{7,4},{8,9},{9,10},{10,1... | collective-permute-start | bytes 393224 | tf_op jit(solution)/shard_map/ppermute | solution.py:360
  10.0 11.9 %collective-permute-start.1 = (bf16[256,256]{1,0:T(8,128)(2,1)S(1)}, bf16[256,256]{1,0:T(8,128)(2,1)S(1)}, u32[]{:S(2)}, u32[]{:S(2)}) collective-permute-start(bf16[256,256]{1,0:T(8,128)(2,1)S(1)} %get-tuple-element.24), channel_id=1, source_target_pairs={{0,2},{1,3},{2,0},{3,1},{4,6},{5,7},{6,4},{7,5},{8,10},{9,11},{10,... | collective-permute-start | bytes 393224 | tf_op jit(solution)/shard_map/ppermute | solution.py:360
  12.6 9.3 %collective-permute-start.2 = (bf16[256,256]{1,0:T(8,128)(2,1)S(1)}, bf16[256,256]{1,0:T(8,128)(2,1)S(1)}, u32[]{:S(2)}, u32[]{:S(2)}) collective-permute-start(bf16[256,256]{1,0:T(8,128)(2,1)S(1)} %get-tuple-element.25), channel_id=1, source_target_pairs={{0,3},{1,0},{2,1},{3,2},{4,7},{5,4},{6,5},{7,6},{8,11},{9,8},{10,9... | collective-permute-start | bytes 393224 | tf_op jit(solution)/shard_map/ppermute | solution.py:360
  16.4 9.0 %copy-start.2 = (bf16[256,256]{1,0:T(8,128)(2,1)S(1)}, bf16[256,256]{1,0:T(8,128)(2,1)}, u32[]{:S(2)}) copy-start(bf16[256,256]{1,0:T(8,128)(2,1)} %gating_ref.1) | copy-start | bytes 393220
  16.4 9.0 %all-to-all-start.1 = ((bf16[8,32,256]{2,1,0:T(8,128)(2,1)}), bf16[8,32,256]{2,1,0:T(8,128)(2,1)S(1)}, u32[]{:S(2)}, u32[]{:S(2)}) async-start(bf16[8,32,256]{2,1,0:T(8,128)(2,1)} %get-tuple-element.21), calls=%async_computation.1 | async-start | bytes 262144 | tf_op jit(solution)/shard_map/all_to_all | solution.py:345
  26.3 8.8 %all-to-all-start.2 = ((bf16[8,32,256]{2,1,0:T(8,128)(2,1)}), bf16[8,32,256]{2,1,0:T(8,128)(2,1)S(1)}, u32[]{:S(2)}, u32[]{:S(2)}) async-start(bf16[8,32,256]{2,1,0:T(8,128)(2,1)} %bitcast.2), calls=%async_computation.2 | async-start | bytes 262144 | tf_op jit(solution)/shard_map/all_to_all | solution.py:345
  29.7 10.7 %collective-permute-start.5 = (bf16[256,256]{1,0:T(8,128)(2,1)S(1)}, bf16[256,256]{1,0:T(8,128)(2,1)S(1)}, u32[]{:S(2)}, u32[]{:S(2)}) collective-permute-start(bf16[256,256]{1,0:T(8,128)(2,1)S(1)} %get-tuple-element.26.refs_0_), channel_id=1, source_target_pairs={{0,3},{1,0},{2,1},{3,2},{4,7},{5,4},{6,5},{7,6},{8,11},{9,8},{10,9... | collective-permute-start | bytes 393224 | tf_op jit(solution)/shard_map/ppermute | solution.py:360
  33.3 12.0 %collective-permute-start.4 = (bf16[256,256]{1,0:T(8,128)(2,1)S(1)}, bf16[256,256]{1,0:T(8,128)(2,1)S(1)}, u32[]{:S(2)}, u32[]{:S(2)}) collective-permute-start(bf16[256,256]{1,0:T(8,128)(2,1)S(1)} %get-tuple-element.26.refs_0_), channel_id=1, source_target_pairs={{0,2},{1,3},{2,0},{3,1},{4,6},{5,7},{6,4},{7,5},{8,10},{9,11},{10,... | collective-permute-start | bytes 393224 | tf_op jit(solution)/shard_map/ppermute | solution.py:360
  33.3 12.0 %collective-permute-start.3 = (bf16[256,256]{1,0:T(8,128)(2,1)S(1)}, bf16[256,256]{1,0:T(8,128)(2,1)S(1)}, u32[]{:S(2)}, u32[]{:S(2)}) collective-permute-start(bf16[256,256]{1,0:T(8,128)(2,1)S(1)} %get-tuple-element.26.refs_0_), channel_id=1, source_target_pairs={{0,1},{1,2},{2,3},{3,0},{4,5},{5,6},{6,7},{7,4},{8,9},{9,10},{10,1... | collective-permute-start | bytes 393224 | tf_op jit(solution)/shard_map/ppermute | solution.py:360
  36.9 10.3 %all-to-all-start.3 = ((bf16[8,64,256]{2,1,0:T(8,128)(2,1)}), bf16[8,64,256]{2,1,0:T(8,128)(2,1)S(1)}, u32[]{:S(2)}, u32[]{:S(2)}) async-start(bf16[8,64,256]{2,1,0:T(8,128)(2,1)} %shard_map.116), calls=%async_computation.3 | async-start | bytes 524288 | tf_op jit(solution)/shard_map/all_to_all | solution.py:345
  40.3 6.9 %copy-start.5 = (f32[256,256]{1,0:T(8,128)S(1)}, f32[256,256]{1,0:T(8,128)}, u32[]{:S(2)}) copy-start(f32[256,256]{1,0:T(8,128)} %get-tuple-element.32.window_ref) | copy-start | bytes 786436

commit v2 on v1

--- a/solution.py
+++ b/solution.py
@@ -18,18 +18,24 @@
 LANES = 128
 
 
-def call(kernel, out_shape, in_specs, scratch=(), micros=1, out_specs=None, moved=0, room=16):
-    return pl.pallas_call(
-        kernel,
+def call(kernel, out_shape, in_specs, scratch=(), micros=1, room=16, after=()):
+    count = len(in_specs)
+
+    def body(*refs):
+        kernel(*refs[:count], *refs[count + len(after) :])
+
+    run = pl.pallas_call(
+        body,
         out_shape=out_shape,
-        in_specs=in_specs,
-        out_specs=jax.tree.map(lambda _: VMEM, out_shape) if out_specs is None else out_specs,
+        in_specs=list(in_specs) + [ANY] * len(after),
+        out_specs=jax.tree.map(lambda _: VMEM, out_shape),
         scratch_shapes=list(scratch),
         cost_estimate=pl.CostEstimate(
-            flops=int(micros * PEAK_FLOPS_A_MICRO), bytes_accessed=moved, transcendentals=0
+            flops=int(micros * PEAK_FLOPS_A_MICRO), bytes_accessed=0, transcendentals=0
         ),
         compiler_params=pltpu.CompilerParams(vmem_limit_bytes=room * 1024 * 1024),
     )
+    return lambda *operands: run(*operands, *after)
 
 
 def within_table(lanes):
@@ -288,16 +294,36 @@
         ).astype(out_refs[step].dtype)
 
 
-def gate_kernel(gating_ref, mixed_ref, *refs):
-    gating_grad_ref, grad_mixed_ref, gated_ref = refs[-3:]
+def total_kernel(gating_ref, *refs):
+    total_ref, grad_mixed_ref = refs[-2:]
     total = refs[0][...].astype(f32)
-    for share in refs[1:-3]:
+    for share in refs[1:-2]:
         total = total + share[...].astype(f32)
-    gates = gating_ref[...].astype(f32)
-    mixed = mixed_ref[...].astype(f32)
-    grad_mixed_ref[...] = (total * gates).astype(bf16)
-    gated_ref[...] = (gates * mixed).astype(bf16)
-    gating_grad_ref[...] = total * mixed
+    total_ref[...] = total
+    grad_mixed_ref[...] = (total * gating_ref[...].astype(f32)).astype(bf16)
+
+
+def pack_kernel(both_ref, *out_refs):
+    me = lax.axis_index("seq")
+    core = lax.rem(me, 2)
+    chip = lax.div(me, 2)
+    for step, out_ref in enumerate(out_refs):
+        block = 2 * lax.bitwise_xor(chip, step) + core
+        for source in range(2):
+            out_ref[source] = both_ref[source, block]
+
+
+def gate_kernel(gating_ref, total_ref, *refs):
+    gating_grad_ref, gated_ref = refs[-2:]
+    pieces = refs[:-2]
+    chip = lax.div(lax.axis_index("seq"), 2)
+    count = gating_ref.shape[0] // len(pieces)
+    for step, piece in enumerate(pieces):
+        place = lax.bitwise_xor(chip, step) if len(pieces) > 1 else 0
+        rows = pl.ds(pl.multiple_of(place * count, count), count)
+        mixed = piece[...].reshape(count, -1).astype(f32)
+        gated_ref[rows] = (gating_ref[rows].astype(f32) * mixed).astype(bf16)
+        gating_grad_ref[rows] = total_ref[rows] * mixed
 
 
 def project_kernel(weight_ref, *refs):
@@ -380,7 +406,7 @@
         spread_kernel,
         tuple(shape((channels, length), bf16) for k in range(parts)),
         [VMEM] * 2,
-        micros=1.0,
+        after=(pairs,),
     )(out_weight, out_grad)
     shares = [shift(partial[step], step) for step in range(1, parts)]
 
@@ -392,20 +418,37 @@
             pltpu.VMEM((2 * height, 2 * length), bf16),
             pltpu.VMEM((height, 2 * length), f32),
         ),
-        micros=2.0,
+        micros=2,
     )(padded(arrived, owned, held), table, twiddle)
-    mixed = exchange(trimmed(mixed_owned, owned, held)).reshape(channels, length)
-
-    gating_grad, grad_mixed, gated = call(
+    chips = shards // 2
+    if chips in (2, 4) and owned == held:
+        def hop(array, distance):
+            return lax.ppermute(array, "seq", [(i, i ^ distance) for i in range(shards)])
+
+        pairs = [[2 * chip, 2 * chip + 1] for chip in range(chips)]
+        both = lax.all_gather(mixed_owned, "seq", axis_index_groups=pairs)
+        pieces = call(
+            pack_kernel,
+            (shape((2, owned, length), bf16),) * chips,
+            [VMEM],
+        )(both)
+        pieces = [pieces[0]] + [hop(pieces[step], 2 * step) for step in range(1, chips)]
+    else:
+        pieces = [exchange(trimmed(mixed_owned, owned, held)).reshape(channels, length)]
+
+    total, grad_mixed = call(
+        total_kernel,
+        (shape((channels, length), f32), shape((channels, length), bf16)),
+        [VMEM] * (2 + len(shares)),
+        after=(pieces[0],),
+    )(gating, partial[0], *shares)
+    grad_whole = exchange(grad_mixed.reshape(shards, owned, length))
+
+    gating_grad, gated = call(
         gate_kernel,
-        (
-            shape((channels, length), f32),
-            shape((channels, length), bf16),
-            shape((channels, length), bf16),
-        ),
-        [VMEM] * (3 + len(shares)),
-    )(gating, mixed, partial[0], *shares)
-    grad_whole = exchange(grad_mixed.reshape(shards, owned, length))
+        (shape((channels, length), f32), shape((channels, length), bf16)),
+        [VMEM] * (2 + len(pieces)),
+    )(gating, total, *pieces)
     gathered = [gated] + [shift(gated, step) for step in range(1, parts)]
     mixed_out = call(
         project_kernel,
@@ -423,6 +466,7 @@
             pltpu.VMEM((2 * height, 2 * length), f32),
         ),
         micros=2.0,
+        after=(gated,),
     )(padded(grad_whole, owned, held), *spectra, table, twiddle)
     returned = exchange(trimmed(grads_owned, owned, held))
     if owned == held:

time: 48.6 us -> 47.2 us (0.971)
  waiting for transfers between devices: 12.8 us -> 7.15 us
  starting transfers between devices: 25.8 us -> 28.1 us
  blocking collectives: 0 us -> 1.99 us
    all_to_all x4 -> x3, waiting for transfers between devices: 5.98 us -> 1.03 us  [exchange(): return lax.all_to_all(array, 'seq', split_axis=0, concat_axis=0, tiled=True)]
    ppermute x0 -> x3, starting transfers between devices: none -> 3.55 us  [hop(): lax.ppermute(array, 'seq', [(i, i ^ distance) for i in range(shards)])]
    all_to_all x4 -> x3, starting transfers between devices: 15.6 us -> 13.4 us  [exchange(): return lax.all_to_all(array, 'seq', split_axis=0, concat_axis=0, tiled=True)]
    all_gather x0 -> x1, blocking collectives: none -> 1.99 us  [per_device(): both = lax.all_gather(mixed_owned, 'seq', axis_index_groups=pairs)]
    ppermute x6, starting transfers between devices: 10.2 us -> 11.2 us  [shift(): lax.ppermute(array, 'chan', [(i, (i + step) % parts) for i in range(parts)])]
    ppermute x6, waiting for transfers between devices: 6.86 us -> 6.11 us  [shift(): lax.ppermute(array, 'chan', [(i, (i + step) % parts) for i in range(parts)])]
    pallas_call x7 -> x9, Pallas kernels: 8.59 us -> 8.61 us  [call(): return lambda *operands: run(*operands, *after)]
  transfers between devices with their start and end apart: 10 -> 12, of which waited for: 6 -> 4; matrix products, arithmetic and copies ran while one was open for 0% -> 0% of each run, Pallas kernels for 10% -> 13%
where the time goes in v2:
time: 47.2 us; the launch traced here: 46.7 us
  starting transfers between devices  28.1 us (60%)
  Pallas kernels  8.61 us (18%)
  waiting for transfers between devices  7.15 us (15%)
  blocking collectives  1.99 us (4%)
  between operations  0.78 us (2%)
    all_to_all x3, starting transfers between devices, exchange(): return lax.all_to_all(array, 'seq', split_axis=0, concat_axis=0, tiled=True)  13.4 us
    ppermute x6, starting transfers between devices, shift(): lax.ppermute(array, 'chan', [(i, (i + step) % parts) for i in range(parts)])  11.2 us
    pallas_call x9, Pallas kernels, call(): return lambda *operands: run(*operands, *after)  8.61 us
    ppermute x6, waiting for transfers between devices, shift(): lax.ppermute(array, 'chan', [(i, (i + step) % parts) for i in range(parts)])  6.11 us
    ppermute x3, starting transfers between devices, hop(): lax.ppermute(array, 'seq', [(i, i ^ distance) for i in range(shards)])  3.55 us
    all_gather x1, blocking collectives, per_device(): both = lax.all_gather(mixed_owned, 'seq', axis_index_groups=pairs)  1.99 us
    all_to_all x3, waiting for transfers between devices, exchange(): return lax.all_to_all(array, 'seq', split_axis=0, concat_axis=0, tiled=True)  1.03 us
  transfers between devices with their start and end apart: 12, of which 4 were waited for; matrix products, arithmetic and copies ran while one was open for 0% of the time, Pallas kernels for 13%

profile of v2, /device:TPU:0, one launch (start us, length us, event | category | flops | bytes accessed | tf_op | source)
XLA Modules:
  0.0 46.7 jit_solution(4020169668113452268)
XLA Ops:
  0.6 1.9 %shard_map.111 = (bf16[8,64,256]{2,1,0:T(8,128)(2,1)}, f32[256,256]{1,0:T(8,128)}) custom-call(f32[1,256]{1,0:T(1,128)} %bitcast.4, f32[256,256]{1,0:T(8,128)} %refs_1_.3, bf16[256,256]{1,0:T(8,128)(2,1)} %refs_2_.2), custom_call_target="tpu_custom_call" | custom-call | flops 1150000000 | tf_op jit(solution)/shard_map/pallas_call | solution.py:38
  2.6 0.0 copy-start
  2.6 0.0 copy-start.2
  2.6 5.3 %all-to-all-start = ((bf16[8,64,256]{2,1,0:T(8,128)(2,1)}), bf16[8,64,256]{2,1,0:T(8,128)(2,1)S(1)}, u32[]{:S(2)}, u32[]{:S(2)}) async-start(bf16[8,64,256]{2,1,0:T(8,128)(2,1)} %get-tuple-element.25.refs_2_), calls=%async_computation | async-start | bytes 524288 | tf_op jit(solution)/shard_map/all_to_all | solution.py:371
  7.9 0.0 copy-start.4
  7.9 0.0 copy-start.5
  7.9 0.5 %shard_map.112 = (bf16[256,256]{1,0:T(8,128)(2,1)S(1)}, bf16[256,256]{1,0:T(8,128)(2,1)S(1)}, bf16[256,256]{1,0:T(8,128)(2,1)S(1)}, bf16[256,256]{1,0:T(8,128)(2,1)S(1)}) custom-call(bf16[1024,512]{1,0:T(8,128)(2,1)S(1)} %copy-done.1, bf16[256,512]{1,0:T(8,128)(2,1)S(1)} %copy-done.2, bf16[8,64,256]{2,1,0:T(8,128)(2,1)S(1)} %copy-done), custom_call_target="tpu_custom_call" | custom-call | flops 1150000000 | tf_op jit(solution)/shard_map/pallas_call | solution.py:38
  8.4 1.6 %collective-permute-start = (bf16[256,256]{1,0:T(8,128)(2,1)S(1)}, bf16[256,256]{1,0:T(8,128)(2,1)S(1)}, u32[]{:S(2)}, u32[]{:S(2)}) collective-permute-start(bf16[256,256]{1,0:T(8,128)(2,1)S(1)} %get-tuple-element.27), channel_id=1, source_target_pairs={{0,1},{1,2},{2,3},{3,0},{4,5},{5,6},{6,7},{7,4},{8,9},{9,10},{10,1... | collective-permute-start | bytes 393224 | tf_op jit(solution)/shard_map/ppermute | solution.py:386
  10.0 2.6 %collective-permute-start.1 = (bf16[256,256]{1,0:T(8,128)(2,1)S(1)}, bf16[256,256]{1,0:T(8,128)(2,1)S(1)}, u32[]{:S(2)}, u32[]{:S(2)}) collective-permute-start(bf16[256,256]{1,0:T(8,128)(2,1)S(1)} %get-tuple-element.28), channel_id=1, source_target_pairs={{0,2},{1,3},{2,0},{3,1},{4,6},{5,7},{6,4},{7,5},{8,10},{9,11},{10,... | collective-permute-start | bytes 393224 | tf_op jit(solution)/shard_map/ppermute | solution.py:386
  12.6 1.4 %collective-permute-start.2 = (bf16[256,256]{1,0:T(8,128)(2,1)S(1)}, bf16[256,256]{1,0:T(8,128)(2,1)S(1)}, u32[]{:S(2)}, u32[]{:S(2)}) collective-permute-start(bf16[256,256]{1,0:T(8,128)(2,1)S(1)} %get-tuple-element.29), channel_id=1, source_target_pairs={{0,3},{1,0},{2,1},{3,2},{4,7},{5,4},{6,5},{7,6},{8,11},{9,8},{10,9... | collective-permute-start | bytes 393224 | tf_op jit(solution)/shard_map/ppermute | solution.py:386
  14.0 0.8 %all-to-all-done.refs_0_ = bf16[8,64,256]{2,1,0:T(8,128)(2,1)S(1)} async-done(((bf16[8,64,256]{2,1,0:T(8,128)(2,1)}), bf16[8,64,256]{2,1,0:T(8,128)(2,1)S(1)}, u32[]{:S(2)}, u32[]{:S(2)}) %all-to-all-start) | async-done | bytes 262176 | tf_op jit(solution)/shard_map/all_to_all | solution.py:371
  14.8 1.0 %shard_map.113 = (bf16[8,32,256]{2,1,0:T(8,128)(2,1)S(1)}, bf16[288,256]{1,0:T(8,128)(2,1)S(1)}, bf16[288,256]{1,0:T(8,128)(2,1)S(1)}, bf16[288,256]{1,0:T(8,128)(2,1)S(1)}, bf16[288,256]{1,0:T(8,128)(2,1)S(1)}) custom-call(bf16[8,64,256]{2,1,0:T(8,128)(2,1)S(1)} %all-to-all-done.refs_0_, bf16[512,512]{1,0:T(8,128)(2,1)S(1)} %copy-done.4, ...), custom_call_target="tpu_custom_call" | custom-call | flops 2300000000 | tf_op jit(solution)/shard_map/pallas_call | solution.py:38
  15.8 2.0 %all-gather = bf16[16,32,256]{2,1,0:T(8,128)(2,1)S(1)} all-gather(bf16[8,32,256]{2,1,0:T(8,128)(2,1)S(1)} %get-tuple-element.30), channel_id=2, replica_groups={{0,4},{8,12},{16,20},{24,28},{1,5},{9,13},{17,21},{25,29},{2,6},{10,14}..., dimensions={0}, use_global_device_ids=true | all-gather | bytes 393216 | tf_op jit(solution)/shard_map/all_gather | solution.py:429
  17.8 0.0 copy-start.7
  17.8 1.2 %collective-permute-start.3 = (bf16[2,32,256]{2,1,0:T(8,128)(2,1)S(1)}, bf16[2,32,256]{2,1,0:T(8,128)(2,1)S(1)}, u32[]{:S(2)}, u32[]{:S(2)}) collective-permute-start(bf16[2,32,256]{2,1,0:T(8,128)(2,1)S(1)} %get-tuple-element.33), channel_id=1, source_target_pairs={{0,8},{4,12},{8,0},{12,4},{16,24},{20,28},{24,16},{28,20},{1,9},{5... | collective-permute-start | bytes 98312 | tf_op jit(solution)/shard_map/ppermute | solution.py:426
  19.1 1.5 %collective-permute-start.4 = (bf16[2,32,256]{2,1,0:T(8,128)(2,1)S(1)}, bf16[2,32,256]{2,1,0:T(8,128)(2,1)S(1)}, u32[]{:S(2)}, u32[]{:S(2)}) collective-permute-start(bf16[2,32,256]{2,1,0:T(8,128)(2,1)S(1)} %get-tuple-element.34), channel_id=1, source_target_pairs={{0,16},{4,20},{8,24},{12,28},{16,0},{20,4},{24,8},{28,12},{1,17},{... | collective-permute-start | bytes 98312 | tf_op jit(solution)/shard_map/ppermute | solution.py:426
  20.5 0.8 %collective-permute-start.5 = (bf16[2,32,256]{2,1,0:T(8,128)(2,1)S(1)}, bf16[2,32,256]{2,1,0:T(8,128)(2,1)S(1)}, u32[]{:S(2)}, u32[]{:S(2)}) collective-permute-start(bf16[2,32,256]{2,1,0:T(8,128)(2,1)S(1)} %get-tuple-element.35), channel_id=1, source_target_pairs={{0,24},{4,28},{8,16},{12,20},{16,8},{20,12},{24,0},{28,4},{1,25},{... | collective-permute-start | bytes 98312 | tf_op jit(solution)/shard_map/ppermute | solution.py:426
  21.4 0.5 %collective-permute-done.1.refs_3_ = bf16[256,256]{1,0:T(8,128)(2,1)S(1)} collective-permute-done((bf16[256,256]{1,0:T(8,128)(2,1)S(1)}, bf16[256,256]{1,0:T(8,128)(2,1)S(1)}, u32[]{:S(2)}, u32[]{:S(2)}) %collective-permute-start.1) | collective-permute-done | bytes 131104 | tf_op jit(solution)/shard_map/ppermute | solution.py:386
  21.9 0.7 %shard_map.115 = (f32[256,256]{1,0:T(8,128)S(1)}, bf16[256,256]{1,0:T(8,128)(2,1)}) custom-call(bf16[256,256]{1,0:T(8,128)(2,1)S(1)} %copy-done.3, bf16[256,256]{1,0:T(8,128)(2,1)S(1)} %get-tuple-element.26.refs_1_, bf16[256,256]{1,0:T(8,128)(2,1)S(1)} %collective-permute-done.refs_2_, bf16[256,256]{1,0:T(8,128)(2,1)S(1)} %collective-permute-done.1.refs_3_, ...), custom_call_target="tpu_custom_call" | custom-call | flops 1150000000 | tf_op jit(solution)/shard_map/pallas_call | solution.py:38
  22.7 4.0 %all-to-all-start.1 = ((bf16[8,32,256]{2,1,0:T(8,128)(2,1)}), bf16[8,32,256]{2,1,0:T(8,128)(2,1)S(1)}, u32[]{:S(2)}, u32[]{:S(2)}) async-start(bf16[8,32,256]{2,1,0:T(8,128)(2,1)} %bitcast.2), calls=%async_computation.1 | async-start | bytes 262144 | tf_op jit(solution)/shard_map/all_to_all | solution.py:371
  26.7 0.0 collective-permute-done.3.refs_3_
  26.7 0.0 collective-permute-done.5.refs_5_
  26.7 0.8 %shard_map.116 = (f32[256,256]{1,0:T(8,128)}, bf16[256,256]{1,0:T(8,128)(2,1)S(1)}) custom-call(bf16[256,256]{1,0:T(8,128)(2,1)S(1)} %copy-done.3, f32[256,256]{1,0:T(8,128)S(1)} %get-tuple-element.32.refs_1_, bf16[2,32,256]{2,1,0:T(8,128)(2,1)S(1)} %copy-done.8, bf16[2,32,256]{2,1,0:T(8,128)(2,1)S(1)} %collective-permute-done.3.refs_3_, ...), custom_call_target="tpu_custom_call" | custom-call | flops 1150000000 | tf_op jit(solution)/shard_map/pallas_call | solution.py:38
  27.5 4.3 %collective-permute-start.8 = (bf16[256,256]{1,0:T(8,128)(2,1)S(1)}, bf16[256,256]{1,0:T(8,128)(2,1)S(1)}, u32[]{:S(2)}, u32[]{:S(2)}) collective-permute-start(bf16[256,256]{1,0:T(8,128)(2,1)S(1)} %get-tuple-element.36.refs_1_.refs_7_), channel_id=1, source_target_pairs={{0,3},{1,0},{2,1},{3,2},{4,7},{5,4},{6,5},{7,6},{8,11},{9,8},{10,9... | collective-permute-start | bytes 393224 | tf_op jit(solution)/shard_map/ppermute | solution.py:386
  31.8 0.4 collective-permute-start.7
  32.2 0.9 %collective-permute-start.6 = (bf16[256,256]{1,0:T(8,128)(2,1)S(1)}, bf16[256,256]{1,0:T(8,128)(2,1)S(1)}, u32[]{:S(2)}, u32[]{:S(2)}) collective-permute-start(bf16[256,256]{1,0:T(8,128)(2,1)S(1)} %get-tuple-element.36.refs_1_.refs_7_), channel_id=1, source_target_pairs={{0,1},{1,2},{2,3},{3,0},{4,5},{5,6},{6,7},{7,4},{8,9},{9,10},{10,1... | collective-permute-start | bytes 393224 | tf_op jit(solution)/shard_map/ppermute | solution.py:386
  33.1 1.8 %shard_map.118 = bf16[8,64,256]{2,1,0:T(8,128)(2,1)} custom-call(bf16[8,32,256]{2,1,0:T(8,128)(2,1)S(1)} %all-to-all-done.1.refs_0_, bf16[288,256]{1,0:T(8,128)(2,1)S(1)} %get-tuple-element.38.refs_1_, bf16[288,256]{1,0:T(8,128)(2,1)S(1)} %get-tuple-element.39.refs_2_, bf16[288,256]{1,0:T(8,128)(2,1)S(1)} %get-tuple-element.40.refs_3_, ...), custom_call_target="tpu_custom_call" | custom-call | flops 2300000000 | tf_op jit(solution)/shard_map/pallas_call | solution.py:38
  34.8 4.1 %all-to-all-start.2 = ((bf16[8,64,256]{2,1,0:T(8,128)(2,1)}), bf16[8,64,256]{2,1,0:T(8,128)(2,1)S(1)}, u32[]{:S(2)}, u32[]{:S(2)}) async-start(bf16[8,64,256]{2,1,0:T(8,128)(2,1)} %shard_map.118), calls=%async_computation.2 | async-start | bytes 524288 | tf_op jit(solution)/shard_map/all_to_all | solution.py:371
  39.0 5.6 %collective-permute-done.7.refs_3_ = bf16[256,256]{1,0:T(8,128)(2,1)S(1)} collective-permute-done((bf16[256,256]{1,0:T(8,128)(2,1)S(1)}, bf16[256,256]{1,0:T(8,128)(2,1)S(1)}, u32[]{:S(2)}, u32[]{:S(2)}) %collective-permute-start.7) | collective-permute-done | bytes 131104 | tf_op jit(solution)/shard_map/ppermute | solution.py:386
  44.5 1.2 %shard_map.117 = bf16[256,512]{1,0:T(8,128)(2,1)} custom-call(bf16[1024,512]{1,0:T(8,128)(2,1)S(1)} %copy-done.1, bf16[256,256]{1,0:T(8,128)(2,1)S(1)} %get-tuple-element.36.refs_1_.refs_7_, bf16[256,256]{1,0:T(8,128)(2,1)S(1)} %collective-permute-done.6.refs_2_, bf16[256,256]{1,0:T(8,128)(2,1)S(1)} %collective-permute-done.7.refs_3_, ...), custom_call_target="tpu_custom_call" | custom-call | flops 13799999488 | tf_op jit(solution)/shard_map/pallas_call | solution.py:38
  45.7 0.2 all-to-all-done.2.refs_0_
  45.9 0.8 %shard_map.119 = (f32[256,256]{1,0:T(8,128)}, f32[256,256]{1,0:T(8,128)}) custom-call(bf16[8,64,256]{2,1,0:T(8,128)(2,1)S(1)} %all-to-all-done.2.refs_0_, f32[256,256]{1,0:T(8,128)S(1)} %copy-done.6), custom_call_target="tpu_custom_call" | custom-call | flops 1150000000 | tf_op jit(solution)/shard_map/pallas_call | solution.py:38
  (20 shorter events, 0.1 us)
Async XLA Ops:
  0.6 7.3 %copy-start.1 = (bf16[1024,512]{1,0:T(8,128)(2,1)S(1)}, bf16[1024,512]{1,0:T(8,128)(2,1)}, u32[]{:S(2)}) copy-start(bf16[1024,512]{1,0:T(8,128)(2,1)} %refs_0_.7) | copy-start | bytes 3145732
  2.6 5.3 %copy-start = (bf16[8,64,256]{2,1,0:T(8,128)(2,1)S(1)}, bf16[8,64,256]{2,1,0:T(8,128)(2,1)}, u32[]{:S(2)}) copy-start(bf16[8,64,256]{2,1,0:T(8,128)(2,1)} %get-tuple-element.25.refs_2_) | copy-start | bytes 786436
  2.6 5.3 %copy-start.2 = (bf16[256,512]{1,0:T(8,128)(2,1)S(1)}, bf16[256,512]{1,0:T(8,128)(2,1)}, u32[]{:S(2)}) copy-start(bf16[256,512]{1,0:T(8,128)(2,1)} %refs_1_.4) | copy-start | bytes 786436
  2.6 12.3 %all-to-all-start = ((bf16[8,64,256]{2,1,0:T(8,128)(2,1)}), bf16[8,64,256]{2,1,0:T(8,128)(2,1)S(1)}, u32[]{:S(2)}, u32[]{:S(2)}) async-start(bf16[8,64,256]{2,1,0:T(8,128)(2,1)} %get-tuple-element.25.refs_2_), calls=%async_computation | async-start | bytes 524288 | tf_op jit(solution)/shard_map/all_to_all | solution.py:371
  7.9 6.9 %copy-start.4 = (bf16[512,512]{1,0:T(8,128)(2,1)S(1)}, bf16[512,512]{1,0:T(8,128)(2,1)}, u32[]{:S(2)}) copy-start(bf16[512,512]{1,0:T(8,128)(2,1)} %constant.4.clone.refs_1_.refs_5_) | copy-start | bytes 1572868
  7.9 6.9 %copy-start.5 = (f32[9,2,256]{2,1,0:T(2,128)S(1)}, f32[9,2,256]{2,1,0:T(2,128)}, u32[]{:S(2)}) copy-start(f32[9,2,256]{2,1,0:T(2,128)} %constant.5.clone.refs_2_.refs_6_) | copy-start | bytes 55300
  8.4 12.1 %collective-permute-start = (bf16[256,256]{1,0:T(8,128)(2,1)S(1)}, bf16[256,256]{1,0:T(8,128)(2,1)S(1)}, u32[]{:S(2)}, u32[]{:S(2)}) collective-permute-start(bf16[256,256]{1,0:T(8,128)(2,1)S(1)} %get-tuple-element.27), channel_id=1, source_target_pairs={{0,1},{1,2},{2,3},{3,0},{4,5},{5,6},{6,7},{7,4},{8,9},{9,10},{10,1... | collective-permute-start | bytes 393224 | tf_op jit(solution)/shard_map/ppermute | solution.py:386
  10.0 11.9 %collective-permute-start.1 = (bf16[256,256]{1,0:T(8,128)(2,1)S(1)}, bf16[256,256]{1,0:T(8,128)(2,1)S(1)}, u32[]{:S(2)}, u32[]{:S(2)}) collective-permute-start(bf16[256,256]{1,0:T(8,128)(2,1)S(1)} %get-tuple-element.28), channel_id=1, source_target_pairs={{0,2},{1,3},{2,0},{3,1},{4,6},{5,7},{6,4},{7,5},{8,10},{9,11},{10,... | collective-permute-start | bytes 393224 | tf_op jit(solution)/shard_map/ppermute | solution.py:386
  12.6 9.3 %collective-permute-start.2 = (bf16[256,256]{1,0:T(8,128)(2,1)S(1)}, bf16[256,256]{1,0:T(8,128)(2,1)S(1)}, u32[]{:S(2)}, u32[]{:S(2)}) collective-permute-start(bf16[256,256]{1,0:T(8,128)(2,1)S(1)} %get-tuple-element.29), channel_id=1, source_target_pairs={{0,3},{1,0},{2,1},{3,2},{4,7},{5,4},{6,5},{7,6},{8,11},{9,8},{10,9... | collective-permute-start | bytes 393224 | tf_op jit(solution)/shard_map/ppermute | solution.py:386
  17.8 4.1 %copy-start.3 = (bf16[256,256]{1,0:T(8,128)(2,1)S(1)}, bf16[256,256]{1,0:T(8,128)(2,1)}, u32[]{:S(2)}) copy-start(bf16[256,256]{1,0:T(8,128)(2,1)} %refs_0_.6) | copy-start | bytes 393220
  17.8 4.9 %copy-start.7 = (bf16[2,32,256]{2,1,0:T(8,128)(2,1)}, bf16[2,32,256]{2,1,0:T(8,128)(2,1)S(1)}, u32[]{:S(2)}) copy-start(bf16[2,32,256]{2,1,0:T(8,128)(2,1)S(1)} %get-tuple-element.31.refs_5_.refs_2_) | copy-start | bytes 98308
  17.8 8.9 %collective-permute-start.3 = (bf16[2,32,256]{2,1,0:T(8,128)(2,1)S(1)}, bf16[2,32,256]{2,1,0:T(8,128)(2,1)S(1)}, u32[]{:S(2)}, u32[]{:S(2)}) collective-permute-start(bf16[2,32,256]{2,1,0:T(8,128)(2,1)S(1)} %get-tuple-element.33), channel_id=1, source_target_pairs={{0,8},{4,12},{8,0},{12,4},{16,24},{20,28},{24,16},{28,20},{1,9},{5... | collective-permute-start | bytes 98312 | tf_op jit(solution)/shard_map/ppermute | solution.py:426
  19.1 7.6 %collective-permute-start.4 = (bf16[2,32,256]{2,1,0:T(8,128)(2,1)S(1)}, bf16[2,32,256]{2,1,0:T(8,128)(2,1)S(1)}, u32[]{:S(2)}, u32[]{:S(2)}) collective-permute-start(bf16[2,32,256]{2,1,0:T(8,128)(2,1)S(1)} %get-tuple-element.34), channel_id=1, source_target_pairs={{0,16},{4,20},{8,24},{12,28},{16,0},{20,4},{24,8},{28,12},{1,17},{... | collective-permute-start | bytes 98312 | tf_op jit(solution)/shard_map/ppermute | solution.py:426
  20.5 6.2 %collective-permute-start.5 = (bf16[2,32,256]{2,1,0:T(8,128)(2,1)S(1)}, bf16[2,32,256]{2,1,0:T(8,128)(2,1)S(1)}, u32[]{:S(2)}, u32[]{:S(2)}) collective-permute-start(bf16[2,32,256]{2,1,0:T(8,128)(2,1)S(1)} %get-tuple-element.35), channel_id=1, source_target_pairs={{0,24},{4,28},{8,16},{12,20},{16,8},{20,12},{24,0},{28,4},{1,25},{... | collective-permute-start | bytes 98312 | tf_op jit(solution)/shard_map/ppermute | solution.py:426
  22.7 4.0 %copy-start.8 = (bf16[2,32,256]{2,1,0:T(8,128)(2,1)S(1)}, bf16[2,32,256]{2,1,0:T(8,128)(2,1)}, u32[]{:S(2)}) copy-start(bf16[2,32,256]{2,1,0:T(8,128)(2,1)} %copy-done.7) | copy-start | bytes 98308
  22.7 10.4 %all-to-all-start.1 = ((bf16[8,32,256]{2,1,0:T(8,128)(2,1)}), bf16[8,32,256]{2,1,0:T(8,128)(2,1)S(1)}, u32[]{:S(2)}, u32[]{:S(2)}) async-start(bf16[8,32,256]{2,1,0:T(8,128)(2,1)} %bitcast.2), calls=%async_computation.1 | async-start | bytes 262144 | tf_op jit(solution)/shard_map/all_to_all | solution.py:371
  27.5 11.5 %collective-permute-start.8 = (bf16[256,256]{1,0:T(8,128)(2,1)S(1)}, bf16[256,256]{1,0:T(8,128)(2,1)S(1)}, u32[]{:S(2)}, u32[]{:S(2)}) collective-permute-start(bf16[256,256]{1,0:T(8,128)(2,1)S(1)} %get-tuple-element.36.refs_1_.refs_7_), channel_id=1, source_target_pairs={{0,3},{1,0},{2,1},{3,2},{4,7},{5,4},{6,5},{7,6},{8,11},{9,8},{10,9... | collective-permute-start | bytes 393224 | tf_op jit(solution)/shard_map/ppermute | solution.py:386
  31.8 12.7 %collective-permute-start.7 = (bf16[256,256]{1,0:T(8,128)(2,1)S(1)}, bf16[256,256]{1,0:T(8,128)(2,1)S(1)}, u32[]{:S(2)}, u32[]{:S(2)}) collective-permute-start(bf16[256,256]{1,0:T(8,128)(2,1)S(1)} %get-tuple-element.36.refs_1_.refs_7_), channel_id=1, source_target_pairs={{0,2},{1,3},{2,0},{3,1},{4,6},{5,7},{6,4},{7,5},{8,10},{9,11},{10,... | collective-permute-start | bytes 393224 | tf_op jit(solution)/shard_map/ppermute | solution.py:386
  32.2 12.3 %collective-permute-start.6 = (bf16[256,256]{1,0:T(8,128)(2,1)S(1)}, bf16[256,256]{1,0:T(8,128)(2,1)S(1)}, u32[]{:S(2)}, u32[]{:S(2)}) collective-permute-start(bf16[256,256]{1,0:T(8,128)(2,1)S(1)} %get-tuple-element.36.refs_1_.refs_7_), channel_id=1, source_target_pairs={{0,1},{1,2},{2,3},{3,0},{4,5},{5,6},{6,7},{7,4},{8,9},{9,10},{10,1... | collective-permute-start | bytes 393224 | tf_op jit(solution)/shard_map/ppermute | solution.py:386
  34.8 11.0 %all-to-all-start.2 = ((bf16[8,64,256]{2,1,0:T(8,128)(2,1)}), bf16[8,64,256]{2,1,0:T(8,128)(2,1)S(1)}, u32[]{:S(2)}, u32[]{:S(2)}) async-start(bf16[8,64,256]{2,1,0:T(8,128)(2,1)} %shard_map.118), calls=%async_computation.2 | async-start | bytes 524288 | tf_op jit(solution)/shard_map/all_to_all | solution.py:371
  38.9 6.9 %copy-start.6 = (f32[256,256]{1,0:T(8,128)S(1)}, f32[256,256]{1,0:T(8,128)}, u32[]{:S(2)}) copy-start(f32[256,256]{1,0:T(8,128)} %get-tuple-element.42.refs_1_) | copy-start | bytes 786436

commit v3 on v2

--- a/solution.py
+++ b/solution.py
@@ -253,9 +253,15 @@
     last_step(back_ref, height, twiddle_ref, tile_write(out_ref, rows), blocks, rows, lanes)
 
 
-def window_kernel(
-    decay_in, taps_in, signal_in, pair_ref, window_ref, decay_ref, taps_ref, signal_ref, sems
-):
+def window_of(decay_ref, length):
+    channels = decay_ref.shape[1]
+    start = lax.axis_index("seq") * length
+    places = (start + lax.broadcasted_iota(jnp.int32, (1, length), 1)).astype(f32)
+    rates = jnp.broadcast_to(decay_ref[...], (length, channels)).T
+    return jnp.exp(-rates * places) * jnp.sqrt(2.0 * rates)
+
+
+def send_kernel(decay_in, taps_in, signal_in, pair_ref, decay_ref, taps_ref, signal_ref, sems):
     fetches = [
         pltpu.make_async_copy(source, target, sems.at[at])
         for at, (source, target) in enumerate(
@@ -264,15 +270,10 @@
     ]
     for fetch in fetches:
         fetch.start()
-    channels, length = taps_ref.shape
-    shards, twice, _ = pair_ref.shape
+    shards, twice, length = pair_ref.shape
     owned = twice // 2
-    start = lax.axis_index("seq") * length
-    places = (start + lax.broadcasted_iota(jnp.int32, (1, length), 1)).astype(f32)
     fetches[0].wait()
-    rates = jnp.broadcast_to(decay_ref[...], (length, channels)).T
-    window = jnp.exp(-rates * places) * jnp.sqrt(2.0 * rates)
-    window_ref[...] = window
+    window = window_of(decay_ref, length)
     fetches[1].wait()
     fetches[2].wait()
     filters = (taps_ref[...] * window).astype(bf16)
@@ -280,6 +281,10 @@
         rows = slice(shard * owned, (shard + 1) * owned)
         pair_ref[shard, :owned] = signal_ref[rows]
         pair_ref[shard, owned:] = filters[rows]
+
+
+def window_kernel(decay_ref, window_ref):
+    window_ref[...] = window_of(decay_ref, window_ref.shape[1])
 
 
 def spread_kernel(weight_ref, grad_ref, *out_refs):
@@ -299,7 +304,7 @@
     total = refs[0][...].astype(f32)
     for share in refs[1:-2]:
         total = total + share[...].astype(f32)
-    total_ref[...] = total
+    total_ref[...] = total.astype(bf16)
     grad_mixed_ref[...] = (total * gating_ref[...].astype(f32)).astype(bf16)
 
 
@@ -313,21 +318,28 @@
             out_ref[source] = both_ref[source, block]
 
 
-def gate_kernel(gating_ref, total_ref, *refs):
-    gating_grad_ref, gated_ref = refs[-2:]
-    pieces = refs[:-2]
+def mixed_rows(pieces, channels):
     chip = lax.div(lax.axis_index("seq"), 2)
-    count = gating_ref.shape[0] // len(pieces)
+    count = channels // len(pieces)
     for step, piece in enumerate(pieces):
         place = lax.bitwise_xor(chip, step) if len(pieces) > 1 else 0
         rows = pl.ds(pl.multiple_of(place * count, count), count)
-        mixed = piece[...].reshape(count, -1).astype(f32)
-        gated_ref[rows] = (gating_ref[rows].astype(f32) * mixed).astype(bf16)
-        gating_grad_ref[rows] = total_ref[rows] * mixed
+        yield rows, piece[...].reshape(count, -1).astype(f32)
+
+
+def gate_kernel(gating_ref, *refs):
+    for rows, mixed in mixed_rows(refs[:-1], gating_ref.shape[0]):
+        refs[-1][rows] = (gating_ref[rows].astype(f32) * mixed).astype(bf16)
+
+
+def gating_grad_kernel(total_ref, *refs):
+    for rows, mixed in mixed_rows(refs[:-1], total_ref.shape[0]):
+        refs[-1][rows] = total_ref[rows].astype(f32) * mixed
 
 
 def project_kernel(weight_ref, *refs):
-    gated_refs, out_ref = refs[:-1], refs[-1]
+    gated_refs, (out_ref, token_ref) = refs[:-2], refs[-2:]
+    token_ref[...] = jnp.zeros_like(token_ref)
     count = len(gated_refs)
     rows = weight_ref.shape[0] // count
     me = lax.axis_index("chan")
@@ -342,13 +354,18 @@
     out_ref[...] = total.astype(out_ref.dtype)
 
 
-def return_kernel(back_ref, window_ref, signal_ref, taps_ref):
-    shards, twice, _ = back_ref.shape
-    owned = twice // 2
-    for shard in range(shards):
-        rows = slice(shard * owned, (shard + 1) * owned)
-        signal_ref[rows] = back_ref[shard, :owned].astype(f32)
-        taps_ref[rows] = back_ref[shard, owned:].astype(f32) * window_ref[rows]
+def return_kernel(window_ref, *refs):
+    pieces, (signal_ref, taps_ref) = refs[:-2], refs[-2:]
+    chip = lax.div(lax.axis_index("seq"), 2)
+    for step, piece in enumerate(pieces):
+        blocks, twice, _ = piece.shape
+        owned = twice // 2
+        place = lax.bitwise_xor(chip, step) if len(pieces) > 1 else 0
+        for source in range(blocks):
+            first = pl.multiple_of((place * blocks + source) * owned, owned)
+            rows = pl.ds(first, owned)
+            signal_ref[rows] = piece[source, :owned].astype(f32)
+            taps_ref[rows] = piece[source, owned:].astype(f32) * window_ref[rows]
 
 
 def padded(array, owned, held):
@@ -385,10 +402,11 @@
     def shift(array, step):
         return lax.ppermute(array, "chan", [(i, (i + step) % parts) for i in range(parts)])
 
+    rates = decay_rates.reshape(1, channels)
     if owned == held:
-        pairs, window = call(
-            window_kernel,
-            (shape((shards, 2 * owned, length), bf16), shape((channels, length), f32)),
+        pairs = call(
+            send_kernel,
+            shape((shards, 2 * owned, length), bf16),
             [ANY] * 3,
             (
                 pltpu.VMEM((1, channels), f32),
@@ -397,9 +415,9 @@
                 pltpu.SemaphoreType.DMA((3,)),
             ),
             room=62,
-        )(decay_rates.reshape(1, channels), filter_taps, signal)
+        )(rates, filter_taps, signal)
     else:
-        pairs, window = window_plain(decay_rates, filter_taps, signal, shards)
+        pairs = send_plain(decay_rates, filter_taps, signal, shards)
     arrived = exchange(pairs)
 
     partial = call(
@@ -421,38 +439,38 @@
         micros=2,
     )(padded(arrived, owned, held), table, twiddle)
     chips = shards // 2
-    if chips in (2, 4) and owned == held:
-        def hop(array, distance):
-            return lax.ppermute(array, "seq", [(i, i ^ distance) for i in range(shards)])
-
+    direct = chips in (2, 4) and owned == held
+
+    def hop(array, distance):
+        return lax.ppermute(array, "seq", [(i, i ^ distance) for i in range(shards)])
+
+    def bring(array):
+        if not direct:
+            return [exchange(array)]
         pairs = [[2 * chip, 2 * chip + 1] for chip in range(chips)]
-        both = lax.all_gather(mixed_owned, "seq", axis_index_groups=pairs)
-        pieces = call(
-            pack_kernel,
-            (shape((2, owned, length), bf16),) * chips,
-            [VMEM],
+        both = lax.all_gather(array, "seq", axis_index_groups=pairs)
+        packed = call(
+            pack_kernel, (shape((2,) + array.shape[1:], bf16),) * chips, [VMEM], micros=0
         )(both)
-        pieces = [pieces[0]] + [hop(pieces[step], 2 * step) for step in range(1, chips)]
-    else:
-        pieces = [exchange(trimmed(mixed_owned, owned, held)).reshape(channels, length)]
+        return [packed[0]] + [hop(packed[step], 2 * step) for step in range(1, chips)]
+
+    pieces = bring(trimmed(mixed_owned, owned, held))
 
     total, grad_mixed = call(
         total_kernel,
-        (shape((channels, length), f32), shape((channels, length), bf16)),
+        (shape((channels, length), bf16),) * 2,
         [VMEM] * (2 + len(shares)),
         after=(pieces[0],),
     )(gating, partial[0], *shares)
     grad_whole = exchange(grad_mixed.reshape(shards, owned, length))
 
-    gating_grad, gated = call(
-        gate_kernel,
-        (shape((channels, length), f32), shape((channels, length), bf16)),
-        [VMEM] * (2 + len(pieces)),
-    )(gating, total, *pieces)
+    gated = call(gate_kernel, shape((channels, length), bf16), [VMEM] * (1 + len(pieces)))(
+        gating, *pieces
+    )
     gathered = [gated] + [shift(gated, step) for step in range(1, parts)]
-    mixed_out = call(
+    mixed_out, projected = call(
         project_kernel,
-        shape((length, out_weight.shape[1]), bf16),
+        (shape((length, out_weight.shape[1]), bf16), shape((8, LANES), f32)),
         [VMEM] * (1 + parts),
         micros=12.0,
     )(out_weight, *gathered)
@@ -468,31 +486,33 @@
         micros=2.0,
         after=(gated,),
     )(padded(grad_whole, owned, held), *spectra, table, twiddle)
-    returned = exchange(trimmed(grads_owned, owned, held))
+    returned = bring(trimmed(grads_owned, owned, held))
+    gating_grad = call(
+        gating_grad_kernel, shape((channels, length), f32), [VMEM] * (1 + len(pieces)), after=(projected,)
+    )(total, *pieces)
+    window = call(window_kernel, shape((channels, length), f32), [VMEM], after=(projected,))(rates)
     if owned == held:
         signal_grad, taps_grad = call(
             return_kernel,
             (shape((channels, length), f32), shape((channels, length), f32)),
-            [VMEM] * 2,
-        )(returned, window)
+            [VMEM] * (1 + len(returned)),
+        )(window, *returned)
     else:
-        both = returned.reshape(shards, 2, owned, length).astype(f32)
+        both = returned[0].reshape(shards, 2, owned, length).astype(f32)
         signal_grad = both[:, 0].reshape(channels, length)
         taps_grad = both[:, 1].reshape(channels, length) * window
     return (mixed_out, signal_grad, gating_grad, taps_grad)
 
 
-def window_plain(decay_rates, filter_taps, signal, shards):
+def send_plain(decay_rates, filter_taps, signal, shards):
     channels, length = signal.shape
     owned = channels // shards
     places = (lax.axis_index("seq") * length + jnp.arange(length, dtype=jnp.int32)).astype(f32)
     rates = decay_rates[:, None]
     window = jnp.exp(-rates * places[None, :]) * jnp.sqrt(2.0 * rates)
     filters = (filter_taps * window).astype(bf16)
-    pairs = jnp.stack(
-        [signal.reshape(shards, owned, length), filters.reshape(shards, owned, length)], 1
-    )
-    return pairs.reshape(shards, 2 * owned, length), window
+    pairs = jnp.stack([part.reshape(shards, owned, length) for part in (signal, filters)], 1)
+    return pairs.reshape(shards, 2 * owned, length)
 
 
 def solution(mesh):

time: 47.2 us -> 45.4 us (0.962)
  waiting for transfers between devices: 7.15 us -> 2.29 us
  blocking collectives: 1.99 us -> 4.16 us
  local copies, waits for them, and re-layouts: 0.05 us -> 1.37 us
  Pallas kernels: 8.61 us -> 8.05 us
    ppermute x6, waiting for transfers between devices: 6.11 us -> 0.86 us  [shift(): lax.ppermute(array, 'chan', [(i, (i + step) % parts) for i in range(parts)])]
    all_to_all x3 -> x2, starting transfers between devices: 13.4 us -> 9.07 us  [exchange(): return lax.all_to_all(array, 'seq', split_axis=0, concat_axis=0, tiled=True)]
    ppermute x3 -> x6, starting transfers between devices: 3.55 us -> 7.11 us  [hop(): lax.ppermute(array, 'seq', [(i, i ^ distance) for i in range(shards)])]
    all_gather x1 -> x2, blocking collectives: 1.99 us -> 4.16 us  [bring(): both = lax.all_gather(array, 'seq', axis_index_groups=pairs)]
    unnamed x18, local copies, waits for them, and re-layouts: 0.05 us -> 1.37 us
    ppermute x6, starting transfers between devices: 11.2 us -> 12.1 us  [shift(): lax.ppermute(array, 'chan', [(i, (i + step) % parts) for i in range(parts)])]
    ppermute x3 -> x6, waiting for transfers between devices: 0.01 us -> 0.58 us  [hop(): lax.ppermute(array, 'seq', [(i, i ^ distance) for i in range(shards)])]
    pallas_call x9 -> x12, Pallas kernels: 8.61 us -> 8.05 us  [call(): return lambda *operands: run(*operands, *after)]
  transfers between devices with their start and end apart: 12 -> 14, of which waited for: 4 -> 3; matrix products, arithmetic and copies ran while one was open for 0% -> 0% of each run, Pallas kernels for 13% -> 12%
where the time goes in v3:
time: 45.4 us; the launch traced here: 45 us
  starting transfers between devices  28.3 us (62%)
  Pallas kernels  8.05 us (18%)
  blocking collectives  4.16 us (9%)
  waiting for transfers between devices  2.29 us (5%)
  local copies, waits for them, and re-layouts  1.37 us (3%)
  between operations  0.8 us (2%)
    ppermute x6, starting transfers between devices, shift(): lax.ppermute(array, 'chan', [(i, (i + step) % parts) for i in range(parts)])  12.1 us
    all_to_all x2, starting transfers between devices, exchange(): return lax.all_to_all(array, 'seq', split_axis=0, concat_axis=0, tiled=True)  9.07 us
    pallas_call x12, Pallas kernels, call(): return lambda *operands: run(*operands, *after)  8.05 us
    ppermute x6, starting transfers between devices, hop(): lax.ppermute(array, 'seq', [(i, i ^ distance) for i in range(shards)])  7.11 us
    all_gather x2, blocking collectives, bring(): both = lax.all_gather(array, 'seq', axis_index_groups=pairs)  4.16 us
    unnamed x18, local copies, waits for them, and re-layouts  1.37 us
  transfers between devices with their start and end apart: 14, of which 3 were waited for; matrix products, arithmetic and copies ran while one was open for 0% of the time, Pallas kernels for 12%

profile of v3, /device:TPU:0, one launch (start us, length us, event | category | flops | bytes accessed | tf_op | source)
XLA Modules:
  0.0 45.0 jit_solution(13420154246006092466)
XLA Ops:
  0.6 1.8 %shard_map.111.refs_2_ = bf16[8,64,256]{2,1,0:T(8,128)(2,1)} custom-call(f32[1,256]{1,0:T(1,128)} %bitcast.6, f32[256,256]{1,0:T(8,128)} %refs_1_.3, bf16[256,256]{1,0:T(8,128)(2,1)} %refs_2_.2), custom_call_target="tpu_custom_call" | custom-call | flops 1150000000 | tf_op jit(solution)/shard_map/pallas_call | solution.py:38
  2.5 5.3 %all-to-all-start = ((bf16[8,64,256]{2,1,0:T(8,128)(2,1)}), bf16[8,64,256]{2,1,0:T(8,128)(2,1)S(1)}, u32[]{:S(2)}, u32[]{:S(2)}) async-start(bf16[8,64,256]{2,1,0:T(8,128)(2,1)} %shard_map.111.refs_2_), calls=%async_computation | async-start | bytes 524288 | tf_op jit(solution)/shard_map/all_to_all | solution.py:388
  7.9 0.0 copy-start.6
  7.9 0.5 %shard_map.117 = (bf16[256,256]{1,0:T(8,128)(2,1)S(1)}, bf16[256,256]{1,0:T(8,128)(2,1)S(1)}, bf16[256,256]{1,0:T(8,128)(2,1)S(1)}, bf16[256,256]{1,0:T(8,128)(2,1)S(1)}) custom-call(bf16[1024,512]{1,0:T(8,128)(2,1)S(1)} %copy-done.1, bf16[256,512]{1,0:T(8,128)(2,1)S(1)} %copy-done.2, bf16[8,64,256]{2,1,0:T(8,128)(2,1)S(1)} %copy-done), custom_call_target="tpu_custom_call" | custom-call | flops 1150000000 | tf_op jit(solution)/shard_map/pallas_call | solution.py:38
  8.4 1.6 %collective-permute-start.6 = (bf16[256,256]{1,0:T(8,128)(2,1)S(1)}, bf16[256,256]{1,0:T(8,128)(2,1)S(1)}, u32[]{:S(2)}, u32[]{:S(2)}) collective-permute-start(bf16[256,256]{1,0:T(8,128)(2,1)S(1)} %get-tuple-element.35), channel_id=1, source_target_pairs={{0,1},{1,2},{2,3},{3,0},{4,5},{5,6},{6,7},{7,4},{8,9},{9,10},{10,1... | collective-permute-start | bytes 393224 | tf_op jit(solution)/shard_map/ppermute | solution.py:403
  10.0 2.6 %collective-permute-start.7 = (bf16[256,256]{1,0:T(8,128)(2,1)S(1)}, bf16[256,256]{1,0:T(8,128)(2,1)S(1)}, u32[]{:S(2)}, u32[]{:S(2)}) collective-permute-start(bf16[256,256]{1,0:T(8,128)(2,1)S(1)} %get-tuple-element.36), channel_id=1, source_target_pairs={{0,2},{1,3},{2,0},{3,1},{4,6},{5,7},{6,4},{7,5},{8,10},{9,11},{10,... | collective-permute-start | bytes 393224 | tf_op jit(solution)/shard_map/ppermute | solution.py:403
  12.6 1.3 %collective-permute-start.8 = (bf16[256,256]{1,0:T(8,128)(2,1)S(1)}, bf16[256,256]{1,0:T(8,128)(2,1)S(1)}, u32[]{:S(2)}, u32[]{:S(2)}) collective-permute-start(bf16[256,256]{1,0:T(8,128)(2,1)S(1)} %get-tuple-element.37), channel_id=1, source_target_pairs={{0,3},{1,0},{2,1},{3,2},{4,7},{5,4},{6,5},{7,6},{8,11},{9,8},{10,9... | collective-permute-start | bytes 393224 | tf_op jit(solution)/shard_map/ppermute | solution.py:403
  13.9 0.8 %all-to-all-done.refs_0_ = bf16[8,64,256]{2,1,0:T(8,128)(2,1)S(1)} async-done(((bf16[8,64,256]{2,1,0:T(8,128)(2,1)}), bf16[8,64,256]{2,1,0:T(8,128)(2,1)S(1)}, u32[]{:S(2)}, u32[]{:S(2)}) %all-to-all-start) | async-done | bytes 262176 | tf_op jit(solution)/shard_map/all_to_all | solution.py:388
  14.8 1.0 %shard_map.112 = (bf16[8,32,256]{2,1,0:T(8,128)(2,1)S(1)}, bf16[288,256]{1,0:T(8,128)(2,1)S(1)}, bf16[288,256]{1,0:T(8,128)(2,1)S(1)}, bf16[288,256]{1,0:T(8,128)(2,1)S(1)}, bf16[288,256]{1,0:T(8,128)(2,1)S(1)}) custom-call(bf16[8,64,256]{2,1,0:T(8,128)(2,1)S(1)} %all-to-all-done.refs_0_, bf16[512,512]{1,0:T(8,128)(2,1)S(1)} %copy-done.5, ...), custom_call_target="tpu_custom_call" | custom-call | flops 2300000000 | tf_op jit(solution)/shard_map/pallas_call | solution.py:38
  15.7 0.7 %copy-done.7 = bf16[288,256]{1,0:T(8,128)(2,1)} copy-done((bf16[288,256]{1,0:T(8,128)(2,1)}, bf16[288,256]{1,0:T(8,128)(2,1)S(1)}, u32[]{:S(2)}) %copy-start.7) | copy-done | bytes 147480
  16.4 2.0 %all-gather = bf16[16,32,256]{2,1,0:T(8,128)(2,1)S(1)} all-gather(bf16[8,32,256]{2,1,0:T(8,128)(2,1)S(1)} %get-tuple-element.27), channel_id=2, replica_groups={{0,4},{8,12},{16,20},{24,28},{1,5},{9,13},{17,21},{25,29},{2,6},{10,14}..., dimensions={0}, use_global_device_ids=true | all-gather | bytes 393216 | tf_op jit(solution)/shard_map/all_gather | solution.py:451
  18.4 1.2 %collective-permute-start = (bf16[2,32,256]{2,1,0:T(8,128)(2,1)S(1)}, bf16[2,32,256]{2,1,0:T(8,128)(2,1)S(1)}, u32[]{:S(2)}, u32[]{:S(2)}) collective-permute-start(bf16[2,32,256]{2,1,0:T(8,128)(2,1)S(1)} %get-tuple-element.29), channel_id=1, source_target_pairs={{0,8},{4,12},{8,0},{12,4},{16,24},{20,28},{24,16},{28,20},{1,9},{5... | collective-permute-start | bytes 98312 | tf_op jit(solution)/shard_map/ppermute | solution.py:445
  19.6 1.5 %collective-permute-start.1 = (bf16[2,32,256]{2,1,0:T(8,128)(2,1)S(1)}, bf16[2,32,256]{2,1,0:T(8,128)(2,1)S(1)}, u32[]{:S(2)}, u32[]{:S(2)}) collective-permute-start(bf16[2,32,256]{2,1,0:T(8,128)(2,1)S(1)} %get-tuple-element.30), channel_id=1, source_target_pairs={{0,16},{4,20},{8,24},{12,28},{16,0},{20,4},{24,8},{28,12},{1,17},{... | collective-permute-start | bytes 98312 | tf_op jit(solution)/shard_map/ppermute | solution.py:445
  21.1 0.8 %collective-permute-start.2 = (bf16[2,32,256]{2,1,0:T(8,128)(2,1)S(1)}, bf16[2,32,256]{2,1,0:T(8,128)(2,1)S(1)}, u32[]{:S(2)}, u32[]{:S(2)}) collective-permute-start(bf16[2,32,256]{2,1,0:T(8,128)(2,1)S(1)} %get-tuple-element.31), channel_id=1, source_target_pairs={{0,24},{4,28},{8,16},{12,20},{16,8},{20,12},{24,0},{28,4},{1,25},{... | collective-permute-start | bytes 98312 | tf_op jit(solution)/shard_map/ppermute | solution.py:445
  22.0 0.7 %shard_map.118 = (bf16[256,256]{1,0:T(8,128)(2,1)S(1)}, bf16[256,256]{1,0:T(8,128)(2,1)}) custom-call(bf16[256,256]{1,0:T(8,128)(2,1)S(1)} %copy-done.3, bf16[256,256]{1,0:T(8,128)(2,1)S(1)} %get-tuple-element.34.refs_1_, bf16[256,256]{1,0:T(8,128)(2,1)S(1)} %collective-permute-done.6.refs_2_, bf16[256,256]{1,0:T(8,128)(2,1)S(1)} %collective-permute-done.7.refs_3_, ...), custom_call_target="tpu_custom_call" | custom-call | flops 1150000000 | tf_op jit(solution)/shard_map/pallas_call | solution.py:38
  22.7 3.8 %all-to-all-start.1 = ((bf16[8,32,256]{2,1,0:T(8,128)(2,1)}), bf16[8,32,256]{2,1,0:T(8,128)(2,1)S(1)}, u32[]{:S(2)}, u32[]{:S(2)}) async-start(bf16[8,32,256]{2,1,0:T(8,128)(2,1)} %bitcast.2), calls=%async_computation.1 | async-start | bytes 262144 | tf_op jit(solution)/shard_map/all_to_all | solution.py:388
  26.5 0.1 shard_map.114.refs_1_.refs_7_
  26.6 3.3 %collective-permute-start.3 = (bf16[256,256]{1,0:T(8,128)(2,1)S(1)}, bf16[256,256]{1,0:T(8,128)(2,1)S(1)}, u32[]{:S(2)}, u32[]{:S(2)}) collective-permute-start(bf16[256,256]{1,0:T(8,128)(2,1)S(1)} %shard_map.114.refs_1_.refs_7_), channel_id=1, source_target_pairs={{0,1},{1,2},{2,3},{3,0},{4,5},{5,6},{6,7},{7,4},{8,9},{9,10},{10,1... | collective-permute-start | bytes 393224 | tf_op jit(solution)/shard_map/ppermute | solution.py:403
  29.9 1.6 %collective-permute-start.4 = (bf16[256,256]{1,0:T(8,128)(2,1)S(1)}, bf16[256,256]{1,0:T(8,128)(2,1)S(1)}, u32[]{:S(2)}, u32[]{:S(2)}) collective-permute-start(bf16[256,256]{1,0:T(8,128)(2,1)S(1)} %shard_map.114.refs_1_.refs_7_), channel_id=1, source_target_pairs={{0,2},{1,3},{2,0},{3,1},{4,6},{5,7},{6,4},{7,5},{8,10},{9,11},{10,... | collective-permute-start | bytes 393224 | tf_op jit(solution)/shard_map/ppermute | solution.py:403
  31.5 1.6 %collective-permute-start.5 = (bf16[256,256]{1,0:T(8,128)(2,1)S(1)}, bf16[256,256]{1,0:T(8,128)(2,1)S(1)}, u32[]{:S(2)}, u32[]{:S(2)}) collective-permute-start(bf16[256,256]{1,0:T(8,128)(2,1)S(1)} %shard_map.114.refs_1_.refs_7_), channel_id=1, source_target_pairs={{0,3},{1,0},{2,1},{3,2},{4,7},{5,4},{6,5},{7,6},{8,11},{9,8},{10,9... | collective-permute-start | bytes 393224 | tf_op jit(solution)/shard_map/ppermute | solution.py:403
  33.1 1.1 %shard_map.119 = bf16[8,64,256]{2,1,0:T(8,128)(2,1)S(1)} custom-call(bf16[8,32,256]{2,1,0:T(8,128)(2,1)S(1)} %all-to-all-done.1.refs_0_, bf16[288,256]{1,0:T(8,128)(2,1)S(1)} %get-tuple-element.39.refs_1_, bf16[288,256]{1,0:T(8,128)(2,1)S(1)} %get-tuple-element.40.refs_2_, bf16[288,256]{1,0:T(8,128)(2,1)S(1)} %get-tuple-element.41.refs_3_, ...), custom_call_target="tpu_custom_call" | custom-call | flops 2300000000 | tf_op jit(solution)/shard_map/pallas_call | solution.py:38
  34.2 2.2 %all-gather.1 = bf16[16,64,256]{2,1,0:T(8,128)(2,1)S(1)} all-gather(bf16[8,64,256]{2,1,0:T(8,128)(2,1)S(1)} %shard_map.119), channel_id=3, replica_groups={{0,4},{8,12},{16,20},{24,28},{1,5},{9,13},{17,21},{25,29},{2,6},{10,14}..., dimensions={0}, use_global_device_ids=true | all-gather | bytes 786432 | tf_op jit(solution)/shard_map/all_gather | solution.py:451
  36.4 2.0 %collective-permute-start.10 = (bf16[2,64,256]{2,1,0:T(8,128)(2,1)S(1)}, bf16[2,64,256]{2,1,0:T(8,128)(2,1)S(1)}, u32[]{:S(2)}, u32[]{:S(2)}) collective-permute-start(bf16[2,64,256]{2,1,0:T(8,128)(2,1)S(1)} %get-tuple-element.45), channel_id=1, source_target_pairs={{0,16},{4,20},{8,24},{12,28},{16,0},{20,4},{24,8},{28,12},{1,17},{... | collective-permute-start | bytes 196616 | tf_op jit(solution)/shard_map/ppermute | solution.py:445
  38.4 1.4 %collective-permute-start.11 = (bf16[2,64,256]{2,1,0:T(8,128)(2,1)S(1)}, bf16[2,64,256]{2,1,0:T(8,128)(2,1)S(1)}, u32[]{:S(2)}, u32[]{:S(2)}) collective-permute-start(bf16[2,64,256]{2,1,0:T(8,128)(2,1)S(1)} %get-tuple-element.46), channel_id=1, source_target_pairs={{0,24},{4,28},{8,16},{12,20},{16,8},{20,12},{24,0},{28,4},{1,25},{... | collective-permute-start | bytes 196616 | tf_op jit(solution)/shard_map/ppermute | solution.py:445
  39.8 0.1 collective-permute-start.9
  40.0 0.8 %collective-permute-done.4.refs_3_ = bf16[256,256]{1,0:T(8,128)(2,1)S(1)} collective-permute-done((bf16[256,256]{1,0:T(8,128)(2,1)S(1)}, bf16[256,256]{1,0:T(8,128)(2,1)S(1)}, u32[]{:S(2)}, u32[]{:S(2)}) %collective-permute-start.4) | collective-permute-done | bytes 131104 | tf_op jit(solution)/shard_map/ppermute | solution.py:403
  40.8 1.2 %shard_map.115 = (bf16[256,512]{1,0:T(8,128)(2,1)}, f32[8,128]{1,0:T(8,128)S(1)}) custom-call(bf16[1024,512]{1,0:T(8,128)(2,1)S(1)} %copy-done.1, bf16[256,256]{1,0:T(8,128)(2,1)S(1)} %shard_map.114.refs_1_.refs_7_, bf16[256,256]{1,0:T(8,128)(2,1)S(1)} %collective-permute-done.3.refs_2_, bf16[256,256]{1,0:T(8,128)(2,1)S(1)} %collective-permute-done.4.refs_3_, ...), custom_call_target="tpu_custom_call" | custom-call | flops 13799999488 | tf_op jit(solution)/shard_map/pallas_call | solution.py:38
  42.0 0.7 %copy-done.4 = f32[256]{0:T(256)S(1)} copy-done((f32[256]{0:T(256)S(1)}, f32[256]{0:T(256)}, u32[]{:S(2)}) %copy-start.4) | copy-done | bytes 1048
  42.7 0.1 shard_map.116.refs_0_
  42.8 0.8 %shard_map.122 = f32[256,256]{1,0:T(8,128)} custom-call(bf16[256,256]{1,0:T(8,128)(2,1)S(1)} %get-tuple-element.48.refs_0_, bf16[2,32,256]{2,1,0:T(8,128)(2,1)S(1)} %get-tuple-element.28.refs_1_.refs_5_, bf16[2,32,256]{2,1,0:T(8,128)(2,1)S(1)} %collective-permute-done.refs_2_, bf16[2,32,256]{2,1,0:T(8,128)(2,1)S(1)} %collective-permute-done.1.refs_3_, ...), custom_call_target="tpu_custom_call" | custom-call | flops 1150000000 | tf_op jit(solution)/shard_map/pallas_call | solution.py:38
  43.6 0.6 %collective-permute-done.11.refs_4_ = bf16[2,64,256]{2,1,0:T(8,128)(2,1)S(1)} collective-permute-done((bf16[2,64,256]{2,1,0:T(8,128)(2,1)S(1)}, bf16[2,64,256]{2,1,0:T(8,128)(2,1)S(1)}, u32[]{:S(2)}, u32[]{:S(2)}) %collective-permute-start.11) | collective-permute-done | bytes 65568 | tf_op jit(solution)/shard_map/ppermute | solution.py:445
  44.1 0.8 %shard_map.121 = (f32[256,256]{1,0:T(8,128)}, f32[256,256]{1,0:T(8,128)}) custom-call(f32[256,256]{1,0:T(8,128)S(1)} %shard_map.116.refs_0_, bf16[2,64,256]{2,1,0:T(8,128)(2,1)S(1)} %get-tuple-element.43.refs_1_, bf16[2,64,256]{2,1,0:T(8,128)(2,1)S(1)} %collective-permute-done.9.refs_2_, bf16[2,64,256]{2,1,0:T(8,128)(2,1)S(1)} %collective-permute-done.10.refs_3_, ...), custom_call_target="tpu_custom_call" | custom-call | flops 1150000000 | tf_op jit(solution)/shard_map/pallas_call | solution.py:38
  (28 shorter events, 0.1 us)
Async XLA Ops:
  0.6 7.2 %copy-start.1 = (bf16[1024,512]{1,0:T(8,128)(2,1)S(1)}, bf16[1024,512]{1,0:T(8,128)(2,1)}, u32[]{:S(2)}) copy-start(bf16[1024,512]{1,0:T(8,128)(2,1)} %refs_0_.6) | copy-start | bytes 3145732
  2.5 5.3 %copy-start = (bf16[8,64,256]{2,1,0:T(8,128)(2,1)S(1)}, bf16[8,64,256]{2,1,0:T(8,128)(2,1)}, u32[]{:S(2)}) copy-start(bf16[8,64,256]{2,1,0:T(8,128)(2,1)} %shard_map.111.refs_2_) | copy-start | bytes 786436
  2.5 5.3 %copy-start.2 = (bf16[256,512]{1,0:T(8,128)(2,1)S(1)}, bf16[256,512]{1,0:T(8,128)(2,1)}, u32[]{:S(2)}) copy-start(bf16[256,512]{1,0:T(8,128)(2,1)} %refs_1_.4) | copy-start | bytes 786436
  2.5 12.3 %all-to-all-start = ((bf16[8,64,256]{2,1,0:T(8,128)(2,1)}), bf16[8,64,256]{2,1,0:T(8,128)(2,1)S(1)}, u32[]{:S(2)}, u32[]{:S(2)}) async-start(bf16[8,64,256]{2,1,0:T(8,128)(2,1)} %shard_map.111.refs_2_), calls=%async_computation | async-start | bytes 524288 | tf_op jit(solution)/shard_map/all_to_all | solution.py:388
  7.9 6.9 %copy-start.5 = (bf16[512,512]{1,0:T(8,128)(2,1)S(1)}, bf16[512,512]{1,0:T(8,128)(2,1)}, u32[]{:S(2)}) copy-start(bf16[512,512]{1,0:T(8,128)(2,1)} %constant.4.clone.refs_1_.refs_5_) | copy-start | bytes 1572868
  7.9 6.9 %copy-start.6 = (f32[9,2,256]{2,1,0:T(2,128)S(1)}, f32[9,2,256]{2,1,0:T(2,128)}, u32[]{:S(2)}) copy-start(f32[9,2,256]{2,1,0:T(2,128)} %constant.5.clone.refs_2_.refs_6_) | copy-start | bytes 55300
  8.4 12.8 %collective-permute-start.6 = (bf16[256,256]{1,0:T(8,128)(2,1)S(1)}, bf16[256,256]{1,0:T(8,128)(2,1)S(1)}, u32[]{:S(2)}, u32[]{:S(2)}) collective-permute-start(bf16[256,256]{1,0:T(8,128)(2,1)S(1)} %get-tuple-element.35), channel_id=1, source_target_pairs={{0,1},{1,2},{2,3},{3,0},{4,5},{5,6},{6,7},{7,4},{8,9},{9,10},{10,1... | collective-permute-start | bytes 393224 | tf_op jit(solution)/shard_map/ppermute | solution.py:403
  10.0 12.0 %collective-permute-start.7 = (bf16[256,256]{1,0:T(8,128)(2,1)S(1)}, bf16[256,256]{1,0:T(8,128)(2,1)S(1)}, u32[]{:S(2)}, u32[]{:S(2)}) collective-permute-start(bf16[256,256]{1,0:T(8,128)(2,1)S(1)} %get-tuple-element.36), channel_id=1, source_target_pairs={{0,2},{1,3},{2,0},{3,1},{4,6},{5,7},{6,4},{7,5},{8,10},{9,11},{10,... | collective-permute-start | bytes 393224 | tf_op jit(solution)/shard_map/ppermute | solution.py:403
  12.6 9.4 %collective-permute-start.8 = (bf16[256,256]{1,0:T(8,128)(2,1)S(1)}, bf16[256,256]{1,0:T(8,128)(2,1)S(1)}, u32[]{:S(2)}, u32[]{:S(2)}) collective-permute-start(bf16[256,256]{1,0:T(8,128)(2,1)S(1)} %get-tuple-element.37), channel_id=1, source_target_pairs={{0,3},{1,0},{2,1},{3,2},{4,7},{5,4},{6,5},{7,6},{8,11},{9,8},{10,9... | collective-permute-start | bytes 393224 | tf_op jit(solution)/shard_map/ppermute | solution.py:403
  15.7 0.7 %copy-start.7 = (bf16[288,256]{1,0:T(8,128)(2,1)}, bf16[288,256]{1,0:T(8,128)(2,1)S(1)}, u32[]{:S(2)}) copy-start(bf16[288,256]{1,0:T(8,128)(2,1)S(1)} %get-tuple-element.42.refs_4_) | copy-start | bytes 442372
  18.4 3.6 %copy-start.3 = (bf16[256,256]{1,0:T(8,128)(2,1)S(1)}, bf16[256,256]{1,0:T(8,128)(2,1)}, u32[]{:S(2)}) copy-start(bf16[256,256]{1,0:T(8,128)(2,1)} %refs_0_.7) | copy-start | bytes 393220
  18.4 8.1 %collective-permute-start = (bf16[2,32,256]{2,1,0:T(8,128)(2,1)S(1)}, bf16[2,32,256]{2,1,0:T(8,128)(2,1)S(1)}, u32[]{:S(2)}, u32[]{:S(2)}) collective-permute-start(bf16[2,32,256]{2,1,0:T(8,128)(2,1)S(1)} %get-tuple-element.29), channel_id=1, source_target_pairs={{0,8},{4,12},{8,0},{12,4},{16,24},{20,28},{24,16},{28,20},{1,9},{5... | collective-permute-start | bytes 98312 | tf_op jit(solution)/shard_map/ppermute | solution.py:445
  19.6 6.8 %collective-permute-start.1 = (bf16[2,32,256]{2,1,0:T(8,128)(2,1)S(1)}, bf16[2,32,256]{2,1,0:T(8,128)(2,1)S(1)}, u32[]{:S(2)}, u32[]{:S(2)}) collective-permute-start(bf16[2,32,256]{2,1,0:T(8,128)(2,1)S(1)} %get-tuple-element.30), channel_id=1, source_target_pairs={{0,16},{4,20},{8,24},{12,28},{16,0},{20,4},{24,8},{28,12},{1,17},{... | collective-permute-start | bytes 98312 | tf_op jit(solution)/shard_map/ppermute | solution.py:445
  21.1 5.4 %collective-permute-start.2 = (bf16[2,32,256]{2,1,0:T(8,128)(2,1)S(1)}, bf16[2,32,256]{2,1,0:T(8,128)(2,1)S(1)}, u32[]{:S(2)}, u32[]{:S(2)}) collective-permute-start(bf16[2,32,256]{2,1,0:T(8,128)(2,1)S(1)} %get-tuple-element.31), channel_id=1, source_target_pairs={{0,24},{4,28},{8,16},{12,20},{16,8},{20,12},{24,0},{28,4},{1,25},{... | collective-permute-start | bytes 98312 | tf_op jit(solution)/shard_map/ppermute | solution.py:445
  22.7 10.4 %all-to-all-start.1 = ((bf16[8,32,256]{2,1,0:T(8,128)(2,1)}), bf16[8,32,256]{2,1,0:T(8,128)(2,1)S(1)}, u32[]{:S(2)}, u32[]{:S(2)}) async-start(bf16[8,32,256]{2,1,0:T(8,128)(2,1)} %bitcast.2), calls=%async_computation.1 | async-start | bytes 262144 | tf_op jit(solution)/shard_map/all_to_all | solution.py:388
  26.5 6.7 %copy-start.8 = (bf16[288,256]{1,0:T(8,128)(2,1)S(1)}, bf16[288,256]{1,0:T(8,128)(2,1)}, u32[]{:S(2)}) copy-start(bf16[288,256]{1,0:T(8,128)(2,1)} %copy-done.7) | copy-start | bytes 442372
  26.6 13.2 %collective-permute-start.3 = (bf16[256,256]{1,0:T(8,128)(2,1)S(1)}, bf16[256,256]{1,0:T(8,128)(2,1)S(1)}, u32[]{:S(2)}, u32[]{:S(2)}) collective-permute-start(bf16[256,256]{1,0:T(8,128)(2,1)S(1)} %shard_map.114.refs_1_.refs_7_), channel_id=1, source_target_pairs={{0,1},{1,2},{2,3},{3,0},{4,5},{5,6},{6,7},{7,4},{8,9},{9,10},{10,1... | collective-permute-start | bytes 393224 | tf_op jit(solution)/shard_map/ppermute | solution.py:403
  29.9 10.9 %collective-permute-start.4 = (bf16[256,256]{1,0:T(8,128)(2,1)S(1)}, bf16[256,256]{1,0:T(8,128)(2,1)S(1)}, u32[]{:S(2)}, u32[]{:S(2)}) collective-permute-start(bf16[256,256]{1,0:T(8,128)(2,1)S(1)} %shard_map.114.refs_1_.refs_7_), channel_id=1, source_target_pairs={{0,2},{1,3},{2,0},{3,1},{4,6},{5,7},{6,4},{7,5},{8,10},{9,11},{10,... | collective-permute-start | bytes 393224 | tf_op jit(solution)/shard_map/ppermute | solution.py:403
  31.5 9.3 %collective-permute-start.5 = (bf16[256,256]{1,0:T(8,128)(2,1)S(1)}, bf16[256,256]{1,0:T(8,128)(2,1)S(1)}, u32[]{:S(2)}, u32[]{:S(2)}) collective-permute-start(bf16[256,256]{1,0:T(8,128)(2,1)S(1)} %shard_map.114.refs_1_.refs_7_), channel_id=1, source_target_pairs={{0,3},{1,0},{2,1},{3,2},{4,7},{5,4},{6,5},{7,6},{8,11},{9,8},{10,9... | collective-permute-start | bytes 393224 | tf_op jit(solution)/shard_map/ppermute | solution.py:403
  36.4 7.2 %collective-permute-start.10 = (bf16[2,64,256]{2,1,0:T(8,128)(2,1)S(1)}, bf16[2,64,256]{2,1,0:T(8,128)(2,1)S(1)}, u32[]{:S(2)}, u32[]{:S(2)}) collective-permute-start(bf16[2,64,256]{2,1,0:T(8,128)(2,1)S(1)} %get-tuple-element.45), channel_id=1, source_target_pairs={{0,16},{4,20},{8,24},{12,28},{16,0},{20,4},{24,8},{28,12},{1,17},{... | collective-permute-start | bytes 196616 | tf_op jit(solution)/shard_map/ppermute | solution.py:445
  38.4 5.8 %collective-permute-start.11 = (bf16[2,64,256]{2,1,0:T(8,128)(2,1)S(1)}, bf16[2,64,256]{2,1,0:T(8,128)(2,1)S(1)}, u32[]{:S(2)}, u32[]{:S(2)}) collective-permute-start(bf16[2,64,256]{2,1,0:T(8,128)(2,1)S(1)} %get-tuple-element.46), channel_id=1, source_target_pairs={{0,24},{4,28},{8,16},{12,20},{16,8},{20,12},{24,0},{28,4},{1,25},{... | collective-permute-start | bytes 196616 | tf_op jit(solution)/shard_map/ppermute | solution.py:445
  39.8 4.3 %collective-permute-start.9 = (bf16[2,64,256]{2,1,0:T(8,128)(2,1)S(1)}, bf16[2,64,256]{2,1,0:T(8,128)(2,1)S(1)}, u32[]{:S(2)}, u32[]{:S(2)}) collective-permute-start(bf16[2,64,256]{2,1,0:T(8,128)(2,1)S(1)} %get-tuple-element.44), channel_id=1, source_target_pairs={{0,8},{4,12},{8,0},{12,4},{16,24},{20,28},{24,16},{28,20},{1,9},{5... | collective-permute-start | bytes 196616 | tf_op jit(solution)/shard_map/ppermute | solution.py:445
  42.0 0.7 %copy-start.4 = (f32[256]{0:T(256)S(1)}, f32[256]{0:T(256)}, u32[]{:S(2)}) copy-start(f32[256]{0:T(256)} %param.11) | copy-start | bytes 3076

commit v4 on v3

--- a/solution.py
+++ b/solution.py
@@ -283,10 +283,6 @@
         pair_ref[shard, owned:] = filters[rows]
 
 
-def window_kernel(decay_ref, window_ref):
-    window_ref[...] = window_of(decay_ref, window_ref.shape[1])
-
-
 def spread_kernel(weight_ref, grad_ref, *out_refs):
     count = len(out_refs)
     rows = weight_ref.shape[0] // count
@@ -332,15 +328,12 @@
         refs[-1][rows] = (gating_ref[rows].astype(f32) * mixed).astype(bf16)
 
 
-def gating_grad_kernel(total_ref, *refs):
-    for rows, mixed in mixed_rows(refs[:-1], total_ref.shape[0]):
-        refs[-1][rows] = total_ref[rows].astype(f32) * mixed
-
-
-def project_kernel(weight_ref, *refs):
-    gated_refs, (out_ref, token_ref) = refs[:-2], refs[-2:]
-    token_ref[...] = jnp.zeros_like(token_ref)
-    count = len(gated_refs)
+def project_kernel(count, weight_ref, total_ref, decay_ref, *refs):
+    gated_refs, pieces = refs[:count], refs[count:-3]
+    out_ref, gating_grad_ref, window_ref = refs[-3:]
+    window_ref[...] = window_of(decay_ref, total_ref.shape[1])
+    for rows, mixed in mixed_rows(pieces, total_ref.shape[0]):
+        gating_grad_ref[rows] = total_ref[rows].astype(f32) * mixed
     rows = weight_ref.shape[0] // count
     me = lax.axis_index("chan")
     total = None
@@ -354,10 +347,10 @@
     out_ref[...] = total.astype(out_ref.dtype)
 
 
-def return_kernel(window_ref, *refs):
+def return_kernel(order, window_ref, *refs):
     pieces, (signal_ref, taps_ref) = refs[:-2], refs[-2:]
     chip = lax.div(lax.axis_index("seq"), 2)
-    for step, piece in enumerate(pieces):
+    for step, piece in zip(order, pieces):
         blocks, twice, _ = piece.shape
         owned = twice // 2
         place = lax.bitwise_xor(chip, step) if len(pieces) > 1 else 0
@@ -468,12 +461,16 @@
         gating, *pieces
     )
     gathered = [gated] + [shift(gated, step) for step in range(1, parts)]
-    mixed_out, projected = call(
-        project_kernel,
-        (shape((length, out_weight.shape[1]), bf16), shape((8, LANES), f32)),
-        [VMEM] * (1 + parts),
+    mixed_out, gating_grad, window = call(
+        functools.partial(project_kernel, parts),
+        (
+            shape((length, out_weight.shape[1]), bf16),
+            shape((channels, length), f32),
+            shape((channels, length), f32),
+        ),
+        [VMEM] * (3 + parts + len(pieces)),
         micros=12.0,
-    )(out_weight, *gathered)
+    )(out_weight, total, rates, *gathered, *pieces)
 
     grads_owned = call(
         correlate_kernel,
@@ -487,16 +484,13 @@
         after=(gated,),
     )(padded(grad_whole, owned, held), *spectra, table, twiddle)
     returned = bring(trimmed(grads_owned, owned, held))
-    gating_grad = call(
-        gating_grad_kernel, shape((channels, length), f32), [VMEM] * (1 + len(pieces)), after=(projected,)
-    )(total, *pieces)
-    window = call(window_kernel, shape((channels, length), f32), [VMEM], after=(projected,))(rates)
+    order = (0, 2, 3, 1) if len(returned) == 4 else range(len(returned))
     if owned == held:
         signal_grad, taps_grad = call(
-            return_kernel,
+            functools.partial(return_kernel, order),
             (shape((channels, length), f32), shape((channels, length), f32)),
             [VMEM] * (1 + len(returned)),
-        )(window, *returned)
+        )(window, *(returned[step] for step in order))
     else:
         both = returned[0].reshape(shards, 2, owned, length).astype(f32)
         signal_grad = both[:, 0].reshape(channels, length)

time: 45.4 us -> 45.3 us (level)
  waiting for transfers between devices: 2.29 us -> 3.83 us
  Pallas kernels: 8.05 us -> 7.15 us
  local copies, waits for them, and re-layouts: 1.37 us -> 0.7 us
    ppermute x6, waiting for transfers between devices: 0.58 us -> 2.12 us  [hop(): lax.ppermute(array, 'seq', [(i, i ^ distance) for i in range(shards)])]
    pallas_call x12 -> x10, Pallas kernels: 8.05 us -> 7.15 us  [call(): return lambda *operands: run(*operands, *after)]
    unnamed x18, local copies, waits for them, and re-layouts: 1.37 us -> 0.7 us
  transfers between devices with their start and end apart: 14 -> 14, of which waited for: 3 -> 4; matrix products, arithmetic and copies ran while one was open for 0% -> 0% of each run, Pallas kernels for 12% -> 10%
where the time goes in v4:
time: 45.3 us; the launch traced here: 44.9 us
  starting transfers between devices  28.3 us (62%)
  Pallas kernels  7.15 us (16%)
  blocking collectives  4.16 us (9%)
  waiting for transfers between devices  3.83 us (8%)
  between operations  0.79 us (2%)
  local copies, waits for them, and re-layouts  0.7 us (2%)
    ppermute x6, starting transfers between devices, shift(): lax.ppermute(array, 'chan', [(i, (i + step) % parts) for i in range(parts)])  12.1 us
    all_to_all x2, starting transfers between devices, exchange(): return lax.all_to_all(array, 'seq', split_axis=0, concat_axis=0, tiled=True)  9.07 us
    pallas_call x10, Pallas kernels, call(): return lambda *operands: run(*operands, *after)  7.15 us
    ppermute x6, starting transfers between devices, hop(): lax.ppermute(array, 'seq', [(i, i ^ distance) for i in range(shards)])  7.11 us
    all_gather x2, blocking collectives, bring(): both = lax.all_gather(array, 'seq', axis_index_groups=pairs)  4.16 us
    ppermute x6, waiting for transfers between devices, hop(): lax.ppermute(array, 'seq', [(i, i ^ distance) for i in range(shards)])  2.12 us
  transfers between devices with their start and end apart: 14, of which 4 were waited for; matrix products, arithmetic and copies ran while one was open for 0% of the time, Pallas kernels for 10%

profile of v4, /device:TPU:0, one launch (start us, length us, event | category | flops | bytes accessed | tf_op | source)
XLA Modules:
  0.0 44.9 jit_solution(9271227044079002250)
XLA Ops:
  0.6 1.8 %shard_map.111.refs_2_ = bf16[8,64,256]{2,1,0:T(8,128)(2,1)} custom-call(f32[1,256]{1,0:T(1,128)} %bitcast.6, f32[256,256]{1,0:T(8,128)} %refs_1_.3, bf16[256,256]{1,0:T(8,128)(2,1)} %refs_2_.2), custom_call_target="tpu_custom_call" | custom-call | flops 1150000000 | tf_op jit(solution)/shard_map/pallas_call | solution.py:38
  2.5 0.0 copy-start.2
  2.5 5.3 %all-to-all-start = ((bf16[8,64,256]{2,1,0:T(8,128)(2,1)}), bf16[8,64,256]{2,1,0:T(8,128)(2,1)S(1)}, u32[]{:S(2)}, u32[]{:S(2)}) async-start(bf16[8,64,256]{2,1,0:T(8,128)(2,1)} %shard_map.111.refs_2_), calls=%async_computation | async-start | bytes 524288 | tf_op jit(solution)/shard_map/all_to_all | solution.py:381
  7.9 0.0 copy-start.5
  7.9 0.0 copy-start.6
  7.9 0.5 %shard_map.112 = (bf16[256,256]{1,0:T(8,128)(2,1)S(1)}, bf16[256,256]{1,0:T(8,128)(2,1)S(1)}, bf16[256,256]{1,0:T(8,128)(2,1)S(1)}, bf16[256,256]{1,0:T(8,128)(2,1)S(1)}) custom-call(bf16[1024,512]{1,0:T(8,128)(2,1)S(1)} %copy-done.1, bf16[256,512]{1,0:T(8,128)(2,1)S(1)} %copy-done.2, bf16[8,64,256]{2,1,0:T(8,128)(2,1)S(1)} %copy-done), custom_call_target="tpu_custom_call" | custom-call | flops 1150000000 | tf_op jit(solution)/shard_map/pallas_call | solution.py:38
  8.4 1.6 %collective-permute-start = (bf16[256,256]{1,0:T(8,128)(2,1)S(1)}, bf16[256,256]{1,0:T(8,128)(2,1)S(1)}, u32[]{:S(2)}, u32[]{:S(2)}) collective-permute-start(bf16[256,256]{1,0:T(8,128)(2,1)S(1)} %get-tuple-element.29), channel_id=1, source_target_pairs={{0,1},{1,2},{2,3},{3,0},{4,5},{5,6},{6,7},{7,4},{8,9},{9,10},{10,1... | collective-permute-start | bytes 393224 | tf_op jit(solution)/shard_map/ppermute | solution.py:396
  10.0 2.6 %collective-permute-start.1 = (bf16[256,256]{1,0:T(8,128)(2,1)S(1)}, bf16[256,256]{1,0:T(8,128)(2,1)S(1)}, u32[]{:S(2)}, u32[]{:S(2)}) collective-permute-start(bf16[256,256]{1,0:T(8,128)(2,1)S(1)} %get-tuple-element.30), channel_id=1, source_target_pairs={{0,2},{1,3},{2,0},{3,1},{4,6},{5,7},{6,4},{7,5},{8,10},{9,11},{10,... | collective-permute-start | bytes 393224 | tf_op jit(solution)/shard_map/ppermute | solution.py:396
  12.6 1.3 %collective-permute-start.2 = (bf16[256,256]{1,0:T(8,128)(2,1)S(1)}, bf16[256,256]{1,0:T(8,128)(2,1)S(1)}, u32[]{:S(2)}, u32[]{:S(2)}) collective-permute-start(bf16[256,256]{1,0:T(8,128)(2,1)S(1)} %get-tuple-element.31), channel_id=1, source_target_pairs={{0,3},{1,0},{2,1},{3,2},{4,7},{5,4},{6,5},{7,6},{8,11},{9,8},{10,9... | collective-permute-start | bytes 393224 | tf_op jit(solution)/shard_map/ppermute | solution.py:396
  13.9 0.8 %all-to-all-done.refs_0_ = bf16[8,64,256]{2,1,0:T(8,128)(2,1)S(1)} async-done(((bf16[8,64,256]{2,1,0:T(8,128)(2,1)}), bf16[8,64,256]{2,1,0:T(8,128)(2,1)S(1)}, u32[]{:S(2)}, u32[]{:S(2)}) %all-to-all-start) | async-done | bytes 262176 | tf_op jit(solution)/shard_map/all_to_all | solution.py:381
  14.8 1.0 %shard_map.113 = (bf16[8,32,256]{2,1,0:T(8,128)(2,1)S(1)}, bf16[288,256]{1,0:T(8,128)(2,1)S(1)}, bf16[288,256]{1,0:T(8,128)(2,1)S(1)}, bf16[288,256]{1,0:T(8,128)(2,1)S(1)}, bf16[288,256]{1,0:T(8,128)(2,1)S(1)}) custom-call(bf16[8,64,256]{2,1,0:T(8,128)(2,1)S(1)} %all-to-all-done.refs_0_, bf16[512,512]{1,0:T(8,128)(2,1)S(1)} %copy-done.5, ...), custom_call_target="tpu_custom_call" | custom-call | flops 2300000000 | tf_op jit(solution)/shard_map/pallas_call | solution.py:38
  15.7 0.7 %copy-done.7 = bf16[288,256]{1,0:T(8,128)(2,1)} copy-done((bf16[288,256]{1,0:T(8,128)(2,1)}, bf16[288,256]{1,0:T(8,128)(2,1)S(1)}, u32[]{:S(2)}) %copy-start.7) | copy-done | bytes 147480
  16.4 2.0 %all-gather = bf16[16,32,256]{2,1,0:T(8,128)(2,1)S(1)} all-gather(bf16[8,32,256]{2,1,0:T(8,128)(2,1)S(1)} %get-tuple-element.32), channel_id=2, replica_groups={{0,4},{8,12},{16,20},{24,28},{1,5},{9,13},{17,21},{25,29},{2,6},{10,14}..., dimensions={0}, use_global_device_ids=true | all-gather | bytes 393216 | tf_op jit(solution)/shard_map/all_gather | solution.py:444
  18.4 1.2 %collective-permute-start.3 = (bf16[2,32,256]{2,1,0:T(8,128)(2,1)S(1)}, bf16[2,32,256]{2,1,0:T(8,128)(2,1)S(1)}, u32[]{:S(2)}, u32[]{:S(2)}) collective-permute-start(bf16[2,32,256]{2,1,0:T(8,128)(2,1)S(1)} %get-tuple-element.35), channel_id=1, source_target_pairs={{0,8},{4,12},{8,0},{12,4},{16,24},{20,28},{24,16},{28,20},{1,9},{5... | collective-permute-start | bytes 98312 | tf_op jit(solution)/shard_map/ppermute | solution.py:438
  19.6 1.5 %collective-permute-start.4 = (bf16[2,32,256]{2,1,0:T(8,128)(2,1)S(1)}, bf16[2,32,256]{2,1,0:T(8,128)(2,1)S(1)}, u32[]{:S(2)}, u32[]{:S(2)}) collective-permute-start(bf16[2,32,256]{2,1,0:T(8,128)(2,1)S(1)} %get-tuple-element.36), channel_id=1, source_target_pairs={{0,16},{4,20},{8,24},{12,28},{16,0},{20,4},{24,8},{28,12},{1,17},{... | collective-permute-start | bytes 98312 | tf_op jit(solution)/shard_map/ppermute | solution.py:438
  21.1 0.8 %collective-permute-start.5 = (bf16[2,32,256]{2,1,0:T(8,128)(2,1)S(1)}, bf16[2,32,256]{2,1,0:T(8,128)(2,1)S(1)}, u32[]{:S(2)}, u32[]{:S(2)}) collective-permute-start(bf16[2,32,256]{2,1,0:T(8,128)(2,1)S(1)} %get-tuple-element.37), channel_id=1, source_target_pairs={{0,24},{4,28},{8,16},{12,20},{16,8},{20,12},{24,0},{28,4},{1,25},{... | collective-permute-start | bytes 98312 | tf_op jit(solution)/shard_map/ppermute | solution.py:438
  22.0 0.7 %shard_map.115 = (bf16[256,256]{1,0:T(8,128)(2,1)S(1)}, bf16[256,256]{1,0:T(8,128)(2,1)}) custom-call(bf16[256,256]{1,0:T(8,128)(2,1)S(1)} %copy-done.3, bf16[256,256]{1,0:T(8,128)(2,1)S(1)} %get-tuple-element.28.refs_1_, bf16[256,256]{1,0:T(8,128)(2,1)S(1)} %collective-permute-done.refs_2_, bf16[256,256]{1,0:T(8,128)(2,1)S(1)} %collective-permute-done.1.refs_3_, ...), custom_call_target="tpu_custom_call" | custom-call | flops 1150000000 | tf_op jit(solution)/shard_map/pallas_call | solution.py:38
  22.7 3.8 %all-to-all-start.1 = ((bf16[8,32,256]{2,1,0:T(8,128)(2,1)}), bf16[8,32,256]{2,1,0:T(8,128)(2,1)S(1)}, u32[]{:S(2)}, u32[]{:S(2)}) async-start(bf16[8,32,256]{2,1,0:T(8,128)(2,1)} %bitcast.2), calls=%async_computation.1 | async-start | bytes 262144 | tf_op jit(solution)/shard_map/all_to_all | solution.py:381
  26.5 0.1 shard_map.116.refs_3_.refs_7_
  26.6 3.3 %collective-permute-start.6 = (bf16[256,256]{1,0:T(8,128)(2,1)S(1)}, bf16[256,256]{1,0:T(8,128)(2,1)S(1)}, u32[]{:S(2)}, u32[]{:S(2)}) collective-permute-start(bf16[256,256]{1,0:T(8,128)(2,1)S(1)} %shard_map.116.refs_3_.refs_7_), channel_id=1, source_target_pairs={{0,1},{1,2},{2,3},{3,0},{4,5},{5,6},{6,7},{7,4},{8,9},{9,10},{10,1... | collective-permute-start | bytes 393224 | tf_op jit(solution)/shard_map/ppermute | solution.py:396
  29.9 1.6 %collective-permute-start.7 = (bf16[256,256]{1,0:T(8,128)(2,1)S(1)}, bf16[256,256]{1,0:T(8,128)(2,1)S(1)}, u32[]{:S(2)}, u32[]{:S(2)}) collective-permute-start(bf16[256,256]{1,0:T(8,128)(2,1)S(1)} %shard_map.116.refs_3_.refs_7_), channel_id=1, source_target_pairs={{0,2},{1,3},{2,0},{3,1},{4,6},{5,7},{6,4},{7,5},{8,10},{9,11},{10,... | collective-permute-start | bytes 393224 | tf_op jit(solution)/shard_map/ppermute | solution.py:396
  31.5 1.6 %collective-permute-start.8 = (bf16[256,256]{1,0:T(8,128)(2,1)S(1)}, bf16[256,256]{1,0:T(8,128)(2,1)S(1)}, u32[]{:S(2)}, u32[]{:S(2)}) collective-permute-start(bf16[256,256]{1,0:T(8,128)(2,1)S(1)} %shard_map.116.refs_3_.refs_7_), channel_id=1, source_target_pairs={{0,3},{1,0},{2,1},{3,2},{4,7},{5,4},{6,5},{7,6},{8,11},{9,8},{10,9... | collective-permute-start | bytes 393224 | tf_op jit(solution)/shard_map/ppermute | solution.py:396
  33.1 1.1 %shard_map.118 = bf16[8,64,256]{2,1,0:T(8,128)(2,1)S(1)} custom-call(bf16[8,32,256]{2,1,0:T(8,128)(2,1)S(1)} %all-to-all-done.1.refs_0_, bf16[288,256]{1,0:T(8,128)(2,1)S(1)} %get-tuple-element.41.refs_1_, bf16[288,256]{1,0:T(8,128)(2,1)S(1)} %get-tuple-element.42.refs_2_, bf16[288,256]{1,0:T(8,128)(2,1)S(1)} %get-tuple-element.43.refs_3_, ...), custom_call_target="tpu_custom_call" | custom-call | flops 2300000000 | tf_op jit(solution)/shard_map/pallas_call | solution.py:38
  34.2 2.2 %all-gather.1 = bf16[16,64,256]{2,1,0:T(8,128)(2,1)S(1)} all-gather(bf16[8,64,256]{2,1,0:T(8,128)(2,1)S(1)} %shard_map.118), channel_id=3, replica_groups={{0,4},{8,12},{16,20},{24,28},{1,5},{9,13},{17,21},{25,29},{2,6},{10,14}..., dimensions={0}, use_global_device_ids=true | all-gather | bytes 786432 | tf_op jit(solution)/shard_map/all_gather | solution.py:444
  36.4 2.9 %collective-permute-start.10 = (bf16[2,64,256]{2,1,0:T(8,128)(2,1)S(1)}, bf16[2,64,256]{2,1,0:T(8,128)(2,1)S(1)}, u32[]{:S(2)}, u32[]{:S(2)}) collective-permute-start(bf16[2,64,256]{2,1,0:T(8,128)(2,1)S(1)} %get-tuple-element.47), channel_id=1, source_target_pairs={{0,24},{4,28},{8,16},{12,20},{16,8},{20,12},{24,0},{28,4},{1,25},{... | collective-permute-start | bytes 196616 | tf_op jit(solution)/shard_map/ppermute | solution.py:438
  39.3 0.5 %collective-permute-start.11 = (bf16[2,64,256]{2,1,0:T(8,128)(2,1)S(1)}, bf16[2,64,256]{2,1,0:T(8,128)(2,1)S(1)}, u32[]{:S(2)}, u32[]{:S(2)}) collective-permute-start(bf16[2,64,256]{2,1,0:T(8,128)(2,1)S(1)} %get-tuple-element.48), channel_id=1, source_target_pairs={{0,8},{4,12},{8,0},{12,4},{16,24},{20,28},{24,16},{28,20},{1,9},{5... | collective-permute-start | bytes 196616 | tf_op jit(solution)/shard_map/ppermute | solution.py:438
  39.8 0.1 collective-permute-start.9
  40.0 0.8 %collective-permute-done.7.refs_5_ = bf16[256,256]{1,0:T(8,128)(2,1)S(1)} collective-permute-done((bf16[256,256]{1,0:T(8,128)(2,1)S(1)}, bf16[256,256]{1,0:T(8,128)(2,1)S(1)}, u32[]{:S(2)}, u32[]{:S(2)}) %collective-permute-start.7) | collective-permute-done | bytes 131104 | tf_op jit(solution)/shard_map/ppermute | solution.py:396
  40.8 1.2 %shard_map.117 = (bf16[256,512]{1,0:T(8,128)(2,1)}, f32[256,256]{1,0:T(8,128)}, f32[256,256]{1,0:T(8,128)S(1)}) custom-call(bf16[1024,512]{1,0:T(8,128)(2,1)S(1)} %copy-done.1, bf16[256,256]{1,0:T(8,128)(2,1)S(1)} %get-tuple-element.34.refs_1_, f32[1,256]{1,0:T(1,128)S(1)} %bitcast.7, bf16[256,256]{1,0:T(8,128)(2,1)S(1)} %shard_map.116.refs_3_.refs_7_, ...), custom_call_target="tpu_custom_call" | custom-call | flops 13799999488 | tf_op jit(solution)/shard_map/pallas_call | solution.py:38
  42.0 1.6 %collective-permute-done.11.refs_4_ = bf16[2,64,256]{2,1,0:T(8,128)(2,1)S(1)} collective-permute-done((bf16[2,64,256]{2,1,0:T(8,128)(2,1)S(1)}, bf16[2,64,256]{2,1,0:T(8,128)(2,1)S(1)}, u32[]{:S(2)}, u32[]{:S(2)}) %collective-permute-start.11) | collective-permute-done | bytes 65568 | tf_op jit(solution)/shard_map/ppermute | solution.py:438
  43.5 0.6 %collective-permute-done.9.refs_2_ = bf16[2,64,256]{2,1,0:T(8,128)(2,1)S(1)} collective-permute-done((bf16[2,64,256]{2,1,0:T(8,128)(2,1)S(1)}, bf16[2,64,256]{2,1,0:T(8,128)(2,1)S(1)}, u32[]{:S(2)}, u32[]{:S(2)}) %collective-permute-start.9) | collective-permute-done | bytes 65568 | tf_op jit(solution)/shard_map/ppermute | solution.py:438
  44.1 0.8 %shard_map.120 = (f32[256,256]{1,0:T(8,128)}, f32[256,256]{1,0:T(8,128)}) custom-call(f32[256,256]{1,0:T(8,128)S(1)} %get-tuple-element.39.refs_0_, bf16[2,64,256]{2,1,0:T(8,128)(2,1)S(1)} %get-tuple-element.45.refs_1_, bf16[2,64,256]{2,1,0:T(8,128)(2,1)S(1)} %collective-permute-done.9.refs_2_, bf16[2,64,256]{2,1,0:T(8,128)(2,1)S(1)} %collective-permute-done.10.refs_3_, ...), custom_call_target="tpu_custom_call" | custom-call | flops 1150000000 | tf_op jit(solution)/shard_map/pallas_call | solution.py:38
  (26 shorter events, 0.1 us)
Async XLA Ops:
  0.6 7.2 %copy-start.1 = (bf16[1024,512]{1,0:T(8,128)(2,1)S(1)}, bf16[1024,512]{1,0:T(8,128)(2,1)}, u32[]{:S(2)}) copy-start(bf16[1024,512]{1,0:T(8,128)(2,1)} %refs_0_.7) | copy-start | bytes 3145732
  2.5 5.3 %copy-start = (bf16[8,64,256]{2,1,0:T(8,128)(2,1)S(1)}, bf16[8,64,256]{2,1,0:T(8,128)(2,1)}, u32[]{:S(2)}) copy-start(bf16[8,64,256]{2,1,0:T(8,128)(2,1)} %shard_map.111.refs_2_) | copy-start | bytes 786436
  2.5 5.3 %copy-start.2 = (bf16[256,512]{1,0:T(8,128)(2,1)S(1)}, bf16[256,512]{1,0:T(8,128)(2,1)}, u32[]{:S(2)}) copy-start(bf16[256,512]{1,0:T(8,128)(2,1)} %refs_1_.4) | copy-start | bytes 786436
  2.5 12.3 %all-to-all-start = ((bf16[8,64,256]{2,1,0:T(8,128)(2,1)}), bf16[8,64,256]{2,1,0:T(8,128)(2,1)S(1)}, u32[]{:S(2)}, u32[]{:S(2)}) async-start(bf16[8,64,256]{2,1,0:T(8,128)(2,1)} %shard_map.111.refs_2_), calls=%async_computation | async-start | bytes 524288 | tf_op jit(solution)/shard_map/all_to_all | solution.py:381
  7.9 6.9 %copy-start.5 = (bf16[512,512]{1,0:T(8,128)(2,1)S(1)}, bf16[512,512]{1,0:T(8,128)(2,1)}, u32[]{:S(2)}) copy-start(bf16[512,512]{1,0:T(8,128)(2,1)} %constant.4.clone.refs_1_.refs_5_) | copy-start | bytes 1572868
  7.9 6.9 %copy-start.6 = (f32[9,2,256]{2,1,0:T(2,128)S(1)}, f32[9,2,256]{2,1,0:T(2,128)}, u32[]{:S(2)}) copy-start(f32[9,2,256]{2,1,0:T(2,128)} %constant.5.clone.refs_2_.refs_6_) | copy-start | bytes 55300
  8.4 12.8 %collective-permute-start = (bf16[256,256]{1,0:T(8,128)(2,1)S(1)}, bf16[256,256]{1,0:T(8,128)(2,1)S(1)}, u32[]{:S(2)}, u32[]{:S(2)}) collective-permute-start(bf16[256,256]{1,0:T(8,128)(2,1)S(1)} %get-tuple-element.29), channel_id=1, source_target_pairs={{0,1},{1,2},{2,3},{3,0},{4,5},{5,6},{6,7},{7,4},{8,9},{9,10},{10,1... | collective-permute-start | bytes 393224 | tf_op jit(solution)/shard_map/ppermute | solution.py:396
  10.0 12.0 %collective-permute-start.1 = (bf16[256,256]{1,0:T(8,128)(2,1)S(1)}, bf16[256,256]{1,0:T(8,128)(2,1)S(1)}, u32[]{:S(2)}, u32[]{:S(2)}) collective-permute-start(bf16[256,256]{1,0:T(8,128)(2,1)S(1)} %get-tuple-element.30), channel_id=1, source_target_pairs={{0,2},{1,3},{2,0},{3,1},{4,6},{5,7},{6,4},{7,5},{8,10},{9,11},{10,... | collective-permute-start | bytes 393224 | tf_op jit(solution)/shard_map/ppermute | solution.py:396
  12.6 9.4 %collective-permute-start.2 = (bf16[256,256]{1,0:T(8,128)(2,1)S(1)}, bf16[256,256]{1,0:T(8,128)(2,1)S(1)}, u32[]{:S(2)}, u32[]{:S(2)}) collective-permute-start(bf16[256,256]{1,0:T(8,128)(2,1)S(1)} %get-tuple-element.31), channel_id=1, source_target_pairs={{0,3},{1,0},{2,1},{3,2},{4,7},{5,4},{6,5},{7,6},{8,11},{9,8},{10,9... | collective-permute-start | bytes 393224 | tf_op jit(solution)/shard_map/ppermute | solution.py:396
  15.7 0.7 %copy-start.7 = (bf16[288,256]{1,0:T(8,128)(2,1)}, bf16[288,256]{1,0:T(8,128)(2,1)S(1)}, u32[]{:S(2)}) copy-start(bf16[288,256]{1,0:T(8,128)(2,1)S(1)} %get-tuple-element.44.refs_4_) | copy-start | bytes 442372
  18.4 3.6 %copy-start.3 = (bf16[256,256]{1,0:T(8,128)(2,1)S(1)}, bf16[256,256]{1,0:T(8,128)(2,1)}, u32[]{:S(2)}) copy-start(bf16[256,256]{1,0:T(8,128)(2,1)} %refs_0_.6) | copy-start | bytes 393220
  18.4 8.1 %collective-permute-start.3 = (bf16[2,32,256]{2,1,0:T(8,128)(2,1)S(1)}, bf16[2,32,256]{2,1,0:T(8,128)(2,1)S(1)}, u32[]{:S(2)}, u32[]{:S(2)}) collective-permute-start(bf16[2,32,256]{2,1,0:T(8,128)(2,1)S(1)} %get-tuple-element.35), channel_id=1, source_target_pairs={{0,8},{4,12},{8,0},{12,4},{16,24},{20,28},{24,16},{28,20},{1,9},{5... | collective-permute-start | bytes 98312 | tf_op jit(solution)/shard_map/ppermute | solution.py:438
  19.6 6.8 %collective-permute-start.4 = (bf16[2,32,256]{2,1,0:T(8,128)(2,1)S(1)}, bf16[2,32,256]{2,1,0:T(8,128)(2,1)S(1)}, u32[]{:S(2)}, u32[]{:S(2)}) collective-permute-start(bf16[2,32,256]{2,1,0:T(8,128)(2,1)S(1)} %get-tuple-element.36), channel_id=1, source_target_pairs={{0,16},{4,20},{8,24},{12,28},{16,0},{20,4},{24,8},{28,12},{1,17},{... | collective-permute-start | bytes 98312 | tf_op jit(solution)/shard_map/ppermute | solution.py:438
  21.1 5.4 %collective-permute-start.5 = (bf16[2,32,256]{2,1,0:T(8,128)(2,1)S(1)}, bf16[2,32,256]{2,1,0:T(8,128)(2,1)S(1)}, u32[]{:S(2)}, u32[]{:S(2)}) collective-permute-start(bf16[2,32,256]{2,1,0:T(8,128)(2,1)S(1)} %get-tuple-element.37), channel_id=1, source_target_pairs={{0,24},{4,28},{8,16},{12,20},{16,8},{20,12},{24,0},{28,4},{1,25},{... | collective-permute-start | bytes 98312 | tf_op jit(solution)/shard_map/ppermute | solution.py:438
  22.7 10.4 %all-to-all-start.1 = ((bf16[8,32,256]{2,1,0:T(8,128)(2,1)}), bf16[8,32,256]{2,1,0:T(8,128)(2,1)S(1)}, u32[]{:S(2)}, u32[]{:S(2)}) async-start(bf16[8,32,256]{2,1,0:T(8,128)(2,1)} %bitcast.2), calls=%async_computation.1 | async-start | bytes 262144 | tf_op jit(solution)/shard_map/all_to_all | solution.py:381
  26.5 6.7 %copy-start.8 = (bf16[288,256]{1,0:T(8,128)(2,1)S(1)}, bf16[288,256]{1,0:T(8,128)(2,1)}, u32[]{:S(2)}) copy-start(bf16[288,256]{1,0:T(8,128)(2,1)} %copy-done.7) | copy-start | bytes 442372
  26.6 13.3 %collective-permute-start.6 = (bf16[256,256]{1,0:T(8,128)(2,1)S(1)}, bf16[256,256]{1,0:T(8,128)(2,1)S(1)}, u32[]{:S(2)}, u32[]{:S(2)}) collective-permute-start(bf16[256,256]{1,0:T(8,128)(2,1)S(1)} %shard_map.116.refs_3_.refs_7_), channel_id=1, source_target_pairs={{0,1},{1,2},{2,3},{3,0},{4,5},{5,6},{6,7},{7,4},{8,9},{9,10},{10,1... | collective-permute-start | bytes 393224 | tf_op jit(solution)/shard_map/ppermute | solution.py:396
  29.9 10.9 %collective-permute-start.7 = (bf16[256,256]{1,0:T(8,128)(2,1)S(1)}, bf16[256,256]{1,0:T(8,128)(2,1)S(1)}, u32[]{:S(2)}, u32[]{:S(2)}) collective-permute-start(bf16[256,256]{1,0:T(8,128)(2,1)S(1)} %shard_map.116.refs_3_.refs_7_), channel_id=1, source_target_pairs={{0,2},{1,3},{2,0},{3,1},{4,6},{5,7},{6,4},{7,5},{8,10},{9,11},{10,... | collective-permute-start | bytes 393224 | tf_op jit(solution)/shard_map/ppermute | solution.py:396
  31.5 9.3 %collective-permute-start.8 = (bf16[256,256]{1,0:T(8,128)(2,1)S(1)}, bf16[256,256]{1,0:T(8,128)(2,1)S(1)}, u32[]{:S(2)}, u32[]{:S(2)}) collective-permute-start(bf16[256,256]{1,0:T(8,128)(2,1)S(1)} %shard_map.116.refs_3_.refs_7_), channel_id=1, source_target_pairs={{0,3},{1,0},{2,1},{3,2},{4,7},{5,4},{6,5},{7,6},{8,11},{9,8},{10,9... | collective-permute-start | bytes 393224 | tf_op jit(solution)/shard_map/ppermute | solution.py:396
  36.4 5.6 %collective-permute-start.10 = (bf16[2,64,256]{2,1,0:T(8,128)(2,1)S(1)}, bf16[2,64,256]{2,1,0:T(8,128)(2,1)S(1)}, u32[]{:S(2)}, u32[]{:S(2)}) collective-permute-start(bf16[2,64,256]{2,1,0:T(8,128)(2,1)S(1)} %get-tuple-element.47), channel_id=1, source_target_pairs={{0,24},{4,28},{8,16},{12,20},{16,8},{20,12},{24,0},{28,4},{1,25},{... | collective-permute-start | bytes 196616 | tf_op jit(solution)/shard_map/ppermute | solution.py:438
  39.3 4.3 %collective-permute-start.11 = (bf16[2,64,256]{2,1,0:T(8,128)(2,1)S(1)}, bf16[2,64,256]{2,1,0:T(8,128)(2,1)S(1)}, u32[]{:S(2)}, u32[]{:S(2)}) collective-permute-start(bf16[2,64,256]{2,1,0:T(8,128)(2,1)S(1)} %get-tuple-element.48), channel_id=1, source_target_pairs={{0,8},{4,12},{8,0},{12,4},{16,24},{20,28},{24,16},{28,20},{1,9},{5... | collective-permute-start | bytes 196616 | tf_op jit(solution)/shard_map/ppermute | solution.py:438
  39.8 1.0 %copy-start.4 = (f32[256]{0:T(256)S(1)}, f32[256]{0:T(256)}, u32[]{:S(2)}) copy-start(f32[256]{0:T(256)} %param.11) | copy-start | bytes 3076
  39.8 4.3 %collective-permute-start.9 = (bf16[2,64,256]{2,1,0:T(8,128)(2,1)S(1)}, bf16[2,64,256]{2,1,0:T(8,128)(2,1)S(1)}, u32[]{:S(2)}, u32[]{:S(2)}) collective-permute-start(bf16[2,64,256]{2,1,0:T(8,128)(2,1)S(1)} %get-tuple-element.46), channel_id=1, source_target_pairs={{0,16},{4,20},{8,24},{12,28},{16,0},{20,4},{24,8},{28,12},{1,17},{... | collective-permute-start | bytes 196616 | tf_op jit(solution)/shard_map/ppermute | solution.py:438

commit v5 on v4

--- a/solution.py
+++ b/solution.py
@@ -283,12 +283,19 @@
         pair_ref[shard, owned:] = filters[rows]
 
 
-def spread_kernel(weight_ref, grad_ref, *out_refs):
+def look_up(table, index):
+    value = jnp.int32(table[0])
+    for at in range(1, len(table)):
+        value = jnp.where(index == at, jnp.int32(table[at]), value)
+    return value
+
+
+def spread_kernel(routes, weight_ref, grad_ref, *out_refs):
     count = len(out_refs)
     rows = weight_ref.shape[0] // count
     me = lax.axis_index("chan")
     for step in list(range(1, count)) + [0]:
-        place = lax.rem(me + step, count)
+        place = look_up(routes[step], me)
         block = weight_ref[pl.ds(pl.multiple_of(place * rows, rows), rows), :]
         out_refs[step][...] = lax.dot_general(
             block, grad_ref[...], (((1,), (1,)), ((), ())), preferred_element_type=f32
@@ -328,7 +335,8 @@
         refs[-1][rows] = (gating_ref[rows].astype(f32) * mixed).astype(bf16)
 
 
-def project_kernel(count, weight_ref, total_ref, decay_ref, *refs):
+def project_kernel(routes, weight_ref, total_ref, decay_ref, *refs):
+    count = len(routes)
     gated_refs, pieces = refs[:count], refs[count:-3]
     out_ref, gating_grad_ref, window_ref = refs[-3:]
     window_ref[...] = window_of(decay_ref, total_ref.shape[1])
@@ -338,7 +346,7 @@
     me = lax.axis_index("chan")
     total = None
     for step in range(count):
-        place = lax.rem(me + count - step, count)
+        place = look_up([list(routes[step]).index(at) for at in range(count)], me)
         block = weight_ref[pl.ds(pl.multiple_of(place * rows, rows), rows), :]
         term = lax.dot_general(
             gated_refs[step][...], block, (((0,), (0,)), ((), ())), preferred_element_type=f32
@@ -392,8 +400,11 @@
     twiddle = jnp.asarray(twiddle_table(shards, length))
     shape = jax.ShapeDtypeStruct
 
-    def shift(array, step):
-        return lax.ppermute(array, "chan", [(i, (i + step) % parts) for i in range(parts)])
+    routes_2 = [[(i + step) % parts for i in range(parts)] for step in range(parts)]
+    routes_1 = [range(4), [3, 2, 1, 0], [1, 3, 0, 2], [2, 0, 3, 1]] if parts == 4 else routes_2
+
+    def shift(array, route):
+        return lax.ppermute(array, "chan", list(enumerate(route)))
 
     rates = decay_rates.reshape(1, channels)
     if owned == held:
@@ -414,12 +425,12 @@
     arrived = exchange(pairs)
 
     partial = call(
-        spread_kernel,
+        functools.partial(spread_kernel, routes_1),
         tuple(shape((channels, length), bf16) for k in range(parts)),
         [VMEM] * 2,
         after=(pairs,),
     )(out_weight, out_grad)
-    shares = [shift(partial[step], step) for step in range(1, parts)]
+    shares = [shift(partial[step], routes_1[step]) for step in range(1, parts)]
 
     mixed_owned, *spectra = call(
         convolve_kernel,
@@ -460,9 +471,9 @@
     gated = call(gate_kernel, shape((channels, length), bf16), [VMEM] * (1 + len(pieces)))(
         gating, *pieces
     )
-    gathered = [gated] + [shift(gated, step) for step in range(1, parts)]
+    gathered = [gated] + [shift(gated, routes_2[step]) for step in range(1, parts)]
     mixed_out, gating_grad, window = call(
-        functools.partial(project_kernel, parts),
+        functools.partial(project_kernel, routes_2),
         (
             shape((length, out_weight.shape[1]), bf16),
             shape((channels, length), f32),

time: 45.3 us -> 44.8 us (0.989)
  starting transfers between devices: 28.3 us -> 26.8 us
  waiting for transfers between devices: 3.83 us -> 4.89 us
    ppermute x6, starting transfers between devices: 12.1 us -> 10.5 us  [shift(): return lax.ppermute(array, 'chan', list(enumerate(route)))]
    ppermute x6, waiting for transfers between devices: 0.86 us -> 2.34 us  [shift(): return lax.ppermute(array, 'chan', list(enumerate(route)))]
    ppermute x6, waiting for transfers between devices: 2.12 us -> 0.99 us  [hop(): lax.ppermute(array, 'seq', [(i, i ^ distance) for i in range(shards)])]
    all_to_all x2, waiting for transfers between devices: 0.85 us -> 1.56 us  [exchange(): return lax.all_to_all(array, 'seq', split_axis=0, concat_axis=0, tiled=True)]
  transfers between devices with their start and end apart: 14 -> 14, of which waited for: 4 -> 5; matrix products, arithmetic and copies ran while one was open for 0% -> 0% of each run, Pallas kernels for 10% -> 10%
where the time goes in v5:
time: 44.8 us; the launch traced here: 44.5 us
  starting transfers between devices  26.8 us (60%)
  Pallas kernels  7.15 us (16%)
  waiting for transfers between devices  4.89 us (11%)
  blocking collectives  4.16 us (9%)
  between operations  0.8 us (2%)
  local copies, waits for them, and re-layouts  0.7 us (2%)
    ppermute x6, starting transfers between devices, shift(): return lax.ppermute(array, 'chan', list(enumerate(route)))  10.5 us
    all_to_all x2, starting transfers between devices, exchange(): return lax.all_to_all(array, 'seq', split_axis=0, concat_axis=0, tiled=True)  9.15 us
    ppermute x6, starting transfers between devices, hop(): lax.ppermute(array, 'seq', [(i, i ^ distance) for i in range(shards)])  7.18 us
    pallas_call x10, Pallas kernels, call(): return lambda *operands: run(*operands, *after)  7.15 us
    all_gather x2, blocking collectives, bring(): both = lax.all_gather(array, 'seq', axis_index_groups=pairs)  4.16 us
    ppermute x6, waiting for transfers between devices, shift(): return lax.ppermute(array, 'chan', list(enumerate(route)))  2.34 us
    all_to_all x2, waiting for transfers between devices, exchange(): return lax.all_to_all(array, 'seq', split_axis=0, concat_axis=0, tiled=True)  1.56 us
    ppermute x6, waiting for transfers between devices, hop(): lax.ppermute(array, 'seq', [(i, i ^ distance) for i in range(shards)])  0.99 us
  transfers between devices with their start and end apart: 14, of which 5 were waited for; matrix products, arithmetic and copies ran while one was open for 0% of the time, Pallas kernels for 10%

profile of v5, /device:TPU:0, one launch (start us, length us, event | category | flops | bytes accessed | tf_op | source)
XLA Modules:
  0.0 44.5 jit_solution(3333378416029692032)
XLA Ops:
  0.6 1.8 %shard_map.111.refs_2_ = bf16[8,64,256]{2,1,0:T(8,128)(2,1)} custom-call(f32[1,256]{1,0:T(1,128)} %bitcast.6, f32[256,256]{1,0:T(8,128)} %refs_1_.3, bf16[256,256]{1,0:T(8,128)(2,1)} %refs_2_.2), custom_call_target="tpu_custom_call" | custom-call | flops 1150000000 | tf_op jit(solution)/shard_map/pallas_call | solution.py:38
  2.5 0.0 copy-start.2
  2.5 5.3 %all-to-all-start = ((bf16[8,64,256]{2,1,0:T(8,128)(2,1)}), bf16[8,64,256]{2,1,0:T(8,128)(2,1)S(1)}, u32[]{:S(2)}, u32[]{:S(2)}) async-start(bf16[8,64,256]{2,1,0:T(8,128)(2,1)} %shard_map.111.refs_2_), calls=%async_computation | async-start | bytes 524288 | tf_op jit(solution)/shard_map/all_to_all | solution.py:389
  7.9 0.0 copy-start.5
  7.9 0.0 copy-start.6
  7.9 0.5 %shard_map.112 = (bf16[256,256]{1,0:T(8,128)(2,1)S(1)}, bf16[256,256]{1,0:T(8,128)(2,1)S(1)}, bf16[256,256]{1,0:T(8,128)(2,1)S(1)}, bf16[256,256]{1,0:T(8,128)(2,1)S(1)}) custom-call(bf16[1024,512]{1,0:T(8,128)(2,1)S(1)} %copy-done.1, bf16[256,512]{1,0:T(8,128)(2,1)S(1)} %copy-done.2, bf16[8,64,256]{2,1,0:T(8,128)(2,1)S(1)} %copy-done), custom_call_target="tpu_custom_call" | custom-call | flops 1150000000 | tf_op jit(solution)/shard_map/pallas_call | solution.py:38
  8.4 3.7 %collective-permute-start = (bf16[256,256]{1,0:T(8,128)(2,1)S(1)}, bf16[256,256]{1,0:T(8,128)(2,1)S(1)}, u32[]{:S(2)}, u32[]{:S(2)}) collective-permute-start(bf16[256,256]{1,0:T(8,128)(2,1)S(1)} %get-tuple-element.29), channel_id=1, source_target_pairs={{0,3},{1,2},{2,1},{3,0},{4,7},{5,6},{6,5},{7,4},{8,11},{9,10},{10,... | collective-permute-start | bytes 393224 | tf_op jit(solution)/shard_map/ppermute | solution.py:407
  12.0 2.9 %collective-permute-start.2 = (bf16[256,256]{1,0:T(8,128)(2,1)S(1)}, bf16[256,256]{1,0:T(8,128)(2,1)S(1)}, u32[]{:S(2)}, u32[]{:S(2)}) collective-permute-start(bf16[256,256]{1,0:T(8,128)(2,1)S(1)} %get-tuple-element.31), channel_id=1, source_target_pairs={{0,2},{1,0},{2,3},{3,1},{4,6},{5,4},{6,7},{7,5},{8,10},{9,8},{10,1... | collective-permute-start | bytes 393224 | tf_op jit(solution)/shard_map/ppermute | solution.py:407
  15.0 1.0 %shard_map.113 = (bf16[8,32,256]{2,1,0:T(8,128)(2,1)S(1)}, bf16[288,256]{1,0:T(8,128)(2,1)S(1)}, bf16[288,256]{1,0:T(8,128)(2,1)S(1)}, bf16[288,256]{1,0:T(8,128)(2,1)S(1)}, bf16[288,256]{1,0:T(8,128)(2,1)S(1)}) custom-call(bf16[8,64,256]{2,1,0:T(8,128)(2,1)S(1)} %all-to-all-done.refs_0_, bf16[512,512]{1,0:T(8,128)(2,1)S(1)} %copy-done.5, ...), custom_call_target="tpu_custom_call" | custom-call | flops 2300000000 | tf_op jit(solution)/shard_map/pallas_call | solution.py:38
  15.9 0.7 %copy-done.7 = bf16[288,256]{1,0:T(8,128)(2,1)} copy-done((bf16[288,256]{1,0:T(8,128)(2,1)}, bf16[288,256]{1,0:T(8,128)(2,1)S(1)}, u32[]{:S(2)}) %copy-start.7) | copy-done | bytes 147480
  16.6 2.0 %all-gather = bf16[16,32,256]{2,1,0:T(8,128)(2,1)S(1)} all-gather(bf16[8,32,256]{2,1,0:T(8,128)(2,1)S(1)} %get-tuple-element.32), channel_id=2, replica_groups={{0,4},{8,12},{16,20},{24,28},{1,5},{9,13},{17,21},{25,29},{2,6},{10,14}..., dimensions={0}, use_global_device_ids=true | all-gather | bytes 393216 | tf_op jit(solution)/shard_map/all_gather | solution.py:455
  18.6 2.1 %collective-permute-start.3 = (bf16[2,32,256]{2,1,0:T(8,128)(2,1)S(1)}, bf16[2,32,256]{2,1,0:T(8,128)(2,1)S(1)}, u32[]{:S(2)}, u32[]{:S(2)}) collective-permute-start(bf16[2,32,256]{2,1,0:T(8,128)(2,1)S(1)} %get-tuple-element.35), channel_id=1, source_target_pairs={{0,8},{4,12},{8,0},{12,4},{16,24},{20,28},{24,16},{28,20},{1,9},{5... | collective-permute-start | bytes 98312 | tf_op jit(solution)/shard_map/ppermute | solution.py:449
  20.7 1.5 %collective-permute-start.4 = (bf16[2,32,256]{2,1,0:T(8,128)(2,1)S(1)}, bf16[2,32,256]{2,1,0:T(8,128)(2,1)S(1)}, u32[]{:S(2)}, u32[]{:S(2)}) collective-permute-start(bf16[2,32,256]{2,1,0:T(8,128)(2,1)S(1)} %get-tuple-element.36), channel_id=1, source_target_pairs={{0,16},{4,20},{8,24},{12,28},{16,0},{20,4},{24,8},{28,12},{1,17},{... | collective-permute-start | bytes 98312 | tf_op jit(solution)/shard_map/ppermute | solution.py:449
  22.1 0.1 collective-permute-start.5
  22.2 1.6 %collective-permute-done.1.refs_3_ = bf16[256,256]{1,0:T(8,128)(2,1)S(1)} collective-permute-done((bf16[256,256]{1,0:T(8,128)(2,1)S(1)}, bf16[256,256]{1,0:T(8,128)(2,1)S(1)}, u32[]{:S(2)}, u32[]{:S(2)}) %collective-permute-start.1) | collective-permute-done | bytes 131104 | tf_op jit(solution)/shard_map/ppermute | solution.py:407
  23.8 0.7 %shard_map.115 = (bf16[256,256]{1,0:T(8,128)(2,1)S(1)}, bf16[256,256]{1,0:T(8,128)(2,1)}) custom-call(bf16[256,256]{1,0:T(8,128)(2,1)S(1)} %copy-done.3, bf16[256,256]{1,0:T(8,128)(2,1)S(1)} %get-tuple-element.28.refs_1_, bf16[256,256]{1,0:T(8,128)(2,1)S(1)} %collective-permute-done.refs_2_, bf16[256,256]{1,0:T(8,128)(2,1)S(1)} %collective-permute-done.1.refs_3_, ...), custom_call_target="tpu_custom_call" | custom-call | flops 1150000000 | tf_op jit(solution)/shard_map/pallas_call | solution.py:38
  24.5 3.8 %all-to-all-start.1 = ((bf16[8,32,256]{2,1,0:T(8,128)(2,1)}), bf16[8,32,256]{2,1,0:T(8,128)(2,1)S(1)}, u32[]{:S(2)}, u32[]{:S(2)}) async-start(bf16[8,32,256]{2,1,0:T(8,128)(2,1)} %bitcast.2), calls=%async_computation.1 | async-start | bytes 262144 | tf_op jit(solution)/shard_map/all_to_all | solution.py:389
  28.4 0.1 shard_map.116.refs_3_.refs_7_
  28.4 0.1 collective-permute-start.6
  28.5 3.1 %collective-permute-start.7 = (bf16[256,256]{1,0:T(8,128)(2,1)S(1)}, bf16[256,256]{1,0:T(8,128)(2,1)S(1)}, u32[]{:S(2)}, u32[]{:S(2)}) collective-permute-start(bf16[256,256]{1,0:T(8,128)(2,1)S(1)} %shard_map.116.refs_3_.refs_7_), channel_id=1, source_target_pairs={{0,2},{1,3},{2,0},{3,1},{4,6},{5,7},{6,4},{7,5},{8,10},{9,11},{10,... | collective-permute-start | bytes 393224 | tf_op jit(solution)/shard_map/ppermute | solution.py:407
  31.6 0.8 %collective-permute-start.8 = (bf16[256,256]{1,0:T(8,128)(2,1)S(1)}, bf16[256,256]{1,0:T(8,128)(2,1)S(1)}, u32[]{:S(2)}, u32[]{:S(2)}) collective-permute-start(bf16[256,256]{1,0:T(8,128)(2,1)S(1)} %shard_map.116.refs_3_.refs_7_), channel_id=1, source_target_pairs={{0,3},{1,0},{2,1},{3,2},{4,7},{5,4},{6,5},{7,6},{8,11},{9,8},{10,9... | collective-permute-start | bytes 393224 | tf_op jit(solution)/shard_map/ppermute | solution.py:407
  32.3 1.6 %all-to-all-done.1.refs_0_ = bf16[8,32,256]{2,1,0:T(8,128)(2,1)S(1)} async-done(((bf16[8,32,256]{2,1,0:T(8,128)(2,1)}), bf16[8,32,256]{2,1,0:T(8,128)(2,1)S(1)}, u32[]{:S(2)}, u32[]{:S(2)}) %all-to-all-start.1) | async-done | bytes 131104 | tf_op jit(solution)/shard_map/all_to_all | solution.py:389
  33.9 1.1 %shard_map.118 = bf16[8,64,256]{2,1,0:T(8,128)(2,1)S(1)} custom-call(bf16[8,32,256]{2,1,0:T(8,128)(2,1)S(1)} %all-to-all-done.1.refs_0_, bf16[288,256]{1,0:T(8,128)(2,1)S(1)} %get-tuple-element.41.refs_1_, bf16[288,256]{1,0:T(8,128)(2,1)S(1)} %get-tuple-element.42.refs_2_, bf16[288,256]{1,0:T(8,128)(2,1)S(1)} %get-tuple-element.43.refs_3_, ...), custom_call_target="tpu_custom_call" | custom-call | flops 2300000000 | tf_op jit(solution)/shard_map/pallas_call | solution.py:38
  35.0 2.2 %all-gather.1 = bf16[16,64,256]{2,1,0:T(8,128)(2,1)S(1)} all-gather(bf16[8,64,256]{2,1,0:T(8,128)(2,1)S(1)} %shard_map.118), channel_id=3, replica_groups={{0,4},{8,12},{16,20},{24,28},{1,5},{9,13},{17,21},{25,29},{2,6},{10,14}..., dimensions={0}, use_global_device_ids=true | all-gather | bytes 786432 | tf_op jit(solution)/shard_map/all_gather | solution.py:455
  37.2 1.4 %collective-permute-start.10 = (bf16[2,64,256]{2,1,0:T(8,128)(2,1)S(1)}, bf16[2,64,256]{2,1,0:T(8,128)(2,1)S(1)}, u32[]{:S(2)}, u32[]{:S(2)}) collective-permute-start(bf16[2,64,256]{2,1,0:T(8,128)(2,1)S(1)} %get-tuple-element.47), channel_id=1, source_target_pairs={{0,24},{4,28},{8,16},{12,20},{16,8},{20,12},{24,0},{28,4},{1,25},{... | collective-permute-start | bytes 196616 | tf_op jit(solution)/shard_map/ppermute | solution.py:449
  38.6 0.7 %collective-permute-start.11 = (bf16[2,64,256]{2,1,0:T(8,128)(2,1)S(1)}, bf16[2,64,256]{2,1,0:T(8,128)(2,1)S(1)}, u32[]{:S(2)}, u32[]{:S(2)}) collective-permute-start(bf16[2,64,256]{2,1,0:T(8,128)(2,1)S(1)} %get-tuple-element.48), channel_id=1, source_target_pairs={{0,8},{4,12},{8,0},{12,4},{16,24},{20,28},{24,16},{28,20},{1,9},{5... | collective-permute-start | bytes 196616 | tf_op jit(solution)/shard_map/ppermute | solution.py:449
  39.3 1.5 %collective-permute-start.9 = (bf16[2,64,256]{2,1,0:T(8,128)(2,1)S(1)}, bf16[2,64,256]{2,1,0:T(8,128)(2,1)S(1)}, u32[]{:S(2)}, u32[]{:S(2)}) collective-permute-start(bf16[2,64,256]{2,1,0:T(8,128)(2,1)S(1)} %get-tuple-element.46), channel_id=1, source_target_pairs={{0,16},{4,20},{8,24},{12,28},{16,0},{20,4},{24,8},{28,12},{1,17},{... | collective-permute-start | bytes 196616 | tf_op jit(solution)/shard_map/ppermute | solution.py:449
  40.7 0.8 %collective-permute-done.7.refs_5_ = bf16[256,256]{1,0:T(8,128)(2,1)S(1)} collective-permute-done((bf16[256,256]{1,0:T(8,128)(2,1)S(1)}, bf16[256,256]{1,0:T(8,128)(2,1)S(1)}, u32[]{:S(2)}, u32[]{:S(2)}) %collective-permute-start.7) | collective-permute-done | bytes 131104 | tf_op jit(solution)/shard_map/ppermute | solution.py:407
  41.5 1.2 %shard_map.117 = (bf16[256,512]{1,0:T(8,128)(2,1)}, f32[256,256]{1,0:T(8,128)}, f32[256,256]{1,0:T(8,128)S(1)}) custom-call(bf16[1024,512]{1,0:T(8,128)(2,1)S(1)} %copy-done.1, bf16[256,256]{1,0:T(8,128)(2,1)S(1)} %get-tuple-element.34.refs_1_, f32[1,256]{1,0:T(1,128)S(1)} %bitcast.7, bf16[256,256]{1,0:T(8,128)(2,1)S(1)} %shard_map.116.refs_3_.refs_7_, ...), custom_call_target="tpu_custom_call" | custom-call | flops 13799999488 | tf_op jit(solution)/shard_map/pallas_call | solution.py:38
  42.7 0.3 collective-permute-done.10.refs_3_
  43.0 0.7 %collective-permute-done.9.refs_2_ = bf16[2,64,256]{2,1,0:T(8,128)(2,1)S(1)} collective-permute-done((bf16[2,64,256]{2,1,0:T(8,128)(2,1)S(1)}, bf16[2,64,256]{2,1,0:T(8,128)(2,1)S(1)}, u32[]{:S(2)}, u32[]{:S(2)}) %collective-permute-start.9) | collective-permute-done | bytes 65568 | tf_op jit(solution)/shard_map/ppermute | solution.py:449
  43.7 0.8 %shard_map.120 = (f32[256,256]{1,0:T(8,128)}, f32[256,256]{1,0:T(8,128)}) custom-call(f32[256,256]{1,0:T(8,128)S(1)} %get-tuple-element.39.refs_0_, bf16[2,64,256]{2,1,0:T(8,128)(2,1)S(1)} %get-tuple-element.45.refs_1_, bf16[2,64,256]{2,1,0:T(8,128)(2,1)S(1)} %collective-permute-done.9.refs_2_, bf16[2,64,256]{2,1,0:T(8,128)(2,1)S(1)} %collective-permute-done.10.refs_3_, ...), custom_call_target="tpu_custom_call" | custom-call | flops 1150000000 | tf_op jit(solution)/shard_map/pallas_call | solution.py:38
  (26 shorter events, 0.1 us)
Async XLA Ops:
  0.6 7.2 %copy-start.1 = (bf16[1024,512]{1,0:T(8,128)(2,1)S(1)}, bf16[1024,512]{1,0:T(8,128)(2,1)}, u32[]{:S(2)}) copy-start(bf16[1024,512]{1,0:T(8,128)(2,1)} %refs_0_.7) | copy-start | bytes 3145732
  2.5 5.3 %copy-start = (bf16[8,64,256]{2,1,0:T(8,128)(2,1)S(1)}, bf16[8,64,256]{2,1,0:T(8,128)(2,1)}, u32[]{:S(2)}) copy-start(bf16[8,64,256]{2,1,0:T(8,128)(2,1)} %shard_map.111.refs_2_) | copy-start | bytes 786436
  2.5 5.3 %copy-start.2 = (bf16[256,512]{1,0:T(8,128)(2,1)S(1)}, bf16[256,512]{1,0:T(8,128)(2,1)}, u32[]{:S(2)}) copy-start(bf16[256,512]{1,0:T(8,128)(2,1)} %refs_1_.4) | copy-start | bytes 786436
  2.5 12.4 %all-to-all-start = ((bf16[8,64,256]{2,1,0:T(8,128)(2,1)}), bf16[8,64,256]{2,1,0:T(8,128)(2,1)S(1)}, u32[]{:S(2)}, u32[]{:S(2)}) async-start(bf16[8,64,256]{2,1,0:T(8,128)(2,1)} %shard_map.111.refs_2_), calls=%async_computation | async-start | bytes 524288 | tf_op jit(solution)/shard_map/all_to_all | solution.py:389
  7.9 7.1 %copy-start.5 = (bf16[512,512]{1,0:T(8,128)(2,1)S(1)}, bf16[512,512]{1,0:T(8,128)(2,1)}, u32[]{:S(2)}) copy-start(bf16[512,512]{1,0:T(8,128)(2,1)} %constant.4.clone.refs_1_.refs_5_) | copy-start | bytes 1572868
  7.9 7.1 %copy-start.6 = (f32[9,2,256]{2,1,0:T(2,128)S(1)}, f32[9,2,256]{2,1,0:T(2,128)}, u32[]{:S(2)}) copy-start(f32[9,2,256]{2,1,0:T(2,128)} %constant.5.clone.refs_2_.refs_6_) | copy-start | bytes 55300
  8.4 13.8 %collective-permute-start = (bf16[256,256]{1,0:T(8,128)(2,1)S(1)}, bf16[256,256]{1,0:T(8,128)(2,1)S(1)}, u32[]{:S(2)}, u32[]{:S(2)}) collective-permute-start(bf16[256,256]{1,0:T(8,128)(2,1)S(1)} %get-tuple-element.29), channel_id=1, source_target_pairs={{0,3},{1,2},{2,1},{3,0},{4,7},{5,6},{6,5},{7,4},{8,11},{9,10},{10,... | collective-permute-start | bytes 393224 | tf_op jit(solution)/shard_map/ppermute | solution.py:407
  12.0 11.7 %collective-permute-start.1 = (bf16[256,256]{1,0:T(8,128)(2,1)S(1)}, bf16[256,256]{1,0:T(8,128)(2,1)S(1)}, u32[]{:S(2)}, u32[]{:S(2)}) collective-permute-start(bf16[256,256]{1,0:T(8,128)(2,1)S(1)} %get-tuple-element.30), channel_id=1, source_target_pairs={{0,1},{1,3},{2,0},{3,2},{4,5},{5,7},{6,4},{7,6},{8,9},{9,11},{10,8... | collective-permute-start | bytes 393224 | tf_op jit(solution)/shard_map/ppermute | solution.py:407
  12.0 11.7 %collective-permute-start.2 = (bf16[256,256]{1,0:T(8,128)(2,1)S(1)}, bf16[256,256]{1,0:T(8,128)(2,1)S(1)}, u32[]{:S(2)}, u32[]{:S(2)}) collective-permute-start(bf16[256,256]{1,0:T(8,128)(2,1)S(1)} %get-tuple-element.31), channel_id=1, source_target_pairs={{0,2},{1,0},{2,3},{3,1},{4,6},{5,4},{6,7},{7,5},{8,10},{9,8},{10,1... | collective-permute-start | bytes 393224 | tf_op jit(solution)/shard_map/ppermute | solution.py:407
  15.9 0.7 %copy-start.7 = (bf16[288,256]{1,0:T(8,128)(2,1)}, bf16[288,256]{1,0:T(8,128)(2,1)S(1)}, u32[]{:S(2)}) copy-start(bf16[288,256]{1,0:T(8,128)(2,1)S(1)} %get-tuple-element.44.refs_4_) | copy-start | bytes 442372
  18.6 5.2 %copy-start.3 = (bf16[256,256]{1,0:T(8,128)(2,1)S(1)}, bf16[256,256]{1,0:T(8,128)(2,1)}, u32[]{:S(2)}) copy-start(bf16[256,256]{1,0:T(8,128)(2,1)} %refs_0_.6) | copy-start | bytes 393220
  18.6 9.8 %collective-permute-start.3 = (bf16[2,32,256]{2,1,0:T(8,128)(2,1)S(1)}, bf16[2,32,256]{2,1,0:T(8,128)(2,1)S(1)}, u32[]{:S(2)}, u32[]{:S(2)}) collective-permute-start(bf16[2,32,256]{2,1,0:T(8,128)(2,1)S(1)} %get-tuple-element.35), channel_id=1, source_target_pairs={{0,8},{4,12},{8,0},{12,4},{16,24},{20,28},{24,16},{28,20},{1,9},{5... | collective-permute-start | bytes 98312 | tf_op jit(solution)/shard_map/ppermute | solution.py:449
  20.7 7.7 %collective-permute-start.4 = (bf16[2,32,256]{2,1,0:T(8,128)(2,1)S(1)}, bf16[2,32,256]{2,1,0:T(8,128)(2,1)S(1)}, u32[]{:S(2)}, u32[]{:S(2)}) collective-permute-start(bf16[2,32,256]{2,1,0:T(8,128)(2,1)S(1)} %get-tuple-element.36), channel_id=1, source_target_pairs={{0,16},{4,20},{8,24},{12,28},{16,0},{20,4},{24,8},{28,12},{1,17},{... | collective-permute-start | bytes 98312 | tf_op jit(solution)/shard_map/ppermute | solution.py:449
  22.1 6.2 %collective-permute-start.5 = (bf16[2,32,256]{2,1,0:T(8,128)(2,1)S(1)}, bf16[2,32,256]{2,1,0:T(8,128)(2,1)S(1)}, u32[]{:S(2)}, u32[]{:S(2)}) collective-permute-start(bf16[2,32,256]{2,1,0:T(8,128)(2,1)S(1)} %get-tuple-element.37), channel_id=1, source_target_pairs={{0,24},{4,28},{8,16},{12,20},{16,8},{20,12},{24,0},{28,4},{1,25},{... | collective-permute-start | bytes 98312 | tf_op jit(solution)/shard_map/ppermute | solution.py:449
  24.5 9.4 %all-to-all-start.1 = ((bf16[8,32,256]{2,1,0:T(8,128)(2,1)}), bf16[8,32,256]{2,1,0:T(8,128)(2,1)S(1)}, u32[]{:S(2)}, u32[]{:S(2)}) async-start(bf16[8,32,256]{2,1,0:T(8,128)(2,1)} %bitcast.2), calls=%async_computation.1 | async-start | bytes 262144 | tf_op jit(solution)/shard_map/all_to_all | solution.py:389
  28.4 5.5 %copy-start.8 = (bf16[288,256]{1,0:T(8,128)(2,1)S(1)}, bf16[288,256]{1,0:T(8,128)(2,1)}, u32[]{:S(2)}) copy-start(bf16[288,256]{1,0:T(8,128)(2,1)} %copy-done.7) | copy-start | bytes 442372
  28.4 10.8 %collective-permute-start.6 = (bf16[256,256]{1,0:T(8,128)(2,1)S(1)}, bf16[256,256]{1,0:T(8,128)(2,1)S(1)}, u32[]{:S(2)}, u32[]{:S(2)}) collective-permute-start(bf16[256,256]{1,0:T(8,128)(2,1)S(1)} %shard_map.116.refs_3_.refs_7_), channel_id=1, source_target_pairs={{0,1},{1,2},{2,3},{3,0},{4,5},{5,6},{6,7},{7,4},{8,9},{9,10},{10,1... | collective-permute-start | bytes 393224 | tf_op jit(solution)/shard_map/ppermute | solution.py:407
  28.5 13.0 %collective-permute-start.7 = (bf16[256,256]{1,0:T(8,128)(2,1)S(1)}, bf16[256,256]{1,0:T(8,128)(2,1)S(1)}, u32[]{:S(2)}, u32[]{:S(2)}) collective-permute-start(bf16[256,256]{1,0:T(8,128)(2,1)S(1)} %shard_map.116.refs_3_.refs_7_), channel_id=1, source_target_pairs={{0,2},{1,3},{2,0},{3,1},{4,6},{5,7},{6,4},{7,5},{8,10},{9,11},{10,... | collective-permute-start | bytes 393224 | tf_op jit(solution)/shard_map/ppermute | solution.py:407
  31.6 9.9 %collective-permute-start.8 = (bf16[256,256]{1,0:T(8,128)(2,1)S(1)}, bf16[256,256]{1,0:T(8,128)(2,1)S(1)}, u32[]{:S(2)}, u32[]{:S(2)}) collective-permute-start(bf16[256,256]{1,0:T(8,128)(2,1)S(1)} %shard_map.116.refs_3_.refs_7_), channel_id=1, source_target_pairs={{0,3},{1,0},{2,1},{3,2},{4,7},{5,4},{6,5},{7,6},{8,11},{9,8},{10,9... | collective-permute-start | bytes 393224 | tf_op jit(solution)/shard_map/ppermute | solution.py:407
  37.2 5.8 %collective-permute-start.10 = (bf16[2,64,256]{2,1,0:T(8,128)(2,1)S(1)}, bf16[2,64,256]{2,1,0:T(8,128)(2,1)S(1)}, u32[]{:S(2)}, u32[]{:S(2)}) collective-permute-start(bf16[2,64,256]{2,1,0:T(8,128)(2,1)S(1)} %get-tuple-element.47), channel_id=1, source_target_pairs={{0,24},{4,28},{8,16},{12,20},{16,8},{20,12},{24,0},{28,4},{1,25},{... | collective-permute-start | bytes 196616 | tf_op jit(solution)/shard_map/ppermute | solution.py:449
  38.6 4.4 %collective-permute-start.11 = (bf16[2,64,256]{2,1,0:T(8,128)(2,1)S(1)}, bf16[2,64,256]{2,1,0:T(8,128)(2,1)S(1)}, u32[]{:S(2)}, u32[]{:S(2)}) collective-permute-start(bf16[2,64,256]{2,1,0:T(8,128)(2,1)S(1)} %get-tuple-element.48), channel_id=1, source_target_pairs={{0,8},{4,12},{8,0},{12,4},{16,24},{20,28},{24,16},{28,20},{1,9},{5... | collective-permute-start | bytes 196616 | tf_op jit(solution)/shard_map/ppermute | solution.py:449
  39.3 2.2 %copy-start.4 = (f32[256]{0:T(256)S(1)}, f32[256]{0:T(256)}, u32[]{:S(2)}) copy-start(f32[256]{0:T(256)} %param.11) | copy-start | bytes 3076
  39.3 4.4 %collective-permute-start.9 = (bf16[2,64,256]{2,1,0:T(8,128)(2,1)S(1)}, bf16[2,64,256]{2,1,0:T(8,128)(2,1)S(1)}, u32[]{:S(2)}, u32[]{:S(2)}) collective-permute-start(bf16[2,64,256]{2,1,0:T(8,128)(2,1)S(1)} %get-tuple-element.46), channel_id=1, source_target_pairs={{0,16},{4,20},{8,24},{12,28},{16,0},{20,4},{24,8},{28,12},{1,17},{... | collective-permute-start | bytes 196616 | tf_op jit(solution)/shard_map/ppermute | solution.py:449

commit v6 on v5

--- a/solution.py
+++ b/solution.py
@@ -290,16 +290,16 @@
     return value
 
 
-def spread_kernel(routes, weight_ref, grad_ref, *out_refs):
-    count = len(out_refs)
+def spread_kernel(routes, steps, weight_ref, grad_ref, *out_refs):
+    count = len(routes)
     rows = weight_ref.shape[0] // count
     me = lax.axis_index("chan")
-    for step in list(range(1, count)) + [0]:
+    for step, out_ref in zip(steps, out_refs):
         place = look_up(routes[step], me)
         block = weight_ref[pl.ds(pl.multiple_of(place * rows, rows), rows), :]
-        out_refs[step][...] = lax.dot_general(
+        out_ref[...] = lax.dot_general(
             block, grad_ref[...], (((1,), (1,)), ((), ())), preferred_element_type=f32
-        ).astype(out_refs[step].dtype)
+        ).astype(out_ref.dtype)
 
 
 def total_kernel(gating_ref, *refs):
@@ -400,7 +400,7 @@
     twiddle = jnp.asarray(twiddle_table(shards, length))
     shape = jax.ShapeDtypeStruct
 
-    routes_2 = [[(i + step) % parts for i in range(parts)] for step in range(parts)]
+    routes_2 = [[(i - step) % parts for i in range(parts)] for step in range(parts)]
     routes_1 = [range(4), [3, 2, 1, 0], [1, 3, 0, 2], [2, 0, 3, 1]] if parts == 4 else routes_2
 
     def shift(array, route):
@@ -424,12 +424,18 @@
         pairs = send_plain(decay_rates, filter_taps, signal, shards)
     arrived = exchange(pairs)
 
-    partial = call(
-        functools.partial(spread_kernel, routes_1),
-        tuple(shape((channels, length), bf16) for k in range(parts)),
+    part = shape((channels, length), bf16)
+    (first,) = call(functools.partial(spread_kernel, routes_1, [1]), (part,), [VMEM] * 2)(
+        out_weight, out_grad
+    )
+    rest = list(range(2, parts)) + [0]
+    others = call(
+        functools.partial(spread_kernel, routes_1, rest),
+        (part,) * len(rest),
         [VMEM] * 2,
-        after=(pairs,),
+        after=(first,),
     )(out_weight, out_grad)
+    partial = [others[-1], first, *others[:-1]]
     shares = [shift(partial[step], routes_1[step]) for step in range(1, parts)]
 
     mixed_owned, *spectra = call(

time: 44.8 us -> 44.9 us (level)
  local copies, waits for them, and re-layouts: 0.7 us -> 0.04 us
  waiting for transfers between devices: 4.89 us -> 5.34 us
    unnamed x18 -> x16, local copies, waits for them, and re-layouts: 0.7 us -> 0.04 us
    pallas_call x10 -> x11, Pallas kernels: 7.15 us -> 7.34 us  [call(): return lambda *operands: run(*operands, *after)]
  transfers between devices with their start and end apart: 14 -> 14, of which waited for: 5 -> 5; matrix products, arithmetic and copies ran while one was open for 0% -> 0% of each run, Pallas kernels for 10% -> 11%
where the time goes in v6:
time: 44.9 us; the launch traced here: 44.5 us
  starting transfers between devices  26.8 us (60%)
  Pallas kernels  7.34 us (16%)
  waiting for transfers between devices  5.34 us (12%)
  blocking collectives  4.18 us (9%)
  between operations  0.8 us (2%)
    ppermute x6, starting transfers between devices, shift(): return lax.ppermute(array, 'chan', list(enumerate(route)))  10.5 us
    all_to_all x2, starting transfers between devices, exchange(): return lax.all_to_all(array, 'seq', split_axis=0, concat_axis=0, tiled=True)  9.16 us
    pallas_call x11, Pallas kernels, call(): return lambda *operands: run(*operands, *after)  7.34 us
    ppermute x6, starting transfers between devices, hop(): lax.ppermute(array, 'seq', [(i, i ^ distance) for i in range(shards)])  7.18 us
    all_gather x2, blocking collectives, bring(): both = lax.all_gather(array, 'seq', axis_index_groups=pairs)  4.18 us
    ppermute x6, waiting for transfers between devices, shift(): return lax.ppermute(array, 'chan', list(enumerate(route)))  2.47 us
    all_to_all x2, waiting for transfers between devices, exchange(): return lax.all_to_all(array, 'seq', split_axis=0, concat_axis=0, tiled=True)  1.56 us
    ppermute x6, waiting for transfers between devices, hop(): lax.ppermute(array, 'seq', [(i, i ^ distance) for i in range(shards)])  1.31 us
  transfers between devices with their start and end apart: 14, of which 5 were waited for; matrix products, arithmetic and copies ran while one was open for 0% of the time, Pallas kernels for 11%

profile of v6, /device:TPU:0, one launch (start us, length us, event | category | flops | bytes accessed | tf_op | source)
XLA Modules:
  0.0 44.5 jit_solution(12203915345362462271)
XLA Ops:
  0.6 1.8 %shard_map.113 = bf16[8,64,256]{2,1,0:T(8,128)(2,1)} custom-call(f32[1,256]{1,0:T(1,128)} %bitcast.6, f32[256,256]{1,0:T(8,128)} %refs_1_.6, bf16[256,256]{1,0:T(8,128)(2,1)} %refs_2_.2), custom_call_target="tpu_custom_call" | custom-call | flops 1150000000 | tf_op jit(solution)/shard_map/pallas_call | solution.py:38
  2.5 5.3 %all-to-all-start = ((bf16[8,64,256]{2,1,0:T(8,128)(2,1)}), bf16[8,64,256]{2,1,0:T(8,128)(2,1)S(1)}, u32[]{:S(2)}, u32[]{:S(2)}) async-start(bf16[8,64,256]{2,1,0:T(8,128)(2,1)} %shard_map.113), calls=%async_computation | async-start | bytes 524288 | tf_op jit(solution)/shard_map/all_to_all | solution.py:389
  7.8 0.3 shard_map.111.refs_2_
  8.1 0.0 copy-start.4
  8.1 0.0 copy-start.5
  8.1 3.7 %collective-permute-start = (bf16[256,256]{1,0:T(8,128)(2,1)S(1)}, bf16[256,256]{1,0:T(8,128)(2,1)S(1)}, u32[]{:S(2)}, u32[]{:S(2)}) collective-permute-start(bf16[256,256]{1,0:T(8,128)(2,1)S(1)} %shard_map.111.refs_2_), channel_id=1, source_target_pairs={{0,3},{1,2},{2,1},{3,0},{4,7},{5,6},{6,5},{7,4},{8,11},{9,10},{10,... | collective-permute-start | bytes 393224 | tf_op jit(solution)/shard_map/ppermute | solution.py:407
  11.8 0.4 shard_map.112
  12.2 0.1 collective-permute-start.1
  12.3 2.9 %collective-permute-start.2 = (bf16[256,256]{1,0:T(8,128)(2,1)S(1)}, bf16[256,256]{1,0:T(8,128)(2,1)S(1)}, u32[]{:S(2)}, u32[]{:S(2)}) collective-permute-start(bf16[256,256]{1,0:T(8,128)(2,1)S(1)} %get-tuple-element.29), channel_id=1, source_target_pairs={{0,2},{1,0},{2,3},{3,1},{4,6},{5,4},{6,7},{7,5},{8,10},{9,8},{10,1... | collective-permute-start | bytes 393224 | tf_op jit(solution)/shard_map/ppermute | solution.py:407
  15.2 1.0 %shard_map.114 = (bf16[8,32,256]{2,1,0:T(8,128)(2,1)S(1)}, bf16[288,256]{1,0:T(8,128)(2,1)S(1)}, bf16[288,256]{1,0:T(8,128)(2,1)S(1)}, bf16[288,256]{1,0:T(8,128)(2,1)S(1)}, bf16[288,256]{1,0:T(8,128)(2,1)S(1)}) custom-call(bf16[8,64,256]{2,1,0:T(8,128)(2,1)S(1)} %all-to-all-done.refs_0_, bf16[512,512]{1,0:T(8,128)(2,1)S(1)} %copy-done.4, ...), custom_call_target="tpu_custom_call" | custom-call | flops 2300000000 | tf_op jit(solution)/shard_map/pallas_call | solution.py:38
  16.2 2.0 %all-gather = bf16[16,32,256]{2,1,0:T(8,128)(2,1)S(1)} all-gather(bf16[8,32,256]{2,1,0:T(8,128)(2,1)S(1)} %get-tuple-element.30), channel_id=2, replica_groups={{0,4},{8,12},{16,20},{24,28},{1,5},{9,13},{17,21},{25,29},{2,6},{10,14}..., dimensions={0}, use_global_device_ids=true | all-gather | bytes 393216 | tf_op jit(solution)/shard_map/all_gather | solution.py:461
  18.2 2.1 %collective-permute-start.3 = (bf16[2,32,256]{2,1,0:T(8,128)(2,1)S(1)}, bf16[2,32,256]{2,1,0:T(8,128)(2,1)S(1)}, u32[]{:S(2)}, u32[]{:S(2)}) collective-permute-start(bf16[2,32,256]{2,1,0:T(8,128)(2,1)S(1)} %get-tuple-element.33), channel_id=1, source_target_pairs={{0,8},{4,12},{8,0},{12,4},{16,24},{20,28},{24,16},{28,20},{1,9},{5... | collective-permute-start | bytes 98312 | tf_op jit(solution)/shard_map/ppermute | solution.py:455
  20.3 1.5 %collective-permute-start.4 = (bf16[2,32,256]{2,1,0:T(8,128)(2,1)S(1)}, bf16[2,32,256]{2,1,0:T(8,128)(2,1)S(1)}, u32[]{:S(2)}, u32[]{:S(2)}) collective-permute-start(bf16[2,32,256]{2,1,0:T(8,128)(2,1)S(1)} %get-tuple-element.34), channel_id=1, source_target_pairs={{0,16},{4,20},{8,24},{12,28},{16,0},{20,4},{24,8},{28,12},{1,17},{... | collective-permute-start | bytes 98312 | tf_op jit(solution)/shard_map/ppermute | solution.py:455
  21.7 0.1 collective-permute-start.5
  21.8 1.7 %collective-permute-done.1.refs_3_ = bf16[256,256]{1,0:T(8,128)(2,1)S(1)} collective-permute-done((bf16[256,256]{1,0:T(8,128)(2,1)S(1)}, bf16[256,256]{1,0:T(8,128)(2,1)S(1)}, u32[]{:S(2)}, u32[]{:S(2)}) %collective-permute-start.1) | collective-permute-done | bytes 131104 | tf_op jit(solution)/shard_map/ppermute | solution.py:407
  23.5 0.7 %shard_map.116 = (bf16[256,256]{1,0:T(8,128)(2,1)S(1)}, bf16[256,256]{1,0:T(8,128)(2,1)}) custom-call(bf16[256,256]{1,0:T(8,128)(2,1)S(1)} %copy-done.2, bf16[256,256]{1,0:T(8,128)(2,1)S(1)} %get-tuple-element.27.refs_1_, bf16[256,256]{1,0:T(8,128)(2,1)S(1)} %collective-permute-done.refs_2_, bf16[256,256]{1,0:T(8,128)(2,1)S(1)} %collective-permute-done.1.refs_3_, ...), custom_call_target="tpu_custom_call" | custom-call | flops 1150000000 | tf_op jit(solution)/shard_map/pallas_call | solution.py:38
  24.3 3.8 %all-to-all-start.1 = ((bf16[8,32,256]{2,1,0:T(8,128)(2,1)}), bf16[8,32,256]{2,1,0:T(8,128)(2,1)S(1)}, u32[]{:S(2)}, u32[]{:S(2)}) async-start(bf16[8,32,256]{2,1,0:T(8,128)(2,1)} %bitcast.2), calls=%async_computation.1 | async-start | bytes 262144 | tf_op jit(solution)/shard_map/all_to_all | solution.py:389
  28.2 0.1 shard_map.117.refs_3_.refs_7_
  28.2 0.1 collective-permute-start.8
  28.3 3.0 %collective-permute-start.7 = (bf16[256,256]{1,0:T(8,128)(2,1)S(1)}, bf16[256,256]{1,0:T(8,128)(2,1)S(1)}, u32[]{:S(2)}, u32[]{:S(2)}) collective-permute-start(bf16[256,256]{1,0:T(8,128)(2,1)S(1)} %shard_map.117.refs_3_.refs_7_), channel_id=1, source_target_pairs={{0,2},{1,3},{2,0},{3,1},{4,6},{5,7},{6,4},{7,5},{8,10},{9,11},{10,... | collective-permute-start | bytes 393224 | tf_op jit(solution)/shard_map/ppermute | solution.py:407
  31.3 0.8 %collective-permute-start.6 = (bf16[256,256]{1,0:T(8,128)(2,1)S(1)}, bf16[256,256]{1,0:T(8,128)(2,1)S(1)}, u32[]{:S(2)}, u32[]{:S(2)}) collective-permute-start(bf16[256,256]{1,0:T(8,128)(2,1)S(1)} %shard_map.117.refs_3_.refs_7_), channel_id=1, source_target_pairs={{0,3},{1,0},{2,1},{3,2},{4,7},{5,4},{6,5},{7,6},{8,11},{9,8},{10,9... | collective-permute-start | bytes 393224 | tf_op jit(solution)/shard_map/ppermute | solution.py:407
  32.1 1.6 %all-to-all-done.1.refs_0_ = bf16[8,32,256]{2,1,0:T(8,128)(2,1)S(1)} async-done(((bf16[8,32,256]{2,1,0:T(8,128)(2,1)}), bf16[8,32,256]{2,1,0:T(8,128)(2,1)S(1)}, u32[]{:S(2)}, u32[]{:S(2)}) %all-to-all-start.1) | async-done | bytes 131104 | tf_op jit(solution)/shard_map/all_to_all | solution.py:389
  33.7 1.1 %shard_map.119 = bf16[8,64,256]{2,1,0:T(8,128)(2,1)S(1)} custom-call(bf16[8,32,256]{2,1,0:T(8,128)(2,1)S(1)} %all-to-all-done.1.refs_0_, bf16[288,256]{1,0:T(8,128)(2,1)S(1)} %get-tuple-element.39.refs_1_, bf16[288,256]{1,0:T(8,128)(2,1)S(1)} %get-tuple-element.40.refs_2_, bf16[288,256]{1,0:T(8,128)(2,1)S(1)} %get-tuple-element.41.refs_3_, ...), custom_call_target="tpu_custom_call" | custom-call | flops 2300000000 | tf_op jit(solution)/shard_map/pallas_call | solution.py:38
  34.7 2.2 %all-gather.1 = bf16[16,64,256]{2,1,0:T(8,128)(2,1)S(1)} all-gather(bf16[8,64,256]{2,1,0:T(8,128)(2,1)S(1)} %shard_map.119), channel_id=3, replica_groups={{0,4},{8,12},{16,20},{24,28},{1,5},{9,13},{17,21},{25,29},{2,6},{10,14}..., dimensions={0}, use_global_device_ids=true | all-gather | bytes 786432 | tf_op jit(solution)/shard_map/all_gather | solution.py:461
  36.9 0.6 %collective-permute-start.9 = (bf16[2,64,256]{2,1,0:T(8,128)(2,1)S(1)}, bf16[2,64,256]{2,1,0:T(8,128)(2,1)S(1)}, u32[]{:S(2)}, u32[]{:S(2)}) collective-permute-start(bf16[2,64,256]{2,1,0:T(8,128)(2,1)S(1)} %get-tuple-element.44), channel_id=1, source_target_pairs={{0,16},{4,20},{8,24},{12,28},{16,0},{20,4},{24,8},{28,12},{1,17},{... | collective-permute-start | bytes 196616 | tf_op jit(solution)/shard_map/ppermute | solution.py:455
  37.6 1.5 %collective-permute-start.10 = (bf16[2,64,256]{2,1,0:T(8,128)(2,1)S(1)}, bf16[2,64,256]{2,1,0:T(8,128)(2,1)S(1)}, u32[]{:S(2)}, u32[]{:S(2)}) collective-permute-start(bf16[2,64,256]{2,1,0:T(8,128)(2,1)S(1)} %get-tuple-element.45), channel_id=1, source_target_pairs={{0,24},{4,28},{8,16},{12,20},{16,8},{20,12},{24,0},{28,4},{1,25},{... | collective-permute-start | bytes 196616 | tf_op jit(solution)/shard_map/ppermute | solution.py:455
  39.0 1.5 %collective-permute-start.11 = (bf16[2,64,256]{2,1,0:T(8,128)(2,1)S(1)}, bf16[2,64,256]{2,1,0:T(8,128)(2,1)S(1)}, u32[]{:S(2)}, u32[]{:S(2)}) collective-permute-start(bf16[2,64,256]{2,1,0:T(8,128)(2,1)S(1)} %get-tuple-element.46), channel_id=1, source_target_pairs={{0,8},{4,12},{8,0},{12,4},{16,24},{20,28},{24,16},{28,20},{1,9},{5... | collective-permute-start | bytes 196616 | tf_op jit(solution)/shard_map/ppermute | solution.py:455
  40.5 0.7 %collective-permute-done.7.refs_5_ = bf16[256,256]{1,0:T(8,128)(2,1)S(1)} collective-permute-done((bf16[256,256]{1,0:T(8,128)(2,1)S(1)}, bf16[256,256]{1,0:T(8,128)(2,1)S(1)}, u32[]{:S(2)}, u32[]{:S(2)}) %collective-permute-start.7) | collective-permute-done | bytes 131104 | tf_op jit(solution)/shard_map/ppermute | solution.py:407
  41.2 1.2 %shard_map.118 = (bf16[256,512]{1,0:T(8,128)(2,1)}, f32[256,256]{1,0:T(8,128)}, f32[256,256]{1,0:T(8,128)S(1)}) custom-call(bf16[1024,512]{1,0:T(8,128)(2,1)S(1)} %copy-done, bf16[256,256]{1,0:T(8,128)(2,1)S(1)} %get-tuple-element.32.refs_1_, f32[1,256]{1,0:T(1,128)S(1)} %bitcast.7, bf16[256,256]{1,0:T(8,128)(2,1)S(1)} %shard_map.117.refs_3_.refs_7_, ...), custom_call_target="tpu_custom_call" | custom-call | flops 13799999488 | tf_op jit(solution)/shard_map/pallas_call | solution.py:38
  42.4 1.0 %collective-permute-done.10.refs_3_ = bf16[2,64,256]{2,1,0:T(8,128)(2,1)S(1)} collective-permute-done((bf16[2,64,256]{2,1,0:T(8,128)(2,1)S(1)}, bf16[2,64,256]{2,1,0:T(8,128)(2,1)S(1)}, u32[]{:S(2)}, u32[]{:S(2)}) %collective-permute-start.10) | collective-permute-done | bytes 65568 | tf_op jit(solution)/shard_map/ppermute | solution.py:455
  43.4 0.3 collective-permute-done.11.refs_4_
  43.7 0.8 %shard_map.121 = (f32[256,256]{1,0:T(8,128)}, f32[256,256]{1,0:T(8,128)}) custom-call(f32[256,256]{1,0:T(8,128)S(1)} %get-tuple-element.37.refs_0_, bf16[2,64,256]{2,1,0:T(8,128)(2,1)S(1)} %get-tuple-element.43.refs_1_, bf16[2,64,256]{2,1,0:T(8,128)(2,1)S(1)} %collective-permute-done.9.refs_2_, bf16[2,64,256]{2,1,0:T(8,128)(2,1)S(1)} %collective-permute-done.10.refs_3_, ...), custom_call_target="tpu_custom_call" | custom-call | flops 1150000000 | tf_op jit(solution)/shard_map/pallas_call | solution.py:38
  (25 shorter events, 0.1 us)
Async XLA Ops:
  0.6 7.2 %copy-start = (bf16[1024,512]{1,0:T(8,128)(2,1)S(1)}, bf16[1024,512]{1,0:T(8,128)(2,1)}, u32[]{:S(2)}) copy-start(bf16[1024,512]{1,0:T(8,128)(2,1)} %refs_0_.9) | copy-start | bytes 3145732
  2.5 5.3 %copy-start.1 = (bf16[256,512]{1,0:T(8,128)(2,1)S(1)}, bf16[256,512]{1,0:T(8,128)(2,1)}, u32[]{:S(2)}) copy-start(bf16[256,512]{1,0:T(8,128)(2,1)} %refs_1_.5) | copy-start | bytes 786436
  2.5 12.7 %all-to-all-start = ((bf16[8,64,256]{2,1,0:T(8,128)(2,1)}), bf16[8,64,256]{2,1,0:T(8,128)(2,1)S(1)}, u32[]{:S(2)}, u32[]{:S(2)}) async-start(bf16[8,64,256]{2,1,0:T(8,128)(2,1)} %shard_map.113), calls=%async_computation | async-start | bytes 524288 | tf_op jit(solution)/shard_map/all_to_all | solution.py:389
  8.1 7.1 %copy-start.4 = (bf16[512,512]{1,0:T(8,128)(2,1)S(1)}, bf16[512,512]{1,0:T(8,128)(2,1)}, u32[]{:S(2)}) copy-start(bf16[512,512]{1,0:T(8,128)(2,1)} %constant.4.clone.refs_1_.refs_5_) | copy-start | bytes 1572868
  8.1 7.1 %copy-start.5 = (f32[9,2,256]{2,1,0:T(2,128)S(1)}, f32[9,2,256]{2,1,0:T(2,128)}, u32[]{:S(2)}) copy-start(f32[9,2,256]{2,1,0:T(2,128)} %constant.5.clone.refs_2_.refs_6_) | copy-start | bytes 55300
  8.1 13.6 %collective-permute-start = (bf16[256,256]{1,0:T(8,128)(2,1)S(1)}, bf16[256,256]{1,0:T(8,128)(2,1)S(1)}, u32[]{:S(2)}, u32[]{:S(2)}) collective-permute-start(bf16[256,256]{1,0:T(8,128)(2,1)S(1)} %shard_map.111.refs_2_), channel_id=1, source_target_pairs={{0,3},{1,2},{2,1},{3,0},{4,7},{5,6},{6,5},{7,4},{8,11},{9,10},{10,... | collective-permute-start | bytes 393224 | tf_op jit(solution)/shard_map/ppermute | solution.py:407
  12.2 11.3 %collective-permute-start.1 = (bf16[256,256]{1,0:T(8,128)(2,1)S(1)}, bf16[256,256]{1,0:T(8,128)(2,1)S(1)}, u32[]{:S(2)}, u32[]{:S(2)}) collective-permute-start(bf16[256,256]{1,0:T(8,128)(2,1)S(1)} %get-tuple-element.28), channel_id=1, source_target_pairs={{0,1},{1,3},{2,0},{3,2},{4,5},{5,7},{6,4},{7,6},{8,9},{9,11},{10,8... | collective-permute-start | bytes 393224 | tf_op jit(solution)/shard_map/ppermute | solution.py:407
  12.3 11.3 %collective-permute-start.2 = (bf16[256,256]{1,0:T(8,128)(2,1)S(1)}, bf16[256,256]{1,0:T(8,128)(2,1)S(1)}, u32[]{:S(2)}, u32[]{:S(2)}) collective-permute-start(bf16[256,256]{1,0:T(8,128)(2,1)S(1)} %get-tuple-element.29), channel_id=1, source_target_pairs={{0,2},{1,0},{2,3},{3,1},{4,6},{5,4},{6,7},{7,5},{8,10},{9,8},{10,1... | collective-permute-start | bytes 393224 | tf_op jit(solution)/shard_map/ppermute | solution.py:407
  16.1 2.0 %copy-start.6 = (bf16[288,256]{1,0:T(8,128)(2,1)}, bf16[288,256]{1,0:T(8,128)(2,1)S(1)}, u32[]{:S(2)}) copy-start(bf16[288,256]{1,0:T(8,128)(2,1)S(1)} %get-tuple-element.42.refs_4_) | copy-start | bytes 442372
  18.2 5.4 %copy-start.2 = (bf16[256,256]{1,0:T(8,128)(2,1)S(1)}, bf16[256,256]{1,0:T(8,128)(2,1)}, u32[]{:S(2)}) copy-start(bf16[256,256]{1,0:T(8,128)(2,1)} %refs_0_.8) | copy-start | bytes 393220
  18.2 10.0 %collective-permute-start.3 = (bf16[2,32,256]{2,1,0:T(8,128)(2,1)S(1)}, bf16[2,32,256]{2,1,0:T(8,128)(2,1)S(1)}, u32[]{:S(2)}, u32[]{:S(2)}) collective-permute-start(bf16[2,32,256]{2,1,0:T(8,128)(2,1)S(1)} %get-tuple-element.33), channel_id=1, source_target_pairs={{0,8},{4,12},{8,0},{12,4},{16,24},{20,28},{24,16},{28,20},{1,9},{5... | collective-permute-start | bytes 98312 | tf_op jit(solution)/shard_map/ppermute | solution.py:455
  20.3 7.9 %collective-permute-start.4 = (bf16[2,32,256]{2,1,0:T(8,128)(2,1)S(1)}, bf16[2,32,256]{2,1,0:T(8,128)(2,1)S(1)}, u32[]{:S(2)}, u32[]{:S(2)}) collective-permute-start(bf16[2,32,256]{2,1,0:T(8,128)(2,1)S(1)} %get-tuple-element.34), channel_id=1, source_target_pairs={{0,16},{4,20},{8,24},{12,28},{16,0},{20,4},{24,8},{28,12},{1,17},{... | collective-permute-start | bytes 98312 | tf_op jit(solution)/shard_map/ppermute | solution.py:455
  21.7 6.4 %collective-permute-start.5 = (bf16[2,32,256]{2,1,0:T(8,128)(2,1)S(1)}, bf16[2,32,256]{2,1,0:T(8,128)(2,1)S(1)}, u32[]{:S(2)}, u32[]{:S(2)}) collective-permute-start(bf16[2,32,256]{2,1,0:T(8,128)(2,1)S(1)} %get-tuple-element.35), channel_id=1, source_target_pairs={{0,24},{4,28},{8,16},{12,20},{16,8},{20,12},{24,0},{28,4},{1,25},{... | collective-permute-start | bytes 98312 | tf_op jit(solution)/shard_map/ppermute | solution.py:455
  24.3 9.4 %all-to-all-start.1 = ((bf16[8,32,256]{2,1,0:T(8,128)(2,1)}), bf16[8,32,256]{2,1,0:T(8,128)(2,1)S(1)}, u32[]{:S(2)}, u32[]{:S(2)}) async-start(bf16[8,32,256]{2,1,0:T(8,128)(2,1)} %bitcast.2), calls=%async_computation.1 | async-start | bytes 262144 | tf_op jit(solution)/shard_map/all_to_all | solution.py:389
  28.1 5.5 %copy-start.7 = (bf16[288,256]{1,0:T(8,128)(2,1)S(1)}, bf16[288,256]{1,0:T(8,128)(2,1)}, u32[]{:S(2)}) copy-start(bf16[288,256]{1,0:T(8,128)(2,1)} %copy-done.6) | copy-start | bytes 442372
  28.2 10.8 %collective-permute-start.8 = (bf16[256,256]{1,0:T(8,128)(2,1)S(1)}, bf16[256,256]{1,0:T(8,128)(2,1)S(1)}, u32[]{:S(2)}, u32[]{:S(2)}) collective-permute-start(bf16[256,256]{1,0:T(8,128)(2,1)S(1)} %shard_map.117.refs_3_.refs_7_), channel_id=1, source_target_pairs={{0,1},{1,2},{2,3},{3,0},{4,5},{5,6},{6,7},{7,4},{8,9},{9,10},{10,1... | collective-permute-start | bytes 393224 | tf_op jit(solution)/shard_map/ppermute | solution.py:407
  28.3 13.0 %collective-permute-start.7 = (bf16[256,256]{1,0:T(8,128)(2,1)S(1)}, bf16[256,256]{1,0:T(8,128)(2,1)S(1)}, u32[]{:S(2)}, u32[]{:S(2)}) collective-permute-start(bf16[256,256]{1,0:T(8,128)(2,1)S(1)} %shard_map.117.refs_3_.refs_7_), channel_id=1, source_target_pairs={{0,2},{1,3},{2,0},{3,1},{4,6},{5,7},{6,4},{7,5},{8,10},{9,11},{10,... | collective-permute-start | bytes 393224 | tf_op jit(solution)/shard_map/ppermute | solution.py:407
  31.3 9.9 %collective-permute-start.6 = (bf16[256,256]{1,0:T(8,128)(2,1)S(1)}, bf16[256,256]{1,0:T(8,128)(2,1)S(1)}, u32[]{:S(2)}, u32[]{:S(2)}) collective-permute-start(bf16[256,256]{1,0:T(8,128)(2,1)S(1)} %shard_map.117.refs_3_.refs_7_), channel_id=1, source_target_pairs={{0,3},{1,0},{2,1},{3,2},{4,7},{5,4},{6,5},{7,6},{8,11},{9,8},{10,9... | collective-permute-start | bytes 393224 | tf_op jit(solution)/shard_map/ppermute | solution.py:407
  36.9 5.5 %collective-permute-start.9 = (bf16[2,64,256]{2,1,0:T(8,128)(2,1)S(1)}, bf16[2,64,256]{2,1,0:T(8,128)(2,1)S(1)}, u32[]{:S(2)}, u32[]{:S(2)}) collective-permute-start(bf16[2,64,256]{2,1,0:T(8,128)(2,1)S(1)} %get-tuple-element.44), channel_id=1, source_target_pairs={{0,16},{4,20},{8,24},{12,28},{16,0},{20,4},{24,8},{28,12},{1,17},{... | collective-permute-start | bytes 196616 | tf_op jit(solution)/shard_map/ppermute | solution.py:455
  37.6 5.8 %collective-permute-start.10 = (bf16[2,64,256]{2,1,0:T(8,128)(2,1)S(1)}, bf16[2,64,256]{2,1,0:T(8,128)(2,1)S(1)}, u32[]{:S(2)}, u32[]{:S(2)}) collective-permute-start(bf16[2,64,256]{2,1,0:T(8,128)(2,1)S(1)} %get-tuple-element.45), channel_id=1, source_target_pairs={{0,24},{4,28},{8,16},{12,20},{16,8},{20,12},{24,0},{28,4},{1,25},{... | collective-permute-start | bytes 196616 | tf_op jit(solution)/shard_map/ppermute | solution.py:455
  39.0 2.2 %copy-start.3 = (f32[256]{0:T(256)S(1)}, f32[256]{0:T(256)}, u32[]{:S(2)}) copy-start(f32[256]{0:T(256)} %param.11) | copy-start | bytes 3076
  39.0 4.7 %collective-permute-start.11 = (bf16[2,64,256]{2,1,0:T(8,128)(2,1)S(1)}, bf16[2,64,256]{2,1,0:T(8,128)(2,1)S(1)}, u32[]{:S(2)}, u32[]{:S(2)}) collective-permute-start(bf16[2,64,256]{2,1,0:T(8,128)(2,1)S(1)} %get-tuple-element.46), channel_id=1, source_target_pairs={{0,8},{4,12},{8,0},{12,4},{16,24},{20,28},{24,16},{28,20},{1,9},{5... | collective-permute-start | bytes 196616 | tf_op jit(solution)/shard_map/ppermute | solution.py:455

commit v7 on v5

--- a/solution.py
+++ b/solution.py
@@ -428,7 +428,6 @@
         functools.partial(spread_kernel, routes_1),
         tuple(shape((channels, length), bf16) for k in range(parts)),
         [VMEM] * 2,
-        after=(pairs,),
     )(out_weight, out_grad)
     shares = [shift(partial[step], routes_1[step]) for step in range(1, parts)]
 

time: 44.8 us -> 44.8 us (level)
  local copies, waits for them, and re-layouts: 0.7 us -> 0.04 us
  waiting for transfers between devices: 4.89 us -> 5.52 us
    unnamed x18 -> x16, local copies, waits for them, and re-layouts: 0.7 us -> 0.04 us
    ppermute x6, waiting for transfers between devices: 2.34 us -> 2.96 us  [shift(): return lax.ppermute(array, 'chan', list(enumerate(route)))]
where the time goes in v7:
time: 44.8 us; the launch traced here: 44.5 us
  starting transfers between devices  26.8 us (60%)
  Pallas kernels  7.15 us (16%)
  waiting for transfers between devices  5.52 us (12%)
  blocking collectives  4.18 us (9%)
  between operations  0.79 us (2%)
    ppermute x6, starting transfers between devices, shift(): return lax.ppermute(array, 'chan', list(enumerate(route)))  10.5 us
    all_to_all x2, starting transfers between devices, exchange(): return lax.all_to_all(array, 'seq', split_axis=0, concat_axis=0, tiled=True)  9.16 us
    ppermute x6, starting transfers between devices, hop(): lax.ppermute(array, 'seq', [(i, i ^ distance) for i in range(shards)])  7.18 us
    pallas_call x10, Pallas kernels, call(): return lambda *operands: run(*operands, *after)  7.15 us
    all_gather x2, blocking collectives, bring(): both = lax.all_gather(array, 'seq', axis_index_groups=pairs)  4.18 us
    ppermute x6, waiting for transfers between devices, shift(): return lax.ppermute(array, 'chan', list(enumerate(route)))  2.96 us
    all_to_all x2, waiting for transfers between devices, exchange(): return lax.all_to_all(array, 'seq', split_axis=0, concat_axis=0, tiled=True)  1.56 us
    ppermute x6, waiting for transfers between devices, hop(): lax.ppermute(array, 'seq', [(i, i ^ distance) for i in range(shards)])  1 us
  transfers between devices with their start and end apart: 14, of which 5 were waited for; matrix products, arithmetic and copies ran while one was open for 0% of the time, Pallas kernels for 10%

profile of v7, /device:TPU:0, one launch (start us, length us, event | category | flops | bytes accessed | tf_op | source)
XLA Modules:
  0.0 44.5 jit_solution(8946243794810461815)
XLA Ops:
  0.6 1.8 %shard_map.112 = bf16[8,64,256]{2,1,0:T(8,128)(2,1)} custom-call(f32[1,256]{1,0:T(1,128)} %bitcast.6, f32[256,256]{1,0:T(8,128)} %refs_1_.4, bf16[256,256]{1,0:T(8,128)(2,1)} %refs_2_.2), custom_call_target="tpu_custom_call" | custom-call | flops 1150000000 | tf_op jit(solution)/shard_map/pallas_call | solution.py:38
  2.5 0.0 copy-start.1
  2.5 5.3 %all-to-all-start = ((bf16[8,64,256]{2,1,0:T(8,128)(2,1)}), bf16[8,64,256]{2,1,0:T(8,128)(2,1)S(1)}, u32[]{:S(2)}, u32[]{:S(2)}) async-start(bf16[8,64,256]{2,1,0:T(8,128)(2,1)} %shard_map.112), calls=%async_computation | async-start | bytes 524288 | tf_op jit(solution)/shard_map/all_to_all | solution.py:389
  7.8 0.0 copy-start.4
  7.8 0.0 copy-start.5
  7.9 0.5 %shard_map.111 = (bf16[256,256]{1,0:T(8,128)(2,1)S(1)}, bf16[256,256]{1,0:T(8,128)(2,1)S(1)}, bf16[256,256]{1,0:T(8,128)(2,1)S(1)}, bf16[256,256]{1,0:T(8,128)(2,1)S(1)}) custom-call(bf16[1024,512]{1,0:T(8,128)(2,1)S(1)} %copy-done, bf16[256,512]{1,0:T(8,128)(2,1)S(1)} %copy-done.1), custom_call_target="tpu_custom_call" | custom-call | flops 1150000000 | tf_op jit(solution)/shard_map/pallas_call | solution.py:38
  8.3 3.7 %collective-permute-start = (bf16[256,256]{1,0:T(8,128)(2,1)S(1)}, bf16[256,256]{1,0:T(8,128)(2,1)S(1)}, u32[]{:S(2)}, u32[]{:S(2)}) collective-permute-start(bf16[256,256]{1,0:T(8,128)(2,1)S(1)} %get-tuple-element.29), channel_id=1, source_target_pairs={{0,3},{1,2},{2,1},{3,0},{4,7},{5,6},{6,5},{7,4},{8,11},{9,10},{10,... | collective-permute-start | bytes 393224 | tf_op jit(solution)/shard_map/ppermute | solution.py:407
  12.0 2.9 %collective-permute-start.2 = (bf16[256,256]{1,0:T(8,128)(2,1)S(1)}, bf16[256,256]{1,0:T(8,128)(2,1)S(1)}, u32[]{:S(2)}, u32[]{:S(2)}) collective-permute-start(bf16[256,256]{1,0:T(8,128)(2,1)S(1)} %get-tuple-element.31), channel_id=1, source_target_pairs={{0,2},{1,0},{2,3},{3,1},{4,6},{5,4},{6,7},{7,5},{8,10},{9,8},{10,1... | collective-permute-start | bytes 393224 | tf_op jit(solution)/shard_map/ppermute | solution.py:407
  14.9 1.0 %shard_map.113 = (bf16[8,32,256]{2,1,0:T(8,128)(2,1)S(1)}, bf16[288,256]{1,0:T(8,128)(2,1)S(1)}, bf16[288,256]{1,0:T(8,128)(2,1)S(1)}, bf16[288,256]{1,0:T(8,128)(2,1)S(1)}, bf16[288,256]{1,0:T(8,128)(2,1)S(1)}) custom-call(bf16[8,64,256]{2,1,0:T(8,128)(2,1)S(1)} %all-to-all-done.refs_0_, bf16[512,512]{1,0:T(8,128)(2,1)S(1)} %copy-done.4, ...), custom_call_target="tpu_custom_call" | custom-call | flops 2300000000 | tf_op jit(solution)/shard_map/pallas_call | solution.py:38
  15.9 0.0 copy-start.6
  15.9 2.0 %all-gather = bf16[16,32,256]{2,1,0:T(8,128)(2,1)S(1)} all-gather(bf16[8,32,256]{2,1,0:T(8,128)(2,1)S(1)} %get-tuple-element.32), channel_id=2, replica_groups={{0,4},{8,12},{16,20},{24,28},{1,5},{9,13},{17,21},{25,29},{2,6},{10,14}..., dimensions={0}, use_global_device_ids=true | all-gather | bytes 393216 | tf_op jit(solution)/shard_map/all_gather | solution.py:454
  17.9 2.1 %collective-permute-start.3 = (bf16[2,32,256]{2,1,0:T(8,128)(2,1)S(1)}, bf16[2,32,256]{2,1,0:T(8,128)(2,1)S(1)}, u32[]{:S(2)}, u32[]{:S(2)}) collective-permute-start(bf16[2,32,256]{2,1,0:T(8,128)(2,1)S(1)} %get-tuple-element.35), channel_id=1, source_target_pairs={{0,8},{4,12},{8,0},{12,4},{16,24},{20,28},{24,16},{28,20},{1,9},{5... | collective-permute-start | bytes 98312 | tf_op jit(solution)/shard_map/ppermute | solution.py:448
  20.0 1.5 %collective-permute-start.4 = (bf16[2,32,256]{2,1,0:T(8,128)(2,1)S(1)}, bf16[2,32,256]{2,1,0:T(8,128)(2,1)S(1)}, u32[]{:S(2)}, u32[]{:S(2)}) collective-permute-start(bf16[2,32,256]{2,1,0:T(8,128)(2,1)S(1)} %get-tuple-element.36), channel_id=1, source_target_pairs={{0,16},{4,20},{8,24},{12,28},{16,0},{20,4},{24,8},{28,12},{1,17},{... | collective-permute-start | bytes 98312 | tf_op jit(solution)/shard_map/ppermute | solution.py:448
  21.5 0.1 collective-permute-start.5
  21.6 2.2 %collective-permute-done.1.refs_3_ = bf16[256,256]{1,0:T(8,128)(2,1)S(1)} collective-permute-done((bf16[256,256]{1,0:T(8,128)(2,1)S(1)}, bf16[256,256]{1,0:T(8,128)(2,1)S(1)}, u32[]{:S(2)}, u32[]{:S(2)}) %collective-permute-start.1) | collective-permute-done | bytes 131104 | tf_op jit(solution)/shard_map/ppermute | solution.py:407
  23.7 0.7 %shard_map.115 = (bf16[256,256]{1,0:T(8,128)(2,1)S(1)}, bf16[256,256]{1,0:T(8,128)(2,1)}) custom-call(bf16[256,256]{1,0:T(8,128)(2,1)S(1)} %copy-done.2, bf16[256,256]{1,0:T(8,128)(2,1)S(1)} %get-tuple-element.28.refs_1_, bf16[256,256]{1,0:T(8,128)(2,1)S(1)} %collective-permute-done.refs_2_, bf16[256,256]{1,0:T(8,128)(2,1)S(1)} %collective-permute-done.1.refs_3_, ...), custom_call_target="tpu_custom_call" | custom-call | flops 1150000000 | tf_op jit(solution)/shard_map/pallas_call | solution.py:38
  24.5 3.8 %all-to-all-start.1 = ((bf16[8,32,256]{2,1,0:T(8,128)(2,1)}), bf16[8,32,256]{2,1,0:T(8,128)(2,1)S(1)}, u32[]{:S(2)}, u32[]{:S(2)}) async-start(bf16[8,32,256]{2,1,0:T(8,128)(2,1)} %bitcast.2), calls=%async_computation.1 | async-start | bytes 262144 | tf_op jit(solution)/shard_map/all_to_all | solution.py:389
  28.4 0.1 shard_map.116.refs_3_.refs_7_
  28.4 0.1 collective-permute-start.6
  28.5 3.0 %collective-permute-start.7 = (bf16[256,256]{1,0:T(8,128)(2,1)S(1)}, bf16[256,256]{1,0:T(8,128)(2,1)S(1)}, u32[]{:S(2)}, u32[]{:S(2)}) collective-permute-start(bf16[256,256]{1,0:T(8,128)(2,1)S(1)} %shard_map.116.refs_3_.refs_7_), channel_id=1, source_target_pairs={{0,2},{1,3},{2,0},{3,1},{4,6},{5,7},{6,4},{7,5},{8,10},{9,11},{10,... | collective-permute-start | bytes 393224 | tf_op jit(solution)/shard_map/ppermute | solution.py:407
  31.5 0.8 %collective-permute-start.8 = (bf16[256,256]{1,0:T(8,128)(2,1)S(1)}, bf16[256,256]{1,0:T(8,128)(2,1)S(1)}, u32[]{:S(2)}, u32[]{:S(2)}) collective-permute-start(bf16[256,256]{1,0:T(8,128)(2,1)S(1)} %shard_map.116.refs_3_.refs_7_), channel_id=1, source_target_pairs={{0,3},{1,0},{2,1},{3,2},{4,7},{5,4},{6,5},{7,6},{8,11},{9,8},{10,9... | collective-permute-start | bytes 393224 | tf_op jit(solution)/shard_map/ppermute | solution.py:407
  32.3 1.6 %all-to-all-done.1.refs_0_ = bf16[8,32,256]{2,1,0:T(8,128)(2,1)S(1)} async-done(((bf16[8,32,256]{2,1,0:T(8,128)(2,1)}), bf16[8,32,256]{2,1,0:T(8,128)(2,1)S(1)}, u32[]{:S(2)}, u32[]{:S(2)}) %all-to-all-start.1) | async-done | bytes 131104 | tf_op jit(solution)/shard_map/all_to_all | solution.py:389
  33.9 1.1 %shard_map.118 = bf16[8,64,256]{2,1,0:T(8,128)(2,1)S(1)} custom-call(bf16[8,32,256]{2,1,0:T(8,128)(2,1)S(1)} %all-to-all-done.1.refs_0_, bf16[288,256]{1,0:T(8,128)(2,1)S(1)} %get-tuple-element.41.refs_1_, bf16[288,256]{1,0:T(8,128)(2,1)S(1)} %get-tuple-element.42.refs_2_, bf16[288,256]{1,0:T(8,128)(2,1)S(1)} %get-tuple-element.43.refs_3_, ...), custom_call_target="tpu_custom_call" | custom-call | flops 2300000000 | tf_op jit(solution)/shard_map/pallas_call | solution.py:38
  34.9 2.2 %all-gather.1 = bf16[16,64,256]{2,1,0:T(8,128)(2,1)S(1)} all-gather(bf16[8,64,256]{2,1,0:T(8,128)(2,1)S(1)} %shard_map.118), channel_id=3, replica_groups={{0,4},{8,12},{16,20},{24,28},{1,5},{9,13},{17,21},{25,29},{2,6},{10,14}..., dimensions={0}, use_global_device_ids=true | all-gather | bytes 786432 | tf_op jit(solution)/shard_map/all_gather | solution.py:454
  37.1 1.4 %collective-permute-start.10 = (bf16[2,64,256]{2,1,0:T(8,128)(2,1)S(1)}, bf16[2,64,256]{2,1,0:T(8,128)(2,1)S(1)}, u32[]{:S(2)}, u32[]{:S(2)}) collective-permute-start(bf16[2,64,256]{2,1,0:T(8,128)(2,1)S(1)} %get-tuple-element.47), channel_id=1, source_target_pairs={{0,24},{4,28},{8,16},{12,20},{16,8},{20,12},{24,0},{28,4},{1,25},{... | collective-permute-start | bytes 196616 | tf_op jit(solution)/shard_map/ppermute | solution.py:448
  38.6 0.7 %collective-permute-start.11 = (bf16[2,64,256]{2,1,0:T(8,128)(2,1)S(1)}, bf16[2,64,256]{2,1,0:T(8,128)(2,1)S(1)}, u32[]{:S(2)}, u32[]{:S(2)}) collective-permute-start(bf16[2,64,256]{2,1,0:T(8,128)(2,1)S(1)} %get-tuple-element.48), channel_id=1, source_target_pairs={{0,8},{4,12},{8,0},{12,4},{16,24},{20,28},{24,16},{28,20},{1,9},{5... | collective-permute-start | bytes 196616 | tf_op jit(solution)/shard_map/ppermute | solution.py:448
  39.2 1.5 %collective-permute-start.9 = (bf16[2,64,256]{2,1,0:T(8,128)(2,1)S(1)}, bf16[2,64,256]{2,1,0:T(8,128)(2,1)S(1)}, u32[]{:S(2)}, u32[]{:S(2)}) collective-permute-start(bf16[2,64,256]{2,1,0:T(8,128)(2,1)S(1)} %get-tuple-element.46), channel_id=1, source_target_pairs={{0,16},{4,20},{8,24},{12,28},{16,0},{20,4},{24,8},{28,12},{1,17},{... | collective-permute-start | bytes 196616 | tf_op jit(solution)/shard_map/ppermute | solution.py:448
  40.7 0.8 %collective-permute-done.7.refs_5_ = bf16[256,256]{1,0:T(8,128)(2,1)S(1)} collective-permute-done((bf16[256,256]{1,0:T(8,128)(2,1)S(1)}, bf16[256,256]{1,0:T(8,128)(2,1)S(1)}, u32[]{:S(2)}, u32[]{:S(2)}) %collective-permute-start.7) | collective-permute-done | bytes 131104 | tf_op jit(solution)/shard_map/ppermute | solution.py:407
  41.5 1.2 %shard_map.117 = (bf16[256,512]{1,0:T(8,128)(2,1)}, f32[256,256]{1,0:T(8,128)}, f32[256,256]{1,0:T(8,128)S(1)}) custom-call(bf16[1024,512]{1,0:T(8,128)(2,1)S(1)} %copy-done, bf16[256,256]{1,0:T(8,128)(2,1)S(1)} %get-tuple-element.34.refs_1_, f32[1,256]{1,0:T(1,128)S(1)} %bitcast.7, bf16[256,256]{1,0:T(8,128)(2,1)S(1)} %shard_map.116.refs_3_.refs_7_, ...), custom_call_target="tpu_custom_call" | custom-call | flops 13799999488 | tf_op jit(solution)/shard_map/pallas_call | solution.py:38
  42.7 0.3 collective-permute-done.10.refs_3_
  43.0 0.7 %collective-permute-done.9.refs_2_ = bf16[2,64,256]{2,1,0:T(8,128)(2,1)S(1)} collective-permute-done((bf16[2,64,256]{2,1,0:T(8,128)(2,1)S(1)}, bf16[2,64,256]{2,1,0:T(8,128)(2,1)S(1)}, u32[]{:S(2)}, u32[]{:S(2)}) %collective-permute-start.9) | collective-permute-done | bytes 65568 | tf_op jit(solution)/shard_map/ppermute | solution.py:448
  43.6 0.8 %shard_map.120 = (f32[256,256]{1,0:T(8,128)}, f32[256,256]{1,0:T(8,128)}) custom-call(f32[256,256]{1,0:T(8,128)S(1)} %get-tuple-element.39.refs_0_, bf16[2,64,256]{2,1,0:T(8,128)(2,1)S(1)} %get-tuple-element.45.refs_1_, bf16[2,64,256]{2,1,0:T(8,128)(2,1)S(1)} %collective-permute-done.9.refs_2_, bf16[2,64,256]{2,1,0:T(8,128)(2,1)S(1)} %collective-permute-done.10.refs_3_, ...), custom_call_target="tpu_custom_call" | custom-call | flops 1150000000 | tf_op jit(solution)/shard_map/pallas_call | solution.py:38
  (24 shorter events, 0.1 us)
Async XLA Ops:
  0.6 7.2 %copy-start = (bf16[1024,512]{1,0:T(8,128)(2,1)S(1)}, bf16[1024,512]{1,0:T(8,128)(2,1)}, u32[]{:S(2)}) copy-start(bf16[1024,512]{1,0:T(8,128)(2,1)} %refs_0_.7) | copy-start | bytes 3145732
  2.5 5.3 %copy-start.1 = (bf16[256,512]{1,0:T(8,128)(2,1)S(1)}, bf16[256,512]{1,0:T(8,128)(2,1)}, u32[]{:S(2)}) copy-start(bf16[256,512]{1,0:T(8,128)(2,1)} %refs_1_.3) | copy-start | bytes 786436
  2.5 12.4 %all-to-all-start = ((bf16[8,64,256]{2,1,0:T(8,128)(2,1)}), bf16[8,64,256]{2,1,0:T(8,128)(2,1)S(1)}, u32[]{:S(2)}, u32[]{:S(2)}) async-start(bf16[8,64,256]{2,1,0:T(8,128)(2,1)} %shard_map.112), calls=%async_computation | async-start | bytes 524288 | tf_op jit(solution)/shard_map/all_to_all | solution.py:389
  7.8 7.1 %copy-start.4 = (bf16[512,512]{1,0:T(8,128)(2,1)S(1)}, bf16[512,512]{1,0:T(8,128)(2,1)}, u32[]{:S(2)}) copy-start(bf16[512,512]{1,0:T(8,128)(2,1)} %constant.4.clone.refs_1_.refs_5_) | copy-start | bytes 1572868
  7.8 7.1 %copy-start.5 = (f32[9,2,256]{2,1,0:T(2,128)S(1)}, f32[9,2,256]{2,1,0:T(2,128)}, u32[]{:S(2)}) copy-start(f32[9,2,256]{2,1,0:T(2,128)} %constant.5.clone.refs_2_.refs_6_) | copy-start | bytes 55300
  8.3 13.1 %collective-permute-start = (bf16[256,256]{1,0:T(8,128)(2,1)S(1)}, bf16[256,256]{1,0:T(8,128)(2,1)S(1)}, u32[]{:S(2)}, u32[]{:S(2)}) collective-permute-start(bf16[256,256]{1,0:T(8,128)(2,1)S(1)} %get-tuple-element.29), channel_id=1, source_target_pairs={{0,3},{1,2},{2,1},{3,0},{4,7},{5,6},{6,5},{7,4},{8,11},{9,10},{10,... | collective-permute-start | bytes 393224 | tf_op jit(solution)/shard_map/ppermute | solution.py:407
  12.0 11.7 %collective-permute-start.1 = (bf16[256,256]{1,0:T(8,128)(2,1)S(1)}, bf16[256,256]{1,0:T(8,128)(2,1)S(1)}, u32[]{:S(2)}, u32[]{:S(2)}) collective-permute-start(bf16[256,256]{1,0:T(8,128)(2,1)S(1)} %get-tuple-element.30), channel_id=1, source_target_pairs={{0,1},{1,3},{2,0},{3,2},{4,5},{5,7},{6,4},{7,6},{8,9},{9,11},{10,8... | collective-permute-start | bytes 393224 | tf_op jit(solution)/shard_map/ppermute | solution.py:407
  12.0 11.7 %collective-permute-start.2 = (bf16[256,256]{1,0:T(8,128)(2,1)S(1)}, bf16[256,256]{1,0:T(8,128)(2,1)S(1)}, u32[]{:S(2)}, u32[]{:S(2)}) collective-permute-start(bf16[256,256]{1,0:T(8,128)(2,1)S(1)} %get-tuple-element.31), channel_id=1, source_target_pairs={{0,2},{1,0},{2,3},{3,1},{4,6},{5,4},{6,7},{7,5},{8,10},{9,8},{10,1... | collective-permute-start | bytes 393224 | tf_op jit(solution)/shard_map/ppermute | solution.py:407
  15.9 2.0 %copy-start.6 = (bf16[288,256]{1,0:T(8,128)(2,1)}, bf16[288,256]{1,0:T(8,128)(2,1)S(1)}, u32[]{:S(2)}) copy-start(bf16[288,256]{1,0:T(8,128)(2,1)S(1)} %get-tuple-element.44.refs_4_) | copy-start | bytes 442372
  17.9 5.8 %copy-start.2 = (bf16[256,256]{1,0:T(8,128)(2,1)S(1)}, bf16[256,256]{1,0:T(8,128)(2,1)}, u32[]{:S(2)}) copy-start(bf16[256,256]{1,0:T(8,128)(2,1)} %refs_0_.6) | copy-start | bytes 393220
  17.9 10.4 %collective-permute-start.3 = (bf16[2,32,256]{2,1,0:T(8,128)(2,1)S(1)}, bf16[2,32,256]{2,1,0:T(8,128)(2,1)S(1)}, u32[]{:S(2)}, u32[]{:S(2)}) collective-permute-start(bf16[2,32,256]{2,1,0:T(8,128)(2,1)S(1)} %get-tuple-element.35), channel_id=1, source_target_pairs={{0,8},{4,12},{8,0},{12,4},{16,24},{20,28},{24,16},{28,20},{1,9},{5... | collective-permute-start | bytes 98312 | tf_op jit(solution)/shard_map/ppermute | solution.py:448
  20.0 8.3 %collective-permute-start.4 = (bf16[2,32,256]{2,1,0:T(8,128)(2,1)S(1)}, bf16[2,32,256]{2,1,0:T(8,128)(2,1)S(1)}, u32[]{:S(2)}, u32[]{:S(2)}) collective-permute-start(bf16[2,32,256]{2,1,0:T(8,128)(2,1)S(1)} %get-tuple-element.36), channel_id=1, source_target_pairs={{0,16},{4,20},{8,24},{12,28},{16,0},{20,4},{24,8},{28,12},{1,17},{... | collective-permute-start | bytes 98312 | tf_op jit(solution)/shard_map/ppermute | solution.py:448
  21.5 6.9 %collective-permute-start.5 = (bf16[2,32,256]{2,1,0:T(8,128)(2,1)S(1)}, bf16[2,32,256]{2,1,0:T(8,128)(2,1)S(1)}, u32[]{:S(2)}, u32[]{:S(2)}) collective-permute-start(bf16[2,32,256]{2,1,0:T(8,128)(2,1)S(1)} %get-tuple-element.37), channel_id=1, source_target_pairs={{0,24},{4,28},{8,16},{12,20},{16,8},{20,12},{24,0},{28,4},{1,25},{... | collective-permute-start | bytes 98312 | tf_op jit(solution)/shard_map/ppermute | solution.py:448
  24.5 9.4 %all-to-all-start.1 = ((bf16[8,32,256]{2,1,0:T(8,128)(2,1)}), bf16[8,32,256]{2,1,0:T(8,128)(2,1)S(1)}, u32[]{:S(2)}, u32[]{:S(2)}) async-start(bf16[8,32,256]{2,1,0:T(8,128)(2,1)} %bitcast.2), calls=%async_computation.1 | async-start | bytes 262144 | tf_op jit(solution)/shard_map/all_to_all | solution.py:389
  28.3 5.5 %copy-start.7 = (bf16[288,256]{1,0:T(8,128)(2,1)S(1)}, bf16[288,256]{1,0:T(8,128)(2,1)}, u32[]{:S(2)}) copy-start(bf16[288,256]{1,0:T(8,128)(2,1)} %copy-done.6) | copy-start | bytes 442372
  28.4 10.8 %collective-permute-start.6 = (bf16[256,256]{1,0:T(8,128)(2,1)S(1)}, bf16[256,256]{1,0:T(8,128)(2,1)S(1)}, u32[]{:S(2)}, u32[]{:S(2)}) collective-permute-start(bf16[256,256]{1,0:T(8,128)(2,1)S(1)} %shard_map.116.refs_3_.refs_7_), channel_id=1, source_target_pairs={{0,1},{1,2},{2,3},{3,0},{4,5},{5,6},{6,7},{7,4},{8,9},{9,10},{10,1... | collective-permute-start | bytes 393224 | tf_op jit(solution)/shard_map/ppermute | solution.py:407
  28.5 13.0 %collective-permute-start.7 = (bf16[256,256]{1,0:T(8,128)(2,1)S(1)}, bf16[256,256]{1,0:T(8,128)(2,1)S(1)}, u32[]{:S(2)}, u32[]{:S(2)}) collective-permute-start(bf16[256,256]{1,0:T(8,128)(2,1)S(1)} %shard_map.116.refs_3_.refs_7_), channel_id=1, source_target_pairs={{0,2},{1,3},{2,0},{3,1},{4,6},{5,7},{6,4},{7,5},{8,10},{9,11},{10,... | collective-permute-start | bytes 393224 | tf_op jit(solution)/shard_map/ppermute | solution.py:407
  31.5 9.9 %collective-permute-start.8 = (bf16[256,256]{1,0:T(8,128)(2,1)S(1)}, bf16[256,256]{1,0:T(8,128)(2,1)S(1)}, u32[]{:S(2)}, u32[]{:S(2)}) collective-permute-start(bf16[256,256]{1,0:T(8,128)(2,1)S(1)} %shard_map.116.refs_3_.refs_7_), channel_id=1, source_target_pairs={{0,3},{1,0},{2,1},{3,2},{4,7},{5,4},{6,5},{7,6},{8,11},{9,8},{10,9... | collective-permute-start | bytes 393224 | tf_op jit(solution)/shard_map/ppermute | solution.py:407
  37.1 5.8 %collective-permute-start.10 = (bf16[2,64,256]{2,1,0:T(8,128)(2,1)S(1)}, bf16[2,64,256]{2,1,0:T(8,128)(2,1)S(1)}, u32[]{:S(2)}, u32[]{:S(2)}) collective-permute-start(bf16[2,64,256]{2,1,0:T(8,128)(2,1)S(1)} %get-tuple-element.47), channel_id=1, source_target_pairs={{0,24},{4,28},{8,16},{12,20},{16,8},{20,12},{24,0},{28,4},{1,25},{... | collective-permute-start | bytes 196616 | tf_op jit(solution)/shard_map/ppermute | solution.py:448
  38.6 4.4 %collective-permute-start.11 = (bf16[2,64,256]{2,1,0:T(8,128)(2,1)S(1)}, bf16[2,64,256]{2,1,0:T(8,128)(2,1)S(1)}, u32[]{:S(2)}, u32[]{:S(2)}) collective-permute-start(bf16[2,64,256]{2,1,0:T(8,128)(2,1)S(1)} %get-tuple-element.48), channel_id=1, source_target_pairs={{0,8},{4,12},{8,0},{12,4},{16,24},{20,28},{24,16},{28,20},{1,9},{5... | collective-permute-start | bytes 196616 | tf_op jit(solution)/shard_map/ppermute | solution.py:448
  39.2 2.2 %copy-start.3 = (f32[256]{0:T(256)S(1)}, f32[256]{0:T(256)}, u32[]{:S(2)}) copy-start(f32[256]{0:T(256)} %param.11) | copy-start | bytes 3076
  39.2 4.4 %collective-permute-start.9 = (bf16[2,64,256]{2,1,0:T(8,128)(2,1)S(1)}, bf16[2,64,256]{2,1,0:T(8,128)(2,1)S(1)}, u32[]{:S(2)}, u32[]{:S(2)}) collective-permute-start(bf16[2,64,256]{2,1,0:T(8,128)(2,1)S(1)} %get-tuple-element.46), channel_id=1, source_target_pairs={{0,16},{4,20},{8,24},{12,28},{16,0},{20,4},{24,8},{28,12},{1,17},{... | collective-permute-start | bytes 196616 | tf_op jit(solution)/shard_map/ppermute | solution.py:448
